TPU v7x, 512 devices: a whole 4x4x16 slice. The times are simulated.
512 devices in a mesh: dp: 8 (over y, core), proto: 64 (over x, z).
Axes of the slice: x: 4, y: 4, z: 16, core: 2. Of those that a mesh axis runs over, the one named last changes fastest.
Arguments:
- embeddings: bfloat16 [2048, 3, 256], P(('dp', 'proto')), may hold values from -3 to 3
- prototypes: bfloat16 [65536, 256], P('proto'), may hold values from -2 to 2
Outputs:
- embed_grad: float32 [2048, 3, 256], P(('dp', 'proto'))
- proto_grad: float32 [65536, 256], P('proto')
All inputs are finite; a program needn't handle non-finite values.
Results may differ from a plain program's by a relative error of at most 0.0065.
Values may be sent and summed in bfloat16 or wider, within the bound.
No kernel may reach another device: no remote copies, remote signals or barrier semaphores. Data moves between devices by JAX's collectives and lax.ppermute only.
A program may use at most 64 MiB of HBM per device.

v0:
```python
import jax
import jax.numpy as jnp
from jax import lax
from jax.sharding import PartitionSpec as P

ITERS = 3


def per_device(embeddings, prototypes):
    rows_owned = embeddings.shape[0]
    modes = embeddings.shape[1]
    width = embeddings.shape[2]
    local_protos = prototypes.shape[0]
    raw_rows = embeddings.astype(jnp.float32)
    row_scale = lax.rsqrt(jnp.sum(raw_rows * raw_rows, axis=-1, keepdims=True) + 1e-06)
    unit_rows = (raw_rows * row_scale).astype(jnp.bfloat16)
    raw_protos = prototypes.astype(jnp.float32)
    proto_scale = lax.rsqrt(jnp.sum(raw_protos * raw_protos, axis=-1, keepdims=True) + 1e-06)
    unit_protos = (raw_protos * proto_scale).astype(jnp.bfloat16)
    gathered = lax.all_gather(unit_rows, "proto", axis=0, tiled=True).reshape(-1, width)
    line_count = gathered.shape[0]
    samples = line_count // modes
    block_width = min(256, local_protos)
    block_count = local_protos // block_width

    def scores_at(position):
        protos = unit_protos[position * block_width : (position + 1) * block_width]
        return jnp.dot(gathered, protos.T, preferred_element_type=jnp.float32)

    def row_mass(inverse):
        total = jnp.zeros((line_count,), jnp.float32)
        soft = jnp.zeros((line_count,), jnp.float32)
        for position in range(block_count):
            scores = scores_at(position)
            kernel = jnp.exp(scores * 20.0).reshape(samples, modes, block_width)
            inverse_part = inverse[:, position * block_width : (position + 1) * block_width]
            total = total + jnp.sum(kernel * inverse_part[None], axis=-1).reshape(line_count)
        return (total, soft)

    col_weight = jnp.ones((line_count,), jnp.float32)
    inverse = None
    soft_total = None
    for sweep_id in range(ITERS):
        parts = []
        for column_position in range(block_count):
            column_kernel = jnp.exp(scores_at(column_position) * 20.0)
            parts.append(
                jnp.sum(
                    (column_kernel * col_weight[:, None]).reshape(samples, modes, block_width),
                    axis=0,
                )
            )
        mass = lax.psum(jnp.concatenate(parts, axis=1), "dp")
        inverse = 1.0 / mass
        if sweep_id == 0:
            row_part, soft_part = row_mass(inverse)
            row_total = lax.psum(row_part, "proto")
        else:
            row_part, soft_part = row_mass(inverse)
            row_total = lax.psum(row_part, "proto")
        col_weight = 1.0 / row_total
    soft_part = jnp.zeros((line_count,), jnp.float32)
    for position in range(block_count):
        soft_part = soft_part + jnp.sum(jnp.exp(scores_at(position) * 10.0), axis=-1)
    soft_total = lax.psum(soft_part, "proto")
    coefficient = 64.0 * 10.0 / 6.0
    grad_blocks = []
    for position in range(block_count):
        scores = scores_at(position)
        kernel = jnp.exp(scores * 20.0).reshape(samples, modes, block_width)
        inverse_part = inverse[:, position * block_width : (position + 1) * block_width]
        assigned = kernel * inverse_part[None] * col_weight.reshape(samples, modes, 1)
        predicted = jnp.exp(scores * 10.0).reshape(
            samples, modes, block_width
        ) / soft_total.reshape(samples, modes, 1)
        others = jnp.sum(assigned, axis=1, keepdims=True) - assigned
        logit_part = (coefficient * (2.0 * predicted - others)).astype(jnp.bfloat16)
        grad_blocks.append(logit_part.reshape(line_count, block_width))
    logit_grad = jnp.concatenate(grad_blocks, axis=1)
    unit_grad = lax.psum_scatter(
        jnp.dot(logit_grad, unit_protos, preferred_element_type=jnp.float32),
        "proto",
        scatter_dimension=0,
        tiled=True,
    )
    unit_grad = unit_grad.reshape(rows_owned, modes, width)
    inner = jnp.sum(unit_grad * raw_rows, axis=-1, keepdims=True)
    embed_grad = row_scale * unit_grad - row_scale * row_scale * row_scale * inner * raw_rows
    proto_part = lax.dot_general(
        logit_grad, gathered, (((0,), (0,)), ((), ())), preferred_element_type=jnp.float32
    )
    proto_total = lax.psum(proto_part, "dp")
    proto_inner = jnp.sum(proto_total * raw_protos, axis=-1, keepdims=True)
    proto_grad = (
        proto_scale * proto_total
        - proto_scale * proto_scale * proto_scale * proto_inner * raw_protos
    )
    return (embed_grad, proto_grad)


def solution(mesh):
    in_specs = (P(("dp", "proto"), None, None), P("proto", None))
    out_specs = (P(("dp", "proto"), None, None), P("proto", None))
    return jax.shard_map(
        per_device, mesh=mesh, in_specs=in_specs, out_specs=out_specs, check_vma=False
    )
```

profile of v0, /device:TPU:1, one launch (start us, length us, event | category | flops | bytes accessed | tf_op | source)
XLA Modules:
  0.0 1048.2 jit_solution(4641461067051098239)
XLA Ops:
  9.4 81.3 %all_gather.3 = bf16[256,3,256]{2,1,0:T(4,128)(2,1)S(1)} all-gather(bf16[4,3,256]{2,1,0:T(4,128)(2,1)S(1)} %fusion.40), channel_id=1, replica_groups=mesh['dp'=8,'proto'=64] {'proto'}, dimensions={0}, use_global_device_ids=true | all-gather | bytes 399360 | tf_op jit(solution)/shard_map/all_gather | solution.py:20
  106.3 2.4 reshape.205
  115.9 46.7 %psum.57 = f32[3,1024]{1,0:T(4,128)} all-reduce(f32[3,1024]{1,0:T(4,128)S(1)} %pad_maximum_fusion.3), channel_id=1, replica_groups=mesh['dp'=8,'proto'=64] {'dp'}, use_global_device_ids=true, to_apply=%region_11.0 | all-reduce | flops 3072 | bytes 24576 | tf_op jit(solution)/shard_map/psum | solution.py:53
  182.2 113.0 %psum.58 = f32[768]{0:T(1024)S(1)} all-reduce(f32[768]{0:T(1024)S(1)} %add_add_fusion.2), channel_id=1, replica_groups=mesh['dp'=8,'proto'=64] {'proto'}, use_global_device_ids=true, to_apply=%region_16.0 | all-reduce | flops 768 | bytes 6144 | tf_op jit(solution)/shard_map/psum | solution.py:57
  315.7 51.9 %psum.59 = f32[3,1024]{1,0:T(4,128)} all-reduce(f32[3,1024]{1,0:T(4,128)S(1)} %pad_maximum_fusion.4), channel_id=1, replica_groups=mesh['dp'=8,'proto'=64] {'dp'}, use_global_device_ids=true, to_apply=%region_21.0 | all-reduce | flops 3072 | bytes 24576 | tf_op jit(solution)/shard_map/psum | solution.py:53
  387.5 110.2 %psum.60 = f32[768]{0:T(1024)S(1)} all-reduce(f32[768]{0:T(1024)S(1)} %add_add_fusion.1), channel_id=1, replica_groups=mesh['dp'=8,'proto'=64] {'proto'}, use_global_device_ids=true, to_apply=%region_26.0 | all-reduce | flops 768 | bytes 6144 | tf_op jit(solution)/shard_map/psum | solution.py:60
  518.2 52.1 %psum.61 = f32[3,1024]{1,0:T(4,128)} all-reduce(f32[3,1024]{1,0:T(4,128)S(1)} %pad_maximum_fusion.5), channel_id=1, replica_groups=mesh['dp'=8,'proto'=64] {'dp'}, use_global_device_ids=true, to_apply=%region_31.0 | all-reduce | flops 3072 | bytes 24576 | tf_op jit(solution)/shard_map/psum | solution.py:53
  588.0 114.6 %all-reduce.2 = (f32[768]{0:T(1024)}, f32[768]{0:T(1024)}) all-reduce(f32[768]{0:T(1024)} %add_add_fusion, f32[768]{0:T(1024)S(1)} %add_add_fusion.3), channel_id=1, replica_groups=mesh['dp'=8,'proto'=64] {'proto'}, use_global_device_ids=true, to_apply=%region_36.0 | all-reduce | flops 1536 | bytes 12288 | tf_op jit(solution)/shard_map/psum | solution.py:60
  704.1 3.1 fusion.1
  721.7 3.7 multiply_convert_fusion.3
  727.1 114.6 %fusion = f32[16,256]{1,0:T(8,128)S(1)} fusion(f32[768,256]{1,0:T(8,128)S(1)} %fusion.30), kind=kCustom, calls=%all-reduce-scatter | all-reduce-scatter fusion | flops 262145 | bytes 804864
  843.1 3.5 collective-permute-start
  852.3 6.0 collective-permute-start.13
  858.2 3.7 collective-permute-start.14
  861.9 6.8 collective-permute-start.2
  868.7 6.4 collective-permute-start.3
  875.1 5.4 collective-permute-start.4
  880.5 3.3 collective-permute-start.5
  883.8 8.1 collective-permute-start.6
  891.9 4.3 collective-permute-start.7
  896.3 5.2 collective-permute-start.8
  901.5 4.5 collective-permute-start.9
  906.0 2.9 fusion.29
  913.7 124.7 %all-reduce.5.cloned.1.call-done = f32[1024,256]{1,0:T(8,128)} async-done(((f32[1024,256]{1,0:T(8,128)}), f32[1024,256]{1,0:T(8,128)}) %all-reduce.5.cloned.1.call-update) | async-done | bytes 1048592 | tf_op jit(solution)/shard_map/psum | solution.py:92
  (196 shorter events, 154.6 us)
Async XLA Ops:
  7.2 83.9 %copy-start = (bf16[1024,256]{1,0:T(8,128)(2,1)S(1)}, bf16[1024,256]{1,0:T(8,128)(2,1)}, u32[]{:S(2)}) copy-start(bf16[1024,256]{1,0:T(8,128)(2,1)} %param.3) | copy-start | bytes 1572868
  7.2 1031.3 %all-reduce.5.cloned.1.call-start = ((), (), s32[]{:S(2)}) async-start(), calls=%async_computation | async-start | bytes 2097152 | tf_op jit(solution)/shard_map/psum | solution.py:92
  571.0 10.4 copy-start.31
  721.7 4.9 copy-start.12
  841.8 8.7 collective-permute-start.15
  843.1 9.2 collective-permute-start
  846.6 11.7 %collective-permute-start.1 = (f32[16,256]{1,0:T(8,128)S(1)}, f32[16,256]{1,0:T(8,128)S(1)}, u32[]{:S(2)}, u32[]{:S(2)}) collective-permute-start(f32[16,256]{1,0:T(8,128)S(1)} %fusion), channel_id=1, source_target_pairs={{0,2},{1,3},{2,4},{3,5},{4,6},{5,7},{6,8},{7,9},{8,10},{9,11},{10,... | collective-permute-start | bytes 49160
  847.8 14.1 %collective-permute-start.10 = (f32[16,256]{1,0:T(8,128)S(1)}, f32[16,256]{1,0:T(8,128)S(1)}, u32[]{:S(2)}, u32[]{:S(2)}) collective-permute-start(f32[16,256]{1,0:T(8,128)S(1)} %fusion), channel_id=1, source_target_pairs={{0,11},{1,12},{2,13},{3,14},{4,15},{5,16},{6,17},{7,18},{8,19},{9,... | collective-permute-start | bytes 49160
  849.1 19.6 %collective-permute-start.11 = (f32[16,256]{1,0:T(8,128)S(1)}, f32[16,256]{1,0:T(8,128)S(1)}, u32[]{:S(2)}, u32[]{:S(2)}) collective-permute-start(f32[16,256]{1,0:T(8,128)S(1)} %fusion), channel_id=1, source_target_pairs={{0,12},{1,13},{2,14},{3,15},{4,16},{5,17},{6,18},{7,19},{8,20},{9,... | collective-permute-start | bytes 49160
  850.5 24.6 %collective-permute-start.12 = (f32[16,256]{1,0:T(8,128)S(1)}, f32[16,256]{1,0:T(8,128)S(1)}, u32[]{:S(2)}, u32[]{:S(2)}) collective-permute-start(f32[16,256]{1,0:T(8,128)S(1)} %fusion), channel_id=1, source_target_pairs={{0,13},{1,14},{2,15},{3,16},{4,17},{5,18},{6,19},{7,20},{8,21},{9,... | collective-permute-start | bytes 49160
  852.3 28.2 %collective-permute-start.13 = (f32[16,256]{1,0:T(8,128)S(1)}, f32[16,256]{1,0:T(8,128)S(1)}, u32[]{:S(2)}, u32[]{:S(2)}) collective-permute-start(f32[16,256]{1,0:T(8,128)S(1)} %fusion), channel_id=1, source_target_pairs={{0,14},{1,15},{2,16},{3,17},{4,18},{5,19},{6,20},{7,21},{8,22},{9,... | collective-permute-start | bytes 49160
  858.2 25.5 %collective-permute-start.14 = (f32[16,256]{1,0:T(8,128)S(1)}, f32[16,256]{1,0:T(8,128)S(1)}, u32[]{:S(2)}, u32[]{:S(2)}) collective-permute-start(f32[16,256]{1,0:T(8,128)S(1)} %fusion), channel_id=1, source_target_pairs={{0,15},{1,16},{2,17},{3,18},{4,19},{5,20},{6,21},{7,22},{8,23},{9,... | collective-permute-start | bytes 49160
  861.9 30.0 %collective-permute-start.2 = (f32[16,256]{1,0:T(8,128)S(1)}, f32[16,256]{1,0:T(8,128)S(1)}, u32[]{:S(2)}, u32[]{:S(2)}) collective-permute-start(f32[16,256]{1,0:T(8,128)S(1)} %fusion), channel_id=1, source_target_pairs={{0,3},{1,4},{2,5},{3,6},{4,7},{5,8},{6,9},{7,10},{8,11},{9,12},{10... | collective-permute-start | bytes 49160
  868.7 27.5 %collective-permute-start.3 = (f32[16,256]{1,0:T(8,128)S(1)}, f32[16,256]{1,0:T(8,128)S(1)}, u32[]{:S(2)}, u32[]{:S(2)}) collective-permute-start(f32[16,256]{1,0:T(8,128)S(1)} %fusion), channel_id=1, source_target_pairs={{0,4},{1,5},{2,6},{3,7},{4,8},{5,9},{6,10},{7,11},{8,12},{9,13},{1... | collective-permute-start | bytes 49160
  875.1 26.4 %collective-permute-start.4 = (f32[16,256]{1,0:T(8,128)S(1)}, f32[16,256]{1,0:T(8,128)S(1)}, u32[]{:S(2)}, u32[]{:S(2)}) collective-permute-start(f32[16,256]{1,0:T(8,128)S(1)} %fusion), channel_id=1, source_target_pairs={{0,5},{1,6},{2,7},{3,8},{4,9},{5,10},{6,11},{7,12},{8,13},{9,14},{... | collective-permute-start | bytes 49160
  880.5 30.5 %collective-permute-start.5 = (f32[16,256]{1,0:T(8,128)S(1)}, f32[16,256]{1,0:T(8,128)S(1)}, u32[]{:S(2)}, u32[]{:S(2)}) collective-permute-start(f32[16,256]{1,0:T(8,128)S(1)} %fusion), channel_id=1, source_target_pairs={{0,6},{1,7},{2,8},{3,9},{4,10},{5,11},{6,12},{7,13},{8,14},{9,15},... | collective-permute-start | bytes 49160
  883.8 27.2 %collective-permute-start.6 = (f32[16,256]{1,0:T(8,128)S(1)}, f32[16,256]{1,0:T(8,128)S(1)}, u32[]{:S(2)}, u32[]{:S(2)}) collective-permute-start(f32[16,256]{1,0:T(8,128)S(1)} %fusion), channel_id=1, source_target_pairs={{0,7},{1,8},{2,9},{3,10},{4,11},{5,12},{6,13},{7,14},{8,15},{9,16}... | collective-permute-start | bytes 49160
  891.9 19.1 %collective-permute-start.7 = (f32[16,256]{1,0:T(8,128)S(1)}, f32[16,256]{1,0:T(8,128)S(1)}, u32[]{:S(2)}, u32[]{:S(2)}) collective-permute-start(f32[16,256]{1,0:T(8,128)S(1)} %fusion), channel_id=1, source_target_pairs={{0,8},{1,9},{2,10},{3,11},{4,12},{5,13},{6,14},{7,15},{8,16},{9,17... | collective-permute-start | bytes 49160
  896.3 14.7 %collective-permute-start.8 = (f32[16,256]{1,0:T(8,128)S(1)}, f32[16,256]{1,0:T(8,128)S(1)}, u32[]{:S(2)}, u32[]{:S(2)}) collective-permute-start(f32[16,256]{1,0:T(8,128)S(1)} %fusion), channel_id=1, source_target_pairs={{0,9},{1,10},{2,11},{3,12},{4,13},{5,14},{6,15},{7,16},{8,17},{9,1... | collective-permute-start | bytes 49160
  901.5 9.5 collective-permute-start.9
  909.0 4.1 copy-start.26
  909.0 129.5 %copy-start.1 = (bf16[1024,256]{1,0:T(8,128)(2,1)S(1)}, bf16[1024,256]{1,0:T(8,128)(2,1)}, u32[]{:S(2)}) copy-start(bf16[1024,256]{1,0:T(8,128)(2,1)} %param.3) | copy-start | bytes 1572868
  911.0 129.0 %copy-start.22 = (f32[1024]{0:T(1024)S(1)}, f32[1024]{0:T(1024)}, u32[]{:S(2)}) copy-start(f32[1024]{0:T(1024)} %copy-done.21) | copy-start | bytes 12292
  911.0 129.0 %copy-start.20 = (f32[1024]{0:T(1024)S(1)}, f32[1024]{0:T(1024)}, u32[]{:S(2)}) copy-start(f32[1024]{0:T(1024)} %copy-done.19) | copy-start | bytes 12292
  (26 other events, 42.4 us)
Sparse Core Ops, SparseCore 0:
  909.1 129.2 all-reduce.4
where the time goes:
time: 1050 us
  blocking collectives  684 us (65%)
  waiting for transfers between devices  125 us (12%)
  local copies, waits for them, and re-layouts  87.2 us (8%)
  starting transfers between devices  64.1 us (6%)
  other arithmetic  64 us (6%)
  between operations  15.3 us (1%)
    psum x3, blocking collectives, per_device(): row_total = lax.psum(row_part, 'proto')  338 us
    psum x3, blocking collectives, per_device(): mass = lax.psum(jnp.concatenate(parts, axis=1), 'dp')  151 us
    psum x1, waiting for transfers between devices, per_device(): proto_total = lax.psum(proto_part, 'dp')  125 us
    unnamed x1, blocking collectives  115 us
    all_gather x1, blocking collectives, per_device(): lax.all_gather(unit_rows, 'proto', axis=0, tiled=True).reshape(-1, width)  81.3 us
    unnamed x16, starting transfers between devices  64 us
    mul x22, local copies, waits for them, and re-layouts, row_mass(): kernel * inverse_part[None]  37.9 us
    reshape x11, local copies, waits for them, and re-layouts, per_device(): (column_kernel * col_weight[:, None]).reshape(samples, modes, block_width)  25.6 us
  transfers between devices with their start and end apart: 17, of which 1 were waited for; matrix products, arithmetic and copies ran while one was open for 1% of the time, Pallas kernels for 0%

commit v1 on v0

v1 whole, which is shorter than its diff:
```python
import functools

import jax
import jax.numpy as jnp
from jax import lax
from jax.experimental import pallas as pl
from jax.experimental.pallas import tpu as pltpu
from jax.sharding import Mesh, PartitionSpec as P

F32 = jnp.float32
BF16 = jnp.bfloat16
LANES = 128
COEFFICIENT = 64.0 * 10.0 / 6.0
NT = (((1,), (1,)), ((), ()))
SCALARS = pl.BlockSpec(memory_space=pltpu.SMEM)
WHOLE = pl.BlockSpec(memory_space=pltpu.VMEM)
ANYWHERE = pl.BlockSpec(memory_space=pl.ANY)


def call(body, name, out_shapes, in_specs, scratch=(), out_specs=None, aliases=None):
    many = isinstance(out_shapes, (list, tuple))
    return pl.pallas_call(
        body,
        name=name,
        in_specs=in_specs,
        out_shape=out_shapes,
        out_specs=out_specs or ([WHOLE] * len(out_shapes) if many else WHOLE),
        scratch_shapes=list(scratch),
        input_output_aliases=aliases or {},
        compiler_params=pltpu.CompilerParams(vmem_limit_bytes=28 * 1024 * 1024),
    )


def shape(dims, dtype):
    return jax.ShapeDtypeStruct(dims, dtype)


def tiles_to_line(block, first, count):
    return jnp.concatenate([block[first + j : first + j + 1] for j in range(count)], axis=1)


def line_to_tiles(ref, first, line):
    for j in range(line.shape[1] // LANES):
        ref[first + j : first + j + 1, :] = line[:, j * LANES : (j + 1) * LANES]


def tile_of(pair, tile):
    half = pair.shape[1] // LANES
    return pair[tile // half : tile // half + 1, (tile % half) * LANES : (tile % half + 1) * LANES]


def mode_of(pair, m, tiles):
    return jnp.concatenate([tile_of(pair, m * tiles + j) for j in range(tiles)], axis=1)


def lines_to_pair(lines):
    whole = jnp.concatenate(lines, axis=1)
    half = whole.shape[1] // 2
    return jnp.concatenate([whole[:, :half], whole[:, half:]], axis=0)


def upright(pair):
    count = 2 * pair.shape[1] // LANES
    block = jnp.concatenate([tile_of(pair, t) for t in range(count)] + [tile_of(pair, 0)] * (-count % 8), axis=0).T
    return jnp.concatenate([jnp.broadcast_to(block[:, t : t + 1], (LANES, LANES)) for t in range(count)], axis=0)


def two_terms(line):
    high = line.astype(BF16).astype(F32)
    row = lax.broadcasted_iota(jnp.int32, (16, line.shape[1]), 0)
    return jnp.where(row == 0, high, jnp.where(row == 1, line - high, 0.0)).astype(BF16)


def read_mode(ref, m, modes, owned):
    count = ref.shape[1] // (modes * owned)
    parts = [
        jnp.concatenate([ref[h, pl.ds(m * owned + i, count, stride=modes * owned), :] for h in range(ref.shape[0])], axis=1)
        for i in range(owned)
    ]
    return jnp.concatenate(parts, axis=0)


def score_body(modes, owned, rows_ref, protos_ref, kernel_ref, units_ref, unit_protos_ref, soft_ref, mass_ref, rows32):
    samples = rows_ref.shape[0] // modes
    width = protos_ref.shape[0]
    raw = protos_ref[...].astype(F32)
    scale = lax.rsqrt(jnp.sum(raw * raw, axis=-1, keepdims=True) + 1e-6)
    unit_protos_ref[...] = (raw * scale).astype(BF16)
    for h in range(rows32.shape[0]):
        rows32[h] = rows_ref[:, h * LANES : (h + 1) * LANES].astype(F32)
    lines = []
    for m in range(modes):
        rows = slice(m * samples, (m + 1) * samples)
        raw = read_mode(rows32, m, modes, owned)
        units = (raw * lax.rsqrt(jnp.sum(raw * raw, axis=-1, keepdims=True) + 1e-6)).astype(BF16)
        units_ref[rows, :] = units
        scores = lax.dot_general(units, unit_protos_ref[...], NT, preferred_element_type=F32)
        soft = jnp.exp(scores * 10.0)
        kernel = soft * soft
        kernel_ref[rows, :] = kernel.astype(BF16)
        line_to_tiles(mass_ref, m * (width // LANES), jnp.sum(kernel, axis=0, keepdims=True))
        folded = soft[:, :LANES]
        for j in range(1, width // LANES):
            folded = folded + soft[:, j * LANES : (j + 1) * LANES]
        high = folded.astype(BF16)
        low = (folded - high.astype(F32)).astype(BF16)
        ones = jnp.ones((16, LANES), BF16)
        line = lax.dot_general(ones, high, NT, preferred_element_type=F32)
        line = line + lax.dot_general(ones, low, NT, preferred_element_type=F32)
        lines.append(line[0:1])
    soft_ref[...] = lines_to_pair(lines)


def row_body(modes, mass_ref, kernel_ref, row_ref, inverse_ref):
    samples = kernel_ref.shape[0] // modes
    tiles = kernel_ref.shape[1] // LANES
    inverse = 1.0 / mass_ref[...]
    inverse_ref[...] = inverse
    lines = []
    for m in range(modes):
        terms = two_terms(tiles_to_line(inverse, m * tiles, tiles))
        kernel = kernel_ref[m * samples : (m + 1) * samples, :]
        line = lax.dot_general(terms, kernel, NT, preferred_element_type=F32)
        lines.append(line[0:1] + line[1:2])
    row_ref[...] = lines_to_pair(lines)


def column_body(modes, row_ref, kernel_ref, mass_ref):
    samples = kernel_ref.shape[0] // modes
    width = kernel_ref.shape[1]
    weight = 1.0 / row_ref[...]
    for m in range(modes):
        terms = two_terms(mode_of(weight, m, samples // LANES))
        kernel = kernel_ref[m * samples : (m + 1) * samples, :]
        line = jnp.dot(terms, kernel, preferred_element_type=F32)
        line_to_tiles(mass_ref, m * (width // LANES), line[0:1] + line[1:2])


def pull_body(modes, owned, place_ref, inverse_ref, units_ref, unit_protos_ref, *refs):
    pieces, grad32 = refs[:-1], refs[-1]
    samples = units_ref.shape[0] // modes
    width = unit_protos_ref.shape[0]
    tiles = width // LANES
    chunk = samples // owned // len(pieces)
    for m in range(modes):
        units = units_ref[m * samples : (m + 1) * samples, :]
        soft = jnp.exp(10.0 * lax.dot_general(units, unit_protos_ref[...], NT, preferred_element_type=F32))
        codes = soft * soft * tiles_to_line(inverse_ref[...], m * tiles, tiles)
        for part, value in enumerate((soft, codes)):
            first = (part * modes + m) * samples
            grad32[first : first + samples, :] = jnp.dot(
                value.astype(BF16), unit_protos_ref[...], preferred_element_type=F32
            )
    for step, piece in enumerate(pieces):
        place = lax.rem(place_ref[0] + step, len(pieces)) * chunk
        for j in range(2 * modes * owned):
            first = pl.multiple_of(place + j * (samples // owned), chunk)
            piece[j * chunk : (j + 1) * chunk, :] = grad32[pl.ds(first, chunk), :].astype(BF16)


def combine_body(modes, owned, place_ref, totals_ref, tied_ref, *refs):
    pieces, (rows_ref, weights, unit) = refs[:-3], refs[-3:]
    total = functools.reduce(jnp.add, [piece[...].astype(F32) for piece in pieces])
    height = total.shape[0] // 2
    chunk = height // (modes * owned)
    weights[0] = upright(COEFFICIENT / totals_ref[0:2])
    weights[1] = upright(2.0 * COEFFICIENT / totals_ref[2:4])
    samples = weights.shape[1] // modes

    def weighted(kind, first, m):
        factor = jnp.concatenate(
            [
                weights[kind, pl.ds(pl.multiple_of(m * samples + (i * len(pieces) + place_ref[0]) * chunk, chunk), chunk), :]
                for i in range(owned)
            ],
            axis=0,
        )
        block = total[first + m * owned * chunk : first + (m + 1) * owned * chunk]
        return block * jnp.concatenate([factor] * (block.shape[1] // LANES), axis=1)

    codes = [weighted(0, height, m) for m in range(modes)]
    for m in range(modes):
        others = [codes[n] for n in range(modes) if n != m]
        grad = weighted(1, 0, m) - functools.reduce(jnp.add, others)
        for h in range(unit.shape[0]):
            unit[h, m * owned * chunk : (m + 1) * owned * chunk, :] = grad[:, h * LANES : (h + 1) * LANES]
    for j in range(rows_ref.shape[0]):
        rows_ref[j] = jnp.concatenate(
            [unit[h, pl.ds(j, modes * owned, stride=chunk), :] for h in range(unit.shape[0])], axis=1
        ).astype(BF16)


def proto_body(modes, totals_ref, inverse_ref, units_ref, unit_protos_ref, *refs):
    proto_ref = refs[-1]
    samples = units_ref.shape[0] // modes
    width = unit_protos_ref.shape[0]
    tiles = width // LANES
    inverse = inverse_ref[...].T
    weight = COEFFICIENT / totals_ref[0:2]
    spread = 2.0 * COEFFICIENT / totals_ref[2:4]
    weight = [mode_of(weight, m, samples // LANES) for m in range(modes)]
    spread = [mode_of(spread, m, samples // LANES) for m in range(modes)]
    step = 256
    for k in range(0, width, step):
        scores = lax.dot_general(unit_protos_ref[k : k + step, :], units_ref[...], NT, preferred_element_type=F32)
        codes, predicted = [], []
        for m in range(modes):
            first = m * tiles + k // LANES
            upright_inverse = jnp.concatenate([inverse[:, first + j : first + j + 1] for j in range(step // LANES)], axis=0)
            soft = jnp.exp(10.0 * scores[:, m * samples : (m + 1) * samples])
            codes.append(soft * soft * upright_inverse * weight[m])
            predicted.append(soft * spread[m])
        logit = [
            (predicted[m] - functools.reduce(jnp.add, [codes[n] for n in range(modes) if n != m])).astype(BF16)
            for m in range(modes)
        ]
        proto_ref[k : k + step, :] = jnp.dot(
            jnp.concatenate(logit, axis=1), units_ref[...], preferred_element_type=F32
        ).astype(BF16)


def middle_body(place_ref, parts_ref, protos_ref, tied_ref, grad_ref, tied_out_ref):
    total = jnp.sum(parts_ref[...].astype(F32), axis=0)
    share = total.shape[0]
    raw = protos_ref[pl.ds(pl.multiple_of(place_ref[0] * share, share), share), :].astype(F32)
    scale = lax.rsqrt(jnp.sum(raw * raw, axis=-1, keepdims=True) + 1e-6)
    inner = jnp.sum(total * raw, axis=-1, keepdims=True)
    grad_ref[...] = (scale * total - scale * scale * scale * inner * raw).astype(BF16)


def last_body(parts_ref, raw_ref, grad_ref):
    total = jnp.sum(parts_ref[...].astype(F32), axis=0)
    raw = raw_ref[...].astype(F32)
    scale = lax.rsqrt(jnp.sum(raw * raw, axis=-1, keepdims=True) + 1e-6)
    inner = jnp.sum(total * raw, axis=-1, keepdims=True)
    grad = scale * total - scale * scale * scale * inner * raw
    modes, owned = grad_ref.shape[:2]
    for m in range(modes):
        grad_ref[m] = grad[m * owned : (m + 1) * owned]


def exchange(x, axes):
    return lax.all_to_all(x, axes, 0, 0, tiled=True)


def copies(x, axes, count):
    return exchange(jnp.broadcast_to(x[None], (count,) + x.shape), axes)


def gather(x, axes, count):
    return copies(x, axes, count).reshape((count * x.shape[0],) + x.shape[1:])


def sum_over(x, axes, count):
    return jnp.sum(copies(x.astype(BF16), axes, count).astype(F32), axis=0)


def shift(x, axis, count, step):
    return lax.ppermute(x, axis, [(i, (i + step) % count) for i in range(count)]) if step else x


def per_device(sizes, embeddings, prototypes):
    modes, width = embeddings.shape[1:]
    own_samples = embeddings.shape[0]
    owned = own_samples * modes
    local_protos = prototypes.shape[0]
    ny, nc, nx, nz = (sizes[a] for a in ("y", "core", "x", "z"))
    dp = ("y", "core")
    groups = ny * nc
    lines = owned * nx * nz
    x_lines = lines // nx
    mass_shape = shape((modes * local_protos // LANES, LANES), F32)
    row_shape = shape((2, lines // 2), F32)
    units_shape = shape((lines, width), BF16)
    dp_place = lax.axis_index(dp).reshape(1)
    x_place = lax.axis_index("x").reshape(1)

    row_call = call(functools.partial(row_body, modes), "row_sum", [row_shape, mass_shape], [WHOLE] * 2)
    column_call = call(functools.partial(column_body, modes), "column_sum", mass_shape, [WHOLE] * 2)

    raw_rows = embeddings.transpose(1, 0, 2).reshape(owned, width)
    gathered = gather(gather(raw_rows, "z", nz), "x", nx)
    kernel, units, unit_protos, soft, mass = call(
        functools.partial(score_body, modes, own_samples),
        "scores",
        [shape((lines, local_protos), BF16), units_shape, shape((local_protos, width), BF16), row_shape, mass_shape],
        [WHOLE] * 2,
        [pltpu.VMEM((width // LANES, lines, LANES), F32)],
    )(gathered, prototypes)

    for _ in range(2):
        row, _ = row_call(sum_over(mass, dp, groups), kernel)
        mass = column_call(sum_over(row, ("x", "z"), nx * nz), kernel)
    row, inverse = row_call(sum_over(mass, dp, groups), kernel)
    pieces = call(
        functools.partial(pull_body, modes, own_samples),
        "pull",
        [shape((2 * x_lines, width), BF16)] * nx,
        [SCALARS] + [WHOLE] * 3,
        [pltpu.VMEM((2 * lines, width), F32)],
    )(x_place, inverse, units, unit_protos)
    pieces = [shift(piece, "x", nx, step) for step, piece in enumerate(pieces)]
    totals = sum_over(jnp.concatenate([row, soft], axis=0), ("x", "z"), nx * nz)

    proto_part = call(
        functools.partial(proto_body, modes), "proto_part", shape((local_protos, width), BF16), [WHOLE] * 4 + [ANYWHERE] * nx
    )(totals, inverse, units, unit_protos, *pieces)
    rows = call(
        functools.partial(combine_body, modes, own_samples),
        "combine",
        shape((nz, owned, width), BF16),
        [SCALARS, WHOLE, ANYWHERE] + [WHOLE] * nx,
        [pltpu.VMEM((2, lines, LANES), F32), pltpu.VMEM((width // LANES, x_lines, LANES), F32)],
    )(x_place, totals, proto_part, *pieces)
    proto_part = exchange(proto_part, dp).reshape(groups, local_protos // groups, width)
    proto_grad, rows = call(
        middle_body,
        "middle",
        [shape((local_protos // groups, width), BF16), shape(rows.shape, BF16)],
        [SCALARS, WHOLE, WHOLE, ANYWHERE],
        (),
        [WHOLE, ANYWHERE],
        {3: 1},
    )(dp_place, proto_part, prototypes, rows)
    rows = exchange(rows, "z")
    proto_grad = lax.all_gather(proto_grad, dp, axis=0, tiled=True).astype(F32)
    embed_grad = call(last_body, "last", shape((modes, own_samples, width), F32), [WHOLE] * 2)(rows, raw_rows)
    return (embed_grad.transpose(1, 0, 2), proto_grad)


def solution(mesh):
    sizes = dict(y=mesh.shape["dp"] // 2, core=2, x=4, z=mesh.shape["proto"] // 4)
    fine = Mesh(mesh.devices.reshape(tuple(sizes.values())), tuple(sizes))
    specs = (P(("y", "core", "x", "z"), None, None), P(("x", "z"), None))
    return jax.shard_map(
        functools.partial(per_device, sizes), mesh=fine, in_specs=specs, out_specs=specs, check_vma=False
    )
```

time: 1050 us -> 184 us (0.18)
  blocking collectives: 684 us -> 113 us
  waiting for transfers between devices: 125 us -> 19.1 us
  local copies, waits for them, and re-layouts: 87.2 us -> 2.37 us
  other arithmetic: 64 us -> 1.23 us
  starting transfers between devices: 64.1 us -> 36.5 us
  between operations: 15.3 us -> 0.77 us
  Pallas kernels: 0 us -> 10.7 us
    psum x6 -> x0, blocking collectives: 489 us -> none  [the longest x3 338 us: per_device(): row_total = lax.psum(row_part, 'proto')]
    psum x1 -> x0, waiting for transfers between devices: 125 us -> none  [per_device(): proto_total = lax.psum(proto_part, 'dp')]
    unnamed x1 -> x0, blocking collectives: 115 us -> none
    all_to_all x0 -> x6, blocking collectives: none -> 98.6 us  [exchange(): return lax.all_to_all(x, axes, 0, 0, tiled=True)]
    all_gather x1, blocking collectives: 81.3 us -> 14.1 us  [per_device(): proto_grad = lax.all_gather(proto_grad, dp, axis=0, tiled=True).astype(F32)]
    unnamed x16 -> x0, starting transfers between devices: 64 us -> none
    mul x25 -> x0, local copies, waits for them, and re-layouts: 42.2 us -> none  [the longest x22 37.9 us: row_mass(): kernel * inverse_part[None]]
    reduce_sum x26 -> x6, other arithmetic: 40 us -> 0.12 us  [sum_over(): return jnp.sum(copies(x.astype(BF16), axes, count).astype(F32), axis=0)]
  transfers between devices with their start and end apart: 17 -> 7, of which waited for: 1 -> 5; matrix products, arithmetic and copies ran while one was open for 1% -> 1% of each run, Pallas kernels for 0% -> 2%
where the time goes in v1:
time: 184 us; the launch traced here: 183 us
  blocking collectives  113 us (61%)
  starting transfers between devices  36.5 us (20%)
  waiting for transfers between devices  19.1 us (10%)
  Pallas kernels  10.7 us (6%)
  local copies, waits for them, and re-layouts  2.37 us (1%)
    all_to_all x6, blocking collectives, exchange(): return lax.all_to_all(x, axes, 0, 0, tiled=True)  98.6 us
    all_to_all x4, starting transfers between devices, exchange(): return lax.all_to_all(x, axes, 0, 0, tiled=True)  26.1 us
    all_to_all x4, waiting for transfers between devices, exchange(): return lax.all_to_all(x, axes, 0, 0, tiled=True)  17 us
    all_gather x1, blocking collectives, per_device(): proto_grad = lax.all_gather(proto_grad, dp, axis=0, tiled=True).astype(F32)  14.1 us
    ppermute x3, starting transfers between devices, shift(): lax.ppermute(x, axis, [(i, (i + step) % count) for i in range(count)])  10.4 us
  transfers between devices with their start and end apart: 7, of which 5 were waited for; matrix products, arithmetic and copies ran while one was open for 1% of the time, Pallas kernels for 2%

profile of v1, /device:TPU:1, one launch (start us, length us, event | category | flops | bytes accessed | tf_op | source)
XLA Modules:
  0.0 183.3 jit_solution(4953970973906968374)
XLA Ops:
  1.4 27.5 %all_to_all.54 = bf16[16,12,256]{2,1,0:T(8,128)(2,1)S(1)} all-to-all(bf16[16,12,256]{2,1,0:T(8,128)(2,1)S(1)} %broadcast_in_dim.21), channel_id=1, replica_groups=mesh['y'=4,'core'=2,'x'=4,'z'=16] {'z'}, dimensions={0} | all-to-all | bytes 196608 | tf_op jit(solution)/shard_map/all_to_all | solution.py:243
  29.0 10.0 %all_to_all.55 = bf16[4,192,256]{2,1,0:T(8,128)(2,1)S(1)} all-to-all(bf16[4,192,256]{2,1,0:T(8,128)(2,1)S(1)} %broadcast_in_dim.23), channel_id=1, replica_groups=mesh['y'=4,'core'=2,'x'=4,'z'=16] {'x'}, dimensions={0} | all-to-all | bytes 786432 | tf_op jit(solution)/shard_map/all_to_all | solution.py:243
  39.1 1.5 scores.1
  40.6 14.1 %all_to_all.56 = bf16[8,24,128]{2,1,0:T(8,128)(2,1)S(1)} all-to-all(bf16[8,24,128]{2,1,0:T(8,128)(2,1)S(1)} %broadcast_in_dim.24), channel_id=1, replica_groups=mesh['y'=4,'core'=2,'x'=4,'z'=16] {'y','core'}, dimensions={0} | all-to-all | bytes 98304 | tf_op jit(solution)/shard_map/all_to_all | solution.py:243
  54.7 1.0 row_sum.3
  55.8 18.7 %all_to_all.57 = bf16[64,2,384]{2,1,0:T(2,128)(2,1)S(1)} all-to-all(bf16[64,2,384]{2,1,0:T(2,128)(2,1)S(1)} %broadcast_in_dim.25), channel_id=1, replica_groups=mesh['y'=4,'core'=2,'x'=4,'z'=16] {'x','z'}, dimensions={0} | all-to-all | bytes 196608 | tf_op jit(solution)/shard_map/all_to_all | solution.py:243
  74.8 9.9 %all_to_all.58 = bf16[8,24,128]{2,1,0:T(8,128)(2,1)S(1)} all-to-all(bf16[8,24,128]{2,1,0:T(8,128)(2,1)S(1)} %broadcast_in_dim.26), channel_id=1, replica_groups=mesh['y'=4,'core'=2,'x'=4,'z'=16] {'y','core'}, dimensions={0} | all-to-all | bytes 98304 | tf_op jit(solution)/shard_map/all_to_all | solution.py:243
  85.7 18.3 %all_to_all.59 = bf16[64,2,384]{2,1,0:T(2,128)(2,1)S(1)} all-to-all(bf16[64,2,384]{2,1,0:T(2,128)(2,1)S(1)} %broadcast_in_dim.27), channel_id=1, replica_groups=mesh['y'=4,'core'=2,'x'=4,'z'=16] {'x','z'}, dimensions={0} | all-to-all | bytes 196608 | tf_op jit(solution)/shard_map/all_to_all | solution.py:243
  105.0 6.0 %all-to-all-start.6 = ((bf16[8,24,128]{2,1,0:T(8,128)(2,1)}), bf16[8,24,128]{2,1,0:T(8,128)(2,1)S(1)}, u32[]{:S(2)}, u32[]{:S(2)}) async-start(bf16[8,24,128]{2,1,0:T(8,128)(2,1)} %broadcast_in_dim.28), calls=%async_computation.6 | async-start | bytes 98304 | tf_op jit(solution)/shard_map/all_to_all | solution.py:243
  111.0 4.8 %all-to-all-done.6 = bf16[8,24,128]{2,1,0:T(8,128)(2,1)S(1)} async-done(((bf16[8,24,128]{2,1,0:T(8,128)(2,1)}), bf16[8,24,128]{2,1,0:T(8,128)(2,1)S(1)}, u32[]{:S(2)}, u32[]{:S(2)}) %all-to-all-start.6) | async-done | bytes 49184 | tf_op jit(solution)/shard_map/all_to_all | solution.py:243
  117.1 4.8 %all-to-all-start.7 = ((bf16[64,4,384]{2,1,0:T(4,128)(2,1)}), bf16[64,4,384]{2,1,0:T(4,128)(2,1)S(1)}, u32[]{:S(2)}, u32[]{:S(2)}) async-start(bf16[64,4,384]{2,1,0:T(4,128)(2,1)} %broadcast_in_dim.29), calls=%async_computation.7 | async-start | bytes 393216 | tf_op jit(solution)/shard_map/all_to_all | solution.py:243
  121.9 1.8 pull.1
  123.7 2.9 %collective-permute-start = (bf16[384,256]{1,0:T(8,128)(2,1)S(1)}, bf16[384,256]{1,0:T(8,128)(2,1)S(1)}, u32[]{:S(2)}, u32[]{:S(2)}) collective-permute-start(bf16[384,256]{1,0:T(8,128)(2,1)S(1)} %get-tuple-element.27), channel_id=1, source_target_pairs={{0,16},{16,32},{32,48},{48,0},{1,17},{17,33},{33,49},{49,1},{2,18}... | collective-permute-start | bytes 589832 | tf_op jit(solution)/shard_map/ppermute | solution.py:259
  126.7 4.5 %collective-permute-start.1 = (bf16[384,256]{1,0:T(8,128)(2,1)S(1)}, bf16[384,256]{1,0:T(8,128)(2,1)S(1)}, u32[]{:S(2)}, u32[]{:S(2)}) collective-permute-start(bf16[384,256]{1,0:T(8,128)(2,1)S(1)} %get-tuple-element.28), channel_id=1, source_target_pairs={{0,32},{16,48},{32,0},{48,16},{1,33},{17,49},{33,1},{49,17},{2,34}... | collective-permute-start | bytes 589832 | tf_op jit(solution)/shard_map/ppermute | solution.py:259
  131.2 3.0 %collective-permute-start.2 = (bf16[384,256]{1,0:T(8,128)(2,1)S(1)}, bf16[384,256]{1,0:T(8,128)(2,1)S(1)}, u32[]{:S(2)}, u32[]{:S(2)}) collective-permute-start(bf16[384,256]{1,0:T(8,128)(2,1)S(1)} %get-tuple-element.29), channel_id=1, source_target_pairs={{0,48},{16,0},{32,16},{48,32},{1,49},{17,1},{33,17},{49,33},{2,50}... | collective-permute-start | bytes 589832 | tf_op jit(solution)/shard_map/ppermute | solution.py:259
  134.2 3.9 %all-to-all-done.7 = bf16[64,4,384]{2,1,0:T(4,128)(2,1)S(1)} async-done(((bf16[64,4,384]{2,1,0:T(4,128)(2,1)}), bf16[64,4,384]{2,1,0:T(4,128)(2,1)S(1)}, u32[]{:S(2)}, u32[]{:S(2)}) %all-to-all-start.7) | async-done | bytes 196640 | tf_op jit(solution)/shard_map/all_to_all | solution.py:243
  138.9 1.3 collective-permute-done.2.refs_3_
  140.2 2.3 %proto_part.1.tied_ref = bf16[1024,256]{1,0:T(8,128)(2,1)} custom-call(f32[4,384]{1,0:T(4,128)S(1)} %convert_reduce_fusion.totals_ref, f32[24,128]{1,0:T(8,128)S(1)} %get-tuple-element.23.inverse_ref, bf16[768,256]{1,0:T(8,128)(2,1)S(1)} %get-tuple-element.24.units_ref, bf16[1024,256]{1,0:T(8,128)(2,1)S(1)} %get-tuple-element.25.unit_protos_ref, ...), custom_call_target="tpu_custom_call" | custom-call | tf_op jit(solution)/shard_map/proto_part/pallas_call | solution.py:305
  142.5 5.0 %all-to-all-start.8 = ((bf16[8,128,256]{2,1,0:T(8,128)(2,1)}), bf16[8,128,256]{2,1,0:T(8,128)(2,1)S(1)}, u32[]{:S(2)}, u32[]{:S(2)}) async-start(bf16[8,128,256]{2,1,0:T(8,128)(2,1)} %bitcast.4), calls=%async_computation.8 | async-start | bytes 1048576 | tf_op jit(solution)/shard_map/all_to_all | solution.py:243
  147.4 1.2 combine.1.tied_ref
  148.6 8.3 %all-to-all-done.8.parts_ref = bf16[8,128,256]{2,1,0:T(8,128)(2,1)S(1)} async-done(((bf16[8,128,256]{2,1,0:T(8,128)(2,1)}), bf16[8,128,256]{2,1,0:T(8,128)(2,1)S(1)}, u32[]{:S(2)}, u32[]{:S(2)}) %all-to-all-start.8) | async-done | bytes 524320 | tf_op jit(solution)/shard_map/all_to_all | solution.py:243
  157.1 10.4 %all-to-all-start.9 = ((bf16[16,12,256]{2,1,0:T(8,128)(2,1)}), bf16[16,12,256]{2,1,0:T(8,128)(2,1)S(1)}, u32[]{:S(2)}, u32[]{:S(2)}) async-start(bf16[16,12,256]{2,1,0:T(8,128)(2,1)} %get-tuple-element.30), calls=%async_computation.9 | async-start | bytes 262144 | tf_op jit(solution)/shard_map/all_to_all | solution.py:243
  167.5 14.1 %all_gather.3 = bf16[1024,256]{1,0:T(8,128)(2,1)S(1)} all-gather(bf16[128,256]{1,0:T(8,128)(2,1)S(1)} %get-tuple-element.31), channel_id=1, replica_groups=mesh['y'=4,'core'=2,'x'=4,'z'=16] {'y','core'}, dimensions={0}, use_global_device_ids=true | all-gather | bytes 589824 | tf_op jit(solution)/shard_map/all_gather | solution.py:326
  181.6 1.0 convert_element_type.52
  (35 shorter events, 6.3 us)
Async XLA Ops:
  0.6 38.4 %copy-start = (bf16[1024,256]{1,0:T(8,128)(2,1)S(1)}, bf16[1024,256]{1,0:T(8,128)(2,1)}, u32[]{:S(2)}) copy-start(bf16[1024,256]{1,0:T(8,128)(2,1)} %protos_ref.3) | copy-start | bytes 1572868
  105.0 10.8 %all-to-all-start.6 = ((bf16[8,24,128]{2,1,0:T(8,128)(2,1)}), bf16[8,24,128]{2,1,0:T(8,128)(2,1)S(1)}, u32[]{:S(2)}, u32[]{:S(2)}) async-start(bf16[8,24,128]{2,1,0:T(8,128)(2,1)} %broadcast_in_dim.28), calls=%async_computation.6 | async-start | bytes 98304 | tf_op jit(solution)/shard_map/all_to_all | solution.py:243
  117.1 21.0 %all-to-all-start.7 = ((bf16[64,4,384]{2,1,0:T(4,128)(2,1)}), bf16[64,4,384]{2,1,0:T(4,128)(2,1)S(1)}, u32[]{:S(2)}, u32[]{:S(2)}) async-start(bf16[64,4,384]{2,1,0:T(4,128)(2,1)} %broadcast_in_dim.29), calls=%async_computation.7 | async-start | bytes 393216 | tf_op jit(solution)/shard_map/all_to_all | solution.py:243
  123.7 14.4 %collective-permute-start = (bf16[384,256]{1,0:T(8,128)(2,1)S(1)}, bf16[384,256]{1,0:T(8,128)(2,1)S(1)}, u32[]{:S(2)}, u32[]{:S(2)}) collective-permute-start(bf16[384,256]{1,0:T(8,128)(2,1)S(1)} %get-tuple-element.27), channel_id=1, source_target_pairs={{0,16},{16,32},{32,48},{48,0},{1,17},{17,33},{33,49},{49,1},{2,18}... | collective-permute-start | bytes 589832 | tf_op jit(solution)/shard_map/ppermute | solution.py:259
  126.7 12.2 %collective-permute-start.1 = (bf16[384,256]{1,0:T(8,128)(2,1)S(1)}, bf16[384,256]{1,0:T(8,128)(2,1)S(1)}, u32[]{:S(2)}, u32[]{:S(2)}) collective-permute-start(bf16[384,256]{1,0:T(8,128)(2,1)S(1)} %get-tuple-element.28), channel_id=1, source_target_pairs={{0,32},{16,48},{32,0},{48,16},{1,33},{17,49},{33,1},{49,17},{2,34}... | collective-permute-start | bytes 589832 | tf_op jit(solution)/shard_map/ppermute | solution.py:259
  131.2 9.0 %collective-permute-start.2 = (bf16[384,256]{1,0:T(8,128)(2,1)S(1)}, bf16[384,256]{1,0:T(8,128)(2,1)S(1)}, u32[]{:S(2)}, u32[]{:S(2)}) collective-permute-start(bf16[384,256]{1,0:T(8,128)(2,1)S(1)} %get-tuple-element.29), channel_id=1, source_target_pairs={{0,48},{16,0},{32,16},{48,32},{1,49},{17,1},{33,17},{49,33},{2,50}... | collective-permute-start | bytes 589832 | tf_op jit(solution)/shard_map/ppermute | solution.py:259
  142.5 14.5 %all-to-all-start.8 = ((bf16[8,128,256]{2,1,0:T(8,128)(2,1)}), bf16[8,128,256]{2,1,0:T(8,128)(2,1)S(1)}, u32[]{:S(2)}, u32[]{:S(2)}) async-start(bf16[8,128,256]{2,1,0:T(8,128)(2,1)} %bitcast.4), calls=%async_computation.8 | async-start | bytes 1048576 | tf_op jit(solution)/shard_map/all_to_all | solution.py:243
  157.1 25.5 %all-to-all-start.9 = ((bf16[16,12,256]{2,1,0:T(8,128)(2,1)}), bf16[16,12,256]{2,1,0:T(8,128)(2,1)S(1)}, u32[]{:S(2)}, u32[]{:S(2)}) async-start(bf16[16,12,256]{2,1,0:T(8,128)(2,1)} %get-tuple-element.30), calls=%async_computation.9 | async-start | bytes 262144 | tf_op jit(solution)/shard_map/all_to_all | solution.py:243

commit v2 on v1

--- a/solution.py
+++ b/solution.py
@@ -71,27 +71,30 @@
     return jnp.where(row == 0, high, jnp.where(row == 1, line - high, 0.0)).astype(BF16)
 
 
-def read_mode(ref, m, modes, owned):
-    count = ref.shape[1] // (modes * owned)
+def read_mode(ref, m, modes, owned, halves):
+    per_owner = halves * modes * owned
+    count = ref.shape[0] // per_owner
     parts = [
-        jnp.concatenate([ref[h, pl.ds(m * owned + i, count, stride=modes * owned), :] for h in range(ref.shape[0])], axis=1)
+        jnp.concatenate(
+            [ref[pl.ds((h * modes + m) * owned + i, count, stride=per_owner), :] for h in range(halves)], axis=1
+        )
         for i in range(owned)
     ]
     return jnp.concatenate(parts, axis=0)
 
 
 def score_body(modes, owned, rows_ref, protos_ref, kernel_ref, units_ref, unit_protos_ref, soft_ref, mass_ref, rows32):
-    samples = rows_ref.shape[0] // modes
+    samples = units_ref.shape[0] // modes
     width = protos_ref.shape[0]
+    halves = protos_ref.shape[1] // LANES
     raw = protos_ref[...].astype(F32)
     scale = lax.rsqrt(jnp.sum(raw * raw, axis=-1, keepdims=True) + 1e-6)
     unit_protos_ref[...] = (raw * scale).astype(BF16)
-    for h in range(rows32.shape[0]):
-        rows32[h] = rows_ref[:, h * LANES : (h + 1) * LANES].astype(F32)
+    rows32[...] = rows_ref[...].astype(F32)
     lines = []
     for m in range(modes):
         rows = slice(m * samples, (m + 1) * samples)
-        raw = read_mode(rows32, m, modes, owned)
+        raw = read_mode(rows32, m, modes, owned, halves)
         units = (raw * lax.rsqrt(jnp.sum(raw * raw, axis=-1, keepdims=True) + 1e-6)).astype(BF16)
         units_ref[rows, :] = units
         scores = lax.dot_general(units, unit_protos_ref[...], NT, preferred_element_type=F32)
@@ -152,7 +155,7 @@
                 value.astype(BF16), unit_protos_ref[...], preferred_element_type=F32
             )
     for step, piece in enumerate(pieces):
-        place = lax.rem(place_ref[0] + step, len(pieces)) * chunk
+        place = lax.bitwise_xor(place_ref[0], jnp.int32(step)) * chunk
         for j in range(2 * modes * owned):
             first = pl.multiple_of(place + j * (samples // owned), chunk)
             piece[j * chunk : (j + 1) * chunk, :] = grad32[pl.ds(first, chunk), :].astype(BF16)
@@ -186,7 +189,7 @@
             unit[h, m * owned * chunk : (m + 1) * owned * chunk, :] = grad[:, h * LANES : (h + 1) * LANES]
     for j in range(rows_ref.shape[0]):
         rows_ref[j] = jnp.concatenate(
-            [unit[h, pl.ds(j, modes * owned, stride=chunk), :] for h in range(unit.shape[0])], axis=1
+            [unit[h, pl.ds(j, modes * owned, stride=chunk), :] for h in range(unit.shape[0])], axis=0
         ).astype(BF16)
 
 
@@ -231,6 +234,8 @@
 def last_body(parts_ref, raw_ref, grad_ref):
     total = jnp.sum(parts_ref[...].astype(F32), axis=0)
     raw = raw_ref[...].astype(F32)
+    count = raw.shape[0]
+    total = jnp.concatenate([total[h : h + count] for h in range(0, total.shape[0], count)], axis=1)
     scale = lax.rsqrt(jnp.sum(raw * raw, axis=-1, keepdims=True) + 1e-6)
     inner = jnp.sum(total * raw, axis=-1, keepdims=True)
     grad = scale * total - scale * scale * scale * inner * raw
@@ -255,8 +260,8 @@
     return jnp.sum(copies(x.astype(BF16), axes, count).astype(F32), axis=0)
 
 
-def shift(x, axis, count, step):
-    return lax.ppermute(x, axis, [(i, (i + step) % count) for i in range(count)]) if step else x
+def swap(x, axis, count, step):
+    return lax.ppermute(x, axis, [(i, i ^ step) for i in range(count)]) if step else x
 
 
 def per_device(sizes, embeddings, prototypes):
@@ -279,13 +284,14 @@
     column_call = call(functools.partial(column_body, modes), "column_sum", mass_shape, [WHOLE] * 2)
 
     raw_rows = embeddings.transpose(1, 0, 2).reshape(owned, width)
-    gathered = gather(gather(raw_rows, "z", nz), "x", nx)
+    raw_tiles = jnp.concatenate([raw_rows[:, h : h + LANES] for h in range(0, width, LANES)], axis=0)
+    gathered = gather(gather(raw_tiles, "z", nz), "x", nx)
     kernel, units, unit_protos, soft, mass = call(
         functools.partial(score_body, modes, own_samples),
         "scores",
         [shape((lines, local_protos), BF16), units_shape, shape((local_protos, width), BF16), row_shape, mass_shape],
         [WHOLE] * 2,
-        [pltpu.VMEM((width // LANES, lines, LANES), F32)],
+        [pltpu.VMEM(gathered.shape, F32)],
     )(gathered, prototypes)
 
     for _ in range(2):
@@ -299,7 +305,7 @@
         [SCALARS] + [WHOLE] * 3,
         [pltpu.VMEM((2 * lines, width), F32)],
     )(x_place, inverse, units, unit_protos)
-    pieces = [shift(piece, "x", nx, step) for step, piece in enumerate(pieces)]
+    pieces = [swap(piece, "x", nx, step) for step, piece in enumerate(pieces)]
     totals = sum_over(jnp.concatenate([row, soft], axis=0), ("x", "z"), nx * nz)
 
     proto_part = call(
@@ -308,7 +314,7 @@
     rows = call(
         functools.partial(combine_body, modes, own_samples),
         "combine",
-        shape((nz, owned, width), BF16),
+        shape((nz, owned * width // LANES, LANES), BF16),
         [SCALARS, WHOLE, ANYWHERE] + [WHOLE] * nx,
         [pltpu.VMEM((2, lines, LANES), F32), pltpu.VMEM((width // LANES, x_lines, LANES), F32)],
     )(x_place, totals, proto_part, *pieces)

time: 184 us -> 186 us (1.011)
  waiting for transfers between devices: 19.1 us -> 23.7 us
  blocking collectives: 113 us -> 111 us
    ppermute x3, waiting for transfers between devices: 2.03 us -> 5.69 us  [swap(): lax.ppermute(x, axis, [(i, i ^ step) for i in range(count)])]
where the time goes in v2:
time: 186 us; the launch traced here: 185 us
  blocking collectives  111 us (60%)
  starting transfers between devices  35.3 us (19%)
  waiting for transfers between devices  23.7 us (13%)
  Pallas kernels  10.5 us (6%)
  local copies, waits for them, and re-layouts  2.38 us (1%)
    all_to_all x6, blocking collectives, exchange(): return lax.all_to_all(x, axes, 0, 0, tiled=True)  97.3 us
    all_to_all x4, starting transfers between devices, exchange(): return lax.all_to_all(x, axes, 0, 0, tiled=True)  25.7 us
    all_to_all x4, waiting for transfers between devices, exchange(): return lax.all_to_all(x, axes, 0, 0, tiled=True)  18.1 us
    all_gather x1, blocking collectives, per_device(): proto_grad = lax.all_gather(proto_grad, dp, axis=0, tiled=True).astype(F32)  14.1 us
    ppermute x3, starting transfers between devices, swap(): lax.ppermute(x, axis, [(i, i ^ step) for i in range(count)])  9.58 us
    ppermute x3, waiting for transfers between devices, swap(): lax.ppermute(x, axis, [(i, i ^ step) for i in range(count)])  5.69 us
  transfers between devices with their start and end apart: 7, of which 5 were waited for; matrix products, arithmetic and copies ran while one was open for 1% of the time, Pallas kernels for 2%

profile of v2, /device:TPU:1, one launch (start us, length us, event | category | flops | bytes accessed | tf_op | source)
XLA Modules:
  0.0 185.3 jit_solution(16318337275575714408)
XLA Ops:
  1.4 27.4 %all_to_all.54 = bf16[16,24,128]{2,1,0:T(8,128)(2,1)S(1)} all-to-all(bf16[16,24,128]{2,1,0:T(8,128)(2,1)S(1)} %broadcast_in_dim.18), channel_id=1, replica_groups=mesh['y'=4,'core'=2,'x'=4,'z'=16] {'z'}, dimensions={0} | all-to-all | bytes 196608 | tf_op jit(solution)/shard_map/all_to_all | solution.py:248
  28.9 10.0 %all_to_all.55 = bf16[4,384,128]{2,1,0:T(8,128)(2,1)S(1)} all-to-all(bf16[4,384,128]{2,1,0:T(8,128)(2,1)S(1)} %broadcast_in_dim.20), channel_id=1, replica_groups=mesh['y'=4,'core'=2,'x'=4,'z'=16] {'x'}, dimensions={0} | all-to-all | bytes 786432 | tf_op jit(solution)/shard_map/all_to_all | solution.py:248
  38.9 1.5 scores.1
  40.5 13.1 %all_to_all.56 = bf16[8,24,128]{2,1,0:T(8,128)(2,1)S(1)} all-to-all(bf16[8,24,128]{2,1,0:T(8,128)(2,1)S(1)} %broadcast_in_dim.21), channel_id=1, replica_groups=mesh['y'=4,'core'=2,'x'=4,'z'=16] {'y','core'}, dimensions={0} | all-to-all | bytes 98304 | tf_op jit(solution)/shard_map/all_to_all | solution.py:248
  53.6 1.0 row_sum.3
  54.7 18.5 %all_to_all.57 = bf16[64,2,384]{2,1,0:T(2,128)(2,1)S(1)} all-to-all(bf16[64,2,384]{2,1,0:T(2,128)(2,1)S(1)} %broadcast_in_dim.22), channel_id=1, replica_groups=mesh['y'=4,'core'=2,'x'=4,'z'=16] {'x','z'}, dimensions={0} | all-to-all | bytes 196608 | tf_op jit(solution)/shard_map/all_to_all | solution.py:248
  73.5 9.9 %all_to_all.58 = bf16[8,24,128]{2,1,0:T(8,128)(2,1)S(1)} all-to-all(bf16[8,24,128]{2,1,0:T(8,128)(2,1)S(1)} %broadcast_in_dim.23), channel_id=1, replica_groups=mesh['y'=4,'core'=2,'x'=4,'z'=16] {'y','core'}, dimensions={0} | all-to-all | bytes 98304 | tf_op jit(solution)/shard_map/all_to_all | solution.py:248
  84.4 18.3 %all_to_all.59 = bf16[64,2,384]{2,1,0:T(2,128)(2,1)S(1)} all-to-all(bf16[64,2,384]{2,1,0:T(2,128)(2,1)S(1)} %broadcast_in_dim.24), channel_id=1, replica_groups=mesh['y'=4,'core'=2,'x'=4,'z'=16] {'x','z'}, dimensions={0} | all-to-all | bytes 196608 | tf_op jit(solution)/shard_map/all_to_all | solution.py:248
  103.7 6.0 %all-to-all-start.6 = ((bf16[8,24,128]{2,1,0:T(8,128)(2,1)}), bf16[8,24,128]{2,1,0:T(8,128)(2,1)S(1)}, u32[]{:S(2)}, u32[]{:S(2)}) async-start(bf16[8,24,128]{2,1,0:T(8,128)(2,1)} %broadcast_in_dim.25), calls=%async_computation.6 | async-start | bytes 98304 | tf_op jit(solution)/shard_map/all_to_all | solution.py:248
  109.7 4.8 %all-to-all-done.6 = bf16[8,24,128]{2,1,0:T(8,128)(2,1)S(1)} async-done(((bf16[8,24,128]{2,1,0:T(8,128)(2,1)}), bf16[8,24,128]{2,1,0:T(8,128)(2,1)S(1)}, u32[]{:S(2)}, u32[]{:S(2)}) %all-to-all-start.6) | async-done | bytes 49184 | tf_op jit(solution)/shard_map/all_to_all | solution.py:248
  115.8 4.8 %all-to-all-start.7 = ((bf16[64,4,384]{2,1,0:T(4,128)(2,1)}), bf16[64,4,384]{2,1,0:T(4,128)(2,1)S(1)}, u32[]{:S(2)}, u32[]{:S(2)}) async-start(bf16[64,4,384]{2,1,0:T(4,128)(2,1)} %broadcast_in_dim.26), calls=%async_computation.7 | async-start | bytes 393216 | tf_op jit(solution)/shard_map/all_to_all | solution.py:248
  120.6 1.6 pull.1
  122.3 2.9 %collective-permute-start = (bf16[384,256]{1,0:T(8,128)(2,1)S(1)}, bf16[384,256]{1,0:T(8,128)(2,1)S(1)}, u32[]{:S(2)}, u32[]{:S(2)}) collective-permute-start(bf16[384,256]{1,0:T(8,128)(2,1)S(1)} %get-tuple-element.27), channel_id=1, source_target_pairs={{0,16},{16,0},{32,48},{48,32},{1,17},{17,1},{33,49},{49,33},{2,18}... | collective-permute-start | bytes 589832 | tf_op jit(solution)/shard_map/ppermute | solution.py:264
  125.2 4.5 %collective-permute-start.1 = (bf16[384,256]{1,0:T(8,128)(2,1)S(1)}, bf16[384,256]{1,0:T(8,128)(2,1)S(1)}, u32[]{:S(2)}, u32[]{:S(2)}) collective-permute-start(bf16[384,256]{1,0:T(8,128)(2,1)S(1)} %get-tuple-element.28), channel_id=1, source_target_pairs={{0,32},{16,48},{32,0},{48,16},{1,33},{17,49},{33,1},{49,17},{2,34}... | collective-permute-start | bytes 589832 | tf_op jit(solution)/shard_map/ppermute | solution.py:264
  129.7 2.2 %collective-permute-start.2 = (bf16[384,256]{1,0:T(8,128)(2,1)S(1)}, bf16[384,256]{1,0:T(8,128)(2,1)S(1)}, u32[]{:S(2)}, u32[]{:S(2)}) collective-permute-start(bf16[384,256]{1,0:T(8,128)(2,1)S(1)} %get-tuple-element.29), channel_id=1, source_target_pairs={{0,48},{16,32},{32,16},{48,0},{1,49},{17,33},{33,17},{49,1},{2,50}... | collective-permute-start | bytes 589832 | tf_op jit(solution)/shard_map/ppermute | solution.py:264
  131.9 4.9 %all-to-all-done.7 = bf16[64,4,384]{2,1,0:T(4,128)(2,1)S(1)} async-done(((bf16[64,4,384]{2,1,0:T(4,128)(2,1)}), bf16[64,4,384]{2,1,0:T(4,128)(2,1)S(1)}, u32[]{:S(2)}, u32[]{:S(2)}) %all-to-all-start.7) | async-done | bytes 196640 | tf_op jit(solution)/shard_map/all_to_all | solution.py:248
  137.5 5.0 %collective-permute-done.2.refs_3_ = bf16[384,256]{1,0:T(8,128)(2,1)S(1)} collective-permute-done((bf16[384,256]{1,0:T(8,128)(2,1)S(1)}, bf16[384,256]{1,0:T(8,128)(2,1)S(1)}, u32[]{:S(2)}, u32[]{:S(2)}) %collective-permute-start.2) | collective-permute-done | bytes 196640 | tf_op jit(solution)/shard_map/ppermute | solution.py:264
  142.5 2.3 %proto_part.1.tied_ref = bf16[1024,256]{1,0:T(8,128)(2,1)} custom-call(f32[4,384]{1,0:T(4,128)S(1)} %convert_reduce_fusion.totals_ref, f32[24,128]{1,0:T(8,128)S(1)} %get-tuple-element.23.inverse_ref, bf16[768,256]{1,0:T(8,128)(2,1)S(1)} %get-tuple-element.24.units_ref, bf16[1024,256]{1,0:T(8,128)(2,1)S(1)} %get-tuple-element.25.unit_protos_ref, ...), custom_call_target="tpu_custom_call" | custom-call | tf_op jit(solution)/shard_map/proto_part/pallas_call | solution.py:311
  144.8 4.2 %all-to-all-start.8 = ((bf16[8,128,256]{2,1,0:T(8,128)(2,1)}), bf16[8,128,256]{2,1,0:T(8,128)(2,1)S(1)}, u32[]{:S(2)}, u32[]{:S(2)}) async-start(bf16[8,128,256]{2,1,0:T(8,128)(2,1)} %bitcast.5), calls=%async_computation.8 | async-start | bytes 1048576 | tf_op jit(solution)/shard_map/all_to_all | solution.py:248
  149.0 1.2 combine.1.tied_ref
  150.2 8.3 %all-to-all-done.8.parts_ref = bf16[8,128,256]{2,1,0:T(8,128)(2,1)S(1)} async-done(((bf16[8,128,256]{2,1,0:T(8,128)(2,1)}), bf16[8,128,256]{2,1,0:T(8,128)(2,1)S(1)}, u32[]{:S(2)}, u32[]{:S(2)}) %all-to-all-start.8) | async-done | bytes 524320 | tf_op jit(solution)/shard_map/all_to_all | solution.py:248
  158.7 10.7 %all-to-all-start.9 = ((bf16[16,24,128]{2,1,0:T(8,128)(2,1)}), bf16[16,24,128]{2,1,0:T(8,128)(2,1)S(1)}, u32[]{:S(2)}, u32[]{:S(2)}) async-start(bf16[16,24,128]{2,1,0:T(8,128)(2,1)} %get-tuple-element.30), calls=%async_computation.9 | async-start | bytes 196608 | tf_op jit(solution)/shard_map/all_to_all | solution.py:248
  169.4 14.1 %all_gather.3 = bf16[1024,256]{1,0:T(8,128)(2,1)S(1)} all-gather(bf16[128,256]{1,0:T(8,128)(2,1)S(1)} %get-tuple-element.31), channel_id=1, replica_groups=mesh['y'=4,'core'=2,'x'=4,'z'=16] {'y','core'}, dimensions={0}, use_global_device_ids=true | all-gather | bytes 589824 | tf_op jit(solution)/shard_map/all_gather | solution.py:332
  183.5 1.0 convert_element_type.52
  (36 shorter events, 6.2 us)
Async XLA Ops:
  0.6 38.3 %copy-start = (bf16[1024,256]{1,0:T(8,128)(2,1)S(1)}, bf16[1024,256]{1,0:T(8,128)(2,1)}, u32[]{:S(2)}) copy-start(bf16[1024,256]{1,0:T(8,128)(2,1)} %protos_ref.3) | copy-start | bytes 1572868
  103.7 10.8 %all-to-all-start.6 = ((bf16[8,24,128]{2,1,0:T(8,128)(2,1)}), bf16[8,24,128]{2,1,0:T(8,128)(2,1)S(1)}, u32[]{:S(2)}, u32[]{:S(2)}) async-start(bf16[8,24,128]{2,1,0:T(8,128)(2,1)} %broadcast_in_dim.25), calls=%async_computation.6 | async-start | bytes 98304 | tf_op jit(solution)/shard_map/all_to_all | solution.py:248
  115.8 21.0 %all-to-all-start.7 = ((bf16[64,4,384]{2,1,0:T(4,128)(2,1)}), bf16[64,4,384]{2,1,0:T(4,128)(2,1)S(1)}, u32[]{:S(2)}, u32[]{:S(2)}) async-start(bf16[64,4,384]{2,1,0:T(4,128)(2,1)} %broadcast_in_dim.26), calls=%async_computation.7 | async-start | bytes 393216 | tf_op jit(solution)/shard_map/all_to_all | solution.py:248
  122.3 14.6 %collective-permute-start = (bf16[384,256]{1,0:T(8,128)(2,1)S(1)}, bf16[384,256]{1,0:T(8,128)(2,1)S(1)}, u32[]{:S(2)}, u32[]{:S(2)}) collective-permute-start(bf16[384,256]{1,0:T(8,128)(2,1)S(1)} %get-tuple-element.27), channel_id=1, source_target_pairs={{0,16},{16,0},{32,48},{48,32},{1,17},{17,1},{33,49},{49,33},{2,18}... | collective-permute-start | bytes 589832 | tf_op jit(solution)/shard_map/ppermute | solution.py:264
  125.2 12.3 %collective-permute-start.1 = (bf16[384,256]{1,0:T(8,128)(2,1)S(1)}, bf16[384,256]{1,0:T(8,128)(2,1)S(1)}, u32[]{:S(2)}, u32[]{:S(2)}) collective-permute-start(bf16[384,256]{1,0:T(8,128)(2,1)S(1)} %get-tuple-element.28), channel_id=1, source_target_pairs={{0,32},{16,48},{32,0},{48,16},{1,33},{17,49},{33,1},{49,17},{2,34}... | collective-permute-start | bytes 589832 | tf_op jit(solution)/shard_map/ppermute | solution.py:264
  129.7 12.8 %collective-permute-start.2 = (bf16[384,256]{1,0:T(8,128)(2,1)S(1)}, bf16[384,256]{1,0:T(8,128)(2,1)S(1)}, u32[]{:S(2)}, u32[]{:S(2)}) collective-permute-start(bf16[384,256]{1,0:T(8,128)(2,1)S(1)} %get-tuple-element.29), channel_id=1, source_target_pairs={{0,48},{16,32},{32,16},{48,0},{1,49},{17,33},{33,17},{49,1},{2,50}... | collective-permute-start | bytes 589832 | tf_op jit(solution)/shard_map/ppermute | solution.py:264
  144.8 13.7 %all-to-all-start.8 = ((bf16[8,128,256]{2,1,0:T(8,128)(2,1)}), bf16[8,128,256]{2,1,0:T(8,128)(2,1)S(1)}, u32[]{:S(2)}, u32[]{:S(2)}) async-start(bf16[8,128,256]{2,1,0:T(8,128)(2,1)} %bitcast.5), calls=%async_computation.8 | async-start | bytes 1048576 | tf_op jit(solution)/shard_map/all_to_all | solution.py:248
  158.7 25.9 %all-to-all-start.9 = ((bf16[16,24,128]{2,1,0:T(8,128)(2,1)}), bf16[16,24,128]{2,1,0:T(8,128)(2,1)S(1)}, u32[]{:S(2)}, u32[]{:S(2)}) async-start(bf16[16,24,128]{2,1,0:T(8,128)(2,1)} %get-tuple-element.30), calls=%async_computation.9 | async-start | bytes 196608 | tf_op jit(solution)/shard_map/all_to_all | solution.py:248

commit v3 on v2

--- a/solution.py
+++ b/solution.py
@@ -139,62 +139,38 @@
         line_to_tiles(mass_ref, m * (width // LANES), line[0:1] + line[1:2])
 
 
-def pull_body(modes, owned, place_ref, inverse_ref, units_ref, unit_protos_ref, *refs):
-    pieces, grad32 = refs[:-1], refs[-1]
+def unit_body(modes, owned, place_ref, totals_ref, inverse_ref, units_ref, unit_protos_ref, tied_ref, *refs):
+    pieces, (weights, sums) = refs[:-2], refs[-2:]
     samples = units_ref.shape[0] // modes
     width = unit_protos_ref.shape[0]
     tiles = width // LANES
     chunk = samples // owned // len(pieces)
-    for m in range(modes):
-        units = units_ref[m * samples : (m + 1) * samples, :]
-        soft = jnp.exp(10.0 * lax.dot_general(units, unit_protos_ref[...], NT, preferred_element_type=F32))
-        codes = soft * soft * tiles_to_line(inverse_ref[...], m * tiles, tiles)
-        for part, value in enumerate((soft, codes)):
-            first = (part * modes + m) * samples
-            grad32[first : first + samples, :] = jnp.dot(
-                value.astype(BF16), unit_protos_ref[...], preferred_element_type=F32
-            )
+    weights[0] = upright(COEFFICIENT / totals_ref[0:2])
+    weights[1] = upright(2.0 * COEFFICIENT / totals_ref[2:4])
+    step = 512
+    for k in range(0, width, step):
+        protos = unit_protos_ref[k : k + step, :]
+        scores = lax.dot_general(units_ref[...], protos, NT, preferred_element_type=F32)
+        codes, predicted = [], []
+        for m in range(modes):
+            rows = slice(m * samples, (m + 1) * samples)
+            soft = jnp.exp(10.0 * scores[rows])
+            inverse = tiles_to_line(inverse_ref[...], m * tiles + k // LANES, step // LANES)
+            codes.append(soft * soft * inverse * jnp.concatenate([weights[0, rows, :]] * (step // LANES), axis=1))
+            predicted.append(soft * jnp.concatenate([weights[1, rows, :]] * (step // LANES), axis=1))
+        for m in range(modes):
+            rows = slice(m * samples, (m + 1) * samples)
+            logit = predicted[m] - functools.reduce(jnp.add, [codes[n] for n in range(modes) if n != m])
+            part = jnp.dot(logit.astype(BF16), protos, preferred_element_type=F32)
+            sums[rows, :] = part if k == 0 else sums[rows, :] + part
     for step, piece in enumerate(pieces):
         place = lax.bitwise_xor(place_ref[0], jnp.int32(step)) * chunk
-        for j in range(2 * modes * owned):
+        for j in range(modes * owned):
             first = pl.multiple_of(place + j * (samples // owned), chunk)
-            piece[j * chunk : (j + 1) * chunk, :] = grad32[pl.ds(first, chunk), :].astype(BF16)
-
-
-def combine_body(modes, owned, place_ref, totals_ref, tied_ref, *refs):
-    pieces, (rows_ref, weights, unit) = refs[:-3], refs[-3:]
-    total = functools.reduce(jnp.add, [piece[...].astype(F32) for piece in pieces])
-    height = total.shape[0] // 2
-    chunk = height // (modes * owned)
-    weights[0] = upright(COEFFICIENT / totals_ref[0:2])
-    weights[1] = upright(2.0 * COEFFICIENT / totals_ref[2:4])
-    samples = weights.shape[1] // modes
-
-    def weighted(kind, first, m):
-        factor = jnp.concatenate(
-            [
-                weights[kind, pl.ds(pl.multiple_of(m * samples + (i * len(pieces) + place_ref[0]) * chunk, chunk), chunk), :]
-                for i in range(owned)
-            ],
-            axis=0,
-        )
-        block = total[first + m * owned * chunk : first + (m + 1) * owned * chunk]
-        return block * jnp.concatenate([factor] * (block.shape[1] // LANES), axis=1)
-
-    codes = [weighted(0, height, m) for m in range(modes)]
-    for m in range(modes):
-        others = [codes[n] for n in range(modes) if n != m]
-        grad = weighted(1, 0, m) - functools.reduce(jnp.add, others)
-        for h in range(unit.shape[0]):
-            unit[h, m * owned * chunk : (m + 1) * owned * chunk, :] = grad[:, h * LANES : (h + 1) * LANES]
-    for j in range(rows_ref.shape[0]):
-        rows_ref[j] = jnp.concatenate(
-            [unit[h, pl.ds(j, modes * owned, stride=chunk), :] for h in range(unit.shape[0])], axis=0
-        ).astype(BF16)
-
-
-def proto_body(modes, totals_ref, inverse_ref, units_ref, unit_protos_ref, *refs):
-    proto_ref = refs[-1]
+            piece[j * chunk : (j + 1) * chunk, :] = sums[pl.ds(first, chunk), :].astype(BF16)
+
+
+def proto_body(modes, totals_ref, inverse_ref, units_ref, unit_protos_ref, proto_ref):
     samples = units_ref.shape[0] // modes
     width = unit_protos_ref.shape[0]
     tiles = width // LANES
@@ -222,13 +198,22 @@
         ).astype(BF16)
 
 
-def middle_body(place_ref, parts_ref, protos_ref, tied_ref, grad_ref, tied_out_ref):
+def middle_body(place_ref, parts_ref, protos_ref, *refs):
+    pieces, (grad_ref, rows_ref, unit) = refs[:-3], refs[-3:]
     total = jnp.sum(parts_ref[...].astype(F32), axis=0)
     share = total.shape[0]
     raw = protos_ref[pl.ds(pl.multiple_of(place_ref[0] * share, share), share), :].astype(F32)
     scale = lax.rsqrt(jnp.sum(raw * raw, axis=-1, keepdims=True) + 1e-6)
     inner = jnp.sum(total * raw, axis=-1, keepdims=True)
     grad_ref[...] = (scale * total - scale * scale * scale * inner * raw).astype(BF16)
+    total = functools.reduce(jnp.add, [piece[...].astype(F32) for piece in pieces])
+    for h in range(unit.shape[0]):
+        unit[h] = total[:, h * LANES : (h + 1) * LANES]
+    cuts = rows_ref.shape[0]
+    for j in range(cuts):
+        rows_ref[j] = jnp.concatenate(
+            [unit[h, pl.ds(j, unit.shape[1] // cuts, stride=cuts), :] for h in range(unit.shape[0])], axis=0
+        ).astype(BF16)
 
 
 def last_body(parts_ref, raw_ref, grad_ref):
@@ -298,36 +283,27 @@
         row, _ = row_call(sum_over(mass, dp, groups), kernel)
         mass = column_call(sum_over(row, ("x", "z"), nx * nz), kernel)
     row, inverse = row_call(sum_over(mass, dp, groups), kernel)
+    totals = sum_over(jnp.concatenate([row, soft], axis=0), ("x", "z"), nx * nz)
+
+    proto_part = call(
+        functools.partial(proto_body, modes), "proto_part", shape((local_protos, width), BF16), [WHOLE] * 4
+    )(totals, inverse, units, unit_protos)
     pieces = call(
-        functools.partial(pull_body, modes, own_samples),
-        "pull",
-        [shape((2 * x_lines, width), BF16)] * nx,
-        [SCALARS] + [WHOLE] * 3,
-        [pltpu.VMEM((2 * lines, width), F32)],
-    )(x_place, inverse, units, unit_protos)
+        functools.partial(unit_body, modes, own_samples),
+        "unit_grad",
+        [shape((x_lines, width), BF16)] * nx,
+        [SCALARS] + [WHOLE] * 4 + [ANYWHERE],
+        [pltpu.VMEM((2, lines, LANES), F32), pltpu.VMEM((lines, width), F32)],
+    )(x_place, totals, inverse, units, unit_protos, proto_part)
+    proto_part = exchange(proto_part, dp).reshape(groups, local_protos // groups, width)
     pieces = [swap(piece, "x", nx, step) for step, piece in enumerate(pieces)]
-    totals = sum_over(jnp.concatenate([row, soft], axis=0), ("x", "z"), nx * nz)
-
-    proto_part = call(
-        functools.partial(proto_body, modes), "proto_part", shape((local_protos, width), BF16), [WHOLE] * 4 + [ANYWHERE] * nx
-    )(totals, inverse, units, unit_protos, *pieces)
-    rows = call(
-        functools.partial(combine_body, modes, own_samples),
-        "combine",
-        shape((nz, owned * width // LANES, LANES), BF16),
-        [SCALARS, WHOLE, ANYWHERE] + [WHOLE] * nx,
-        [pltpu.VMEM((2, lines, LANES), F32), pltpu.VMEM((width // LANES, x_lines, LANES), F32)],
-    )(x_place, totals, proto_part, *pieces)
-    proto_part = exchange(proto_part, dp).reshape(groups, local_protos // groups, width)
     proto_grad, rows = call(
         middle_body,
         "middle",
-        [shape((local_protos // groups, width), BF16), shape(rows.shape, BF16)],
-        [SCALARS, WHOLE, WHOLE, ANYWHERE],
-        (),
-        [WHOLE, ANYWHERE],
-        {3: 1},
-    )(dp_place, proto_part, prototypes, rows)
+        [shape((local_protos // groups, width), BF16), shape((nz, owned * width // LANES, LANES), BF16)],
+        [SCALARS] + [WHOLE] * (2 + nx),
+        [pltpu.VMEM((width // LANES, x_lines, LANES), F32)],
+    )(dp_place, proto_part, prototypes, *pieces)
     rows = exchange(rows, "z")
     proto_grad = lax.all_gather(proto_grad, dp, axis=0, tiled=True).astype(F32)
     embed_grad = call(last_body, "last", shape((modes, own_samples, width), F32), [WHOLE] * 2)(rows, raw_rows)

time: 186 us -> 183 us (0.984)
  blocking collectives: 111 us -> 134 us
  waiting for transfers between devices: 23.7 us -> 9.35 us
  starting transfers between devices: 35.3 us -> 25.5 us
    all_to_all x6 -> x7, blocking collectives: 97.3 us -> 118 us  [exchange(): return lax.all_to_all(x, axes, 0, 0, tiled=True)]
    all_to_all x4 -> x3, waiting for transfers between devices: 18.1 us -> 4.8 us  [exchange(): return lax.all_to_all(x, axes, 0, 0, tiled=True)]
    all_to_all x4 -> x3, starting transfers between devices: 25.7 us -> 15.9 us  [exchange(): return lax.all_to_all(x, axes, 0, 0, tiled=True)]
  transfers between devices with their start and end apart: 7 -> 6, of which waited for: 5 -> 3; matrix products, arithmetic and copies ran while one was open for 1% -> 1% of each run, Pallas kernels for 2% -> 1%
where the time goes in v3:
time: 183 us; the launch traced here: 182 us
  blocking collectives  134 us (73%)
  starting transfers between devices  25.5 us (14%)
  Pallas kernels  10.1 us (6%)
  waiting for transfers between devices  9.35 us (5%)
    all_to_all x7, blocking collectives, exchange(): return lax.all_to_all(x, axes, 0, 0, tiled=True)  118 us
    all_to_all x3, starting transfers between devices, exchange(): return lax.all_to_all(x, axes, 0, 0, tiled=True)  15.9 us
    all_gather x1, blocking collectives, per_device(): proto_grad = lax.all_gather(proto_grad, dp, axis=0, tiled=True).astype(F32)  15.5 us
    ppermute x3, starting transfers between devices, swap(): lax.ppermute(x, axis, [(i, i ^ step) for i in range(count)])  9.62 us
    all_to_all x3, waiting for transfers between devices, exchange(): return lax.all_to_all(x, axes, 0, 0, tiled=True)  4.8 us
    ppermute x3, waiting for transfers between devices, swap(): lax.ppermute(x, axis, [(i, i ^ step) for i in range(count)])  4.55 us
  transfers between devices with their start and end apart: 6, of which 3 were waited for; matrix products, arithmetic and copies ran while one was open for 1% of the time, Pallas kernels for 1%

profile of v3, /device:TPU:1, one launch (start us, length us, event | category | flops | bytes accessed | tf_op | source)
XLA Modules:
  0.0 182.1 jit_solution(6543620933015341640)
XLA Ops:
  1.4 27.4 %all_to_all.54 = bf16[16,24,128]{2,1,0:T(8,128)(2,1)S(1)} all-to-all(bf16[16,24,128]{2,1,0:T(8,128)(2,1)S(1)} %broadcast_in_dim.18), channel_id=1, replica_groups=mesh['y'=4,'core'=2,'x'=4,'z'=16] {'z'}, dimensions={0} | all-to-all | bytes 196608 | tf_op jit(solution)/shard_map/all_to_all | solution.py:233
  28.9 10.0 %all_to_all.55 = bf16[4,384,128]{2,1,0:T(8,128)(2,1)S(1)} all-to-all(bf16[4,384,128]{2,1,0:T(8,128)(2,1)S(1)} %broadcast_in_dim.20), channel_id=1, replica_groups=mesh['y'=4,'core'=2,'x'=4,'z'=16] {'x'}, dimensions={0} | all-to-all | bytes 786432 | tf_op jit(solution)/shard_map/all_to_all | solution.py:233
  38.9 1.5 scores.1
  40.5 13.1 %all_to_all.56 = bf16[8,24,128]{2,1,0:T(8,128)(2,1)S(1)} all-to-all(bf16[8,24,128]{2,1,0:T(8,128)(2,1)S(1)} %broadcast_in_dim.21), channel_id=1, replica_groups=mesh['y'=4,'core'=2,'x'=4,'z'=16] {'y','core'}, dimensions={0} | all-to-all | bytes 98304 | tf_op jit(solution)/shard_map/all_to_all | solution.py:233
  53.6 1.0 row_sum.3
  54.7 18.5 %all_to_all.57 = bf16[64,2,384]{2,1,0:T(2,128)(2,1)S(1)} all-to-all(bf16[64,2,384]{2,1,0:T(2,128)(2,1)S(1)} %broadcast_in_dim.22), channel_id=1, replica_groups=mesh['y'=4,'core'=2,'x'=4,'z'=16] {'x','z'}, dimensions={0} | all-to-all | bytes 196608 | tf_op jit(solution)/shard_map/all_to_all | solution.py:233
  73.5 9.9 %all_to_all.58 = bf16[8,24,128]{2,1,0:T(8,128)(2,1)S(1)} all-to-all(bf16[8,24,128]{2,1,0:T(8,128)(2,1)S(1)} %broadcast_in_dim.23), channel_id=1, replica_groups=mesh['y'=4,'core'=2,'x'=4,'z'=16] {'y','core'}, dimensions={0} | all-to-all | bytes 98304 | tf_op jit(solution)/shard_map/all_to_all | solution.py:233
  83.4 1.0 row_sum.4
  84.4 18.3 %all_to_all.59 = bf16[64,2,384]{2,1,0:T(2,128)(2,1)S(1)} all-to-all(bf16[64,2,384]{2,1,0:T(2,128)(2,1)S(1)} %broadcast_in_dim.24), channel_id=1, replica_groups=mesh['y'=4,'core'=2,'x'=4,'z'=16] {'x','z'}, dimensions={0} | all-to-all | bytes 196608 | tf_op jit(solution)/shard_map/all_to_all | solution.py:233
  103.7 6.0 %all-to-all-start.6 = ((bf16[8,24,128]{2,1,0:T(8,128)(2,1)}), bf16[8,24,128]{2,1,0:T(8,128)(2,1)S(1)}, u32[]{:S(2)}, u32[]{:S(2)}) async-start(bf16[8,24,128]{2,1,0:T(8,128)(2,1)} %broadcast_in_dim.25), calls=%async_computation.6 | async-start | bytes 98304 | tf_op jit(solution)/shard_map/all_to_all | solution.py:233
  109.7 4.8 %all-to-all-done.6 = bf16[8,24,128]{2,1,0:T(8,128)(2,1)S(1)} async-done(((bf16[8,24,128]{2,1,0:T(8,128)(2,1)}), bf16[8,24,128]{2,1,0:T(8,128)(2,1)S(1)}, u32[]{:S(2)}, u32[]{:S(2)}) %all-to-all-start.6) | async-done | bytes 49184 | tf_op jit(solution)/shard_map/all_to_all | solution.py:233
  115.1 20.8 %all_to_all.60 = bf16[64,4,384]{2,1,0:T(4,128)(2,1)S(1)} all-to-all(bf16[64,4,384]{2,1,0:T(4,128)(2,1)S(1)} %broadcast_in_dim.26), channel_id=1, replica_groups=mesh['y'=4,'core'=2,'x'=4,'z'=16] {'x','z'}, dimensions={0} | all-to-all | bytes 393216 | tf_op jit(solution)/shard_map/all_to_all | solution.py:233
  135.9 2.3 %proto_part.1.tied_ref = bf16[1024,256]{1,0:T(8,128)(2,1)} custom-call(f32[4,384]{1,0:T(4,128)S(1)} %convert_reduce_fusion.totals_ref, f32[24,128]{1,0:T(8,128)S(1)} %get-tuple-element.23.inverse_ref, bf16[768,256]{1,0:T(8,128)(2,1)S(1)} %get-tuple-element.24.units_ref, bf16[1024,256]{1,0:T(8,128)(2,1)S(1)} %get-tuple-element.25.unit_protos_ref), custom_call_target="tpu_custom_call" | custom-call | tf_op jit(solution)/shard_map/proto_part/pallas_call | solution.py:288
  138.3 6.4 %all-to-all-start.8 = ((bf16[8,128,256]{2,1,0:T(8,128)(2,1)}), bf16[8,128,256]{2,1,0:T(8,128)(2,1)S(1)}, u32[]{:S(2)}, u32[]{:S(2)}) async-start(bf16[8,128,256]{2,1,0:T(8,128)(2,1)} %bitcast.4), calls=%async_computation.8 | async-start | bytes 1048576 | tf_op jit(solution)/shard_map/all_to_all | solution.py:233
  144.6 1.6 unit_grad.1
  146.3 3.1 %collective-permute-start = (bf16[192,256]{1,0:T(8,128)(2,1)S(1)}, bf16[192,256]{1,0:T(8,128)(2,1)S(1)}, u32[]{:S(2)}, u32[]{:S(2)}) collective-permute-start(bf16[192,256]{1,0:T(8,128)(2,1)S(1)} %get-tuple-element.27), channel_id=1, source_target_pairs={{0,16},{16,0},{32,48},{48,32},{1,17},{17,1},{33,49},{49,33},{2,18}... | collective-permute-start | bytes 294920 | tf_op jit(solution)/shard_map/ppermute | solution.py:249
  149.4 4.5 %collective-permute-start.1 = (bf16[192,256]{1,0:T(8,128)(2,1)S(1)}, bf16[192,256]{1,0:T(8,128)(2,1)S(1)}, u32[]{:S(2)}, u32[]{:S(2)}) collective-permute-start(bf16[192,256]{1,0:T(8,128)(2,1)S(1)} %get-tuple-element.28), channel_id=1, source_target_pairs={{0,32},{16,48},{32,0},{48,16},{1,33},{17,49},{33,1},{49,17},{2,34}... | collective-permute-start | bytes 294920 | tf_op jit(solution)/shard_map/ppermute | solution.py:249
  153.9 2.0 %collective-permute-start.2 = (bf16[192,256]{1,0:T(8,128)(2,1)S(1)}, bf16[192,256]{1,0:T(8,128)(2,1)S(1)}, u32[]{:S(2)}, u32[]{:S(2)}) collective-permute-start(bf16[192,256]{1,0:T(8,128)(2,1)S(1)} %get-tuple-element.29), channel_id=1, source_target_pairs={{0,48},{16,32},{32,16},{48,0},{1,49},{17,33},{33,17},{49,1},{2,50}... | collective-permute-start | bytes 294920 | tf_op jit(solution)/shard_map/ppermute | solution.py:249
  155.9 0.8 collective-permute-done.1.refs_2_
  156.7 3.8 %collective-permute-done.2.refs_3_ = bf16[192,256]{1,0:T(8,128)(2,1)S(1)} collective-permute-done((bf16[192,256]{1,0:T(8,128)(2,1)S(1)}, bf16[192,256]{1,0:T(8,128)(2,1)S(1)}, u32[]{:S(2)}, u32[]{:S(2)}) %collective-permute-start.2) | collective-permute-done | bytes 98336 | tf_op jit(solution)/shard_map/ppermute | solution.py:249
  160.5 0.9 middle.1
  161.3 3.5 %all-to-all-start.9 = ((bf16[16,24,128]{2,1,0:T(8,128)(2,1)}), bf16[16,24,128]{2,1,0:T(8,128)(2,1)S(1)}, u32[]{:S(2)}, u32[]{:S(2)}) async-start(bf16[16,24,128]{2,1,0:T(8,128)(2,1)} %get-tuple-element.30), calls=%async_computation.9 | async-start | bytes 196608 | tf_op jit(solution)/shard_map/all_to_all | solution.py:233
  164.9 15.5 %all_gather.3 = bf16[1024,256]{1,0:T(8,128)(2,1)S(1)} all-gather(bf16[128,256]{1,0:T(8,128)(2,1)S(1)} %get-tuple-element.31), channel_id=1, replica_groups=mesh['y'=4,'core'=2,'x'=4,'z'=16] {'y','core'}, dimensions={0}, use_global_device_ids=true | all-gather | bytes 589824 | tf_op jit(solution)/shard_map/all_gather | solution.py:308
  180.4 1.0 convert_element_type.52
  (34 shorter events, 3.7 us)
Async XLA Ops:
  0.6 38.3 %copy-start = (bf16[1024,256]{1,0:T(8,128)(2,1)S(1)}, bf16[1024,256]{1,0:T(8,128)(2,1)}, u32[]{:S(2)}) copy-start(bf16[1024,256]{1,0:T(8,128)(2,1)} %protos_ref.3) | copy-start | bytes 1572868
  103.7 10.8 %all-to-all-start.6 = ((bf16[8,24,128]{2,1,0:T(8,128)(2,1)}), bf16[8,24,128]{2,1,0:T(8,128)(2,1)S(1)}, u32[]{:S(2)}, u32[]{:S(2)}) async-start(bf16[8,24,128]{2,1,0:T(8,128)(2,1)} %broadcast_in_dim.25), calls=%async_computation.6 | async-start | bytes 98304 | tf_op jit(solution)/shard_map/all_to_all | solution.py:233
  138.3 22.2 %all-to-all-start.8 = ((bf16[8,128,256]{2,1,0:T(8,128)(2,1)}), bf16[8,128,256]{2,1,0:T(8,128)(2,1)S(1)}, u32[]{:S(2)}, u32[]{:S(2)}) async-start(bf16[8,128,256]{2,1,0:T(8,128)(2,1)} %bitcast.4), calls=%async_computation.8 | async-start | bytes 1048576 | tf_op jit(solution)/shard_map/all_to_all | solution.py:233
  146.3 9.6 %collective-permute-start = (bf16[192,256]{1,0:T(8,128)(2,1)S(1)}, bf16[192,256]{1,0:T(8,128)(2,1)S(1)}, u32[]{:S(2)}, u32[]{:S(2)}) collective-permute-start(bf16[192,256]{1,0:T(8,128)(2,1)S(1)} %get-tuple-element.27), channel_id=1, source_target_pairs={{0,16},{16,0},{32,48},{48,32},{1,17},{17,1},{33,49},{49,33},{2,18}... | collective-permute-start | bytes 294920 | tf_op jit(solution)/shard_map/ppermute | solution.py:249
  149.4 7.3 %collective-permute-start.1 = (bf16[192,256]{1,0:T(8,128)(2,1)S(1)}, bf16[192,256]{1,0:T(8,128)(2,1)S(1)}, u32[]{:S(2)}, u32[]{:S(2)}) collective-permute-start(bf16[192,256]{1,0:T(8,128)(2,1)S(1)} %get-tuple-element.28), channel_id=1, source_target_pairs={{0,32},{16,48},{32,0},{48,16},{1,33},{17,49},{33,1},{49,17},{2,34}... | collective-permute-start | bytes 294920 | tf_op jit(solution)/shard_map/ppermute | solution.py:249
  153.9 6.6 %collective-permute-start.2 = (bf16[192,256]{1,0:T(8,128)(2,1)S(1)}, bf16[192,256]{1,0:T(8,128)(2,1)S(1)}, u32[]{:S(2)}, u32[]{:S(2)}) collective-permute-start(bf16[192,256]{1,0:T(8,128)(2,1)S(1)} %get-tuple-element.29), channel_id=1, source_target_pairs={{0,48},{16,32},{32,16},{48,0},{1,49},{17,33},{33,17},{49,1},{2,50}... | collective-permute-start | bytes 294920 | tf_op jit(solution)/shard_map/ppermute | solution.py:249
  161.3 20.1 %all-to-all-start.9 = ((bf16[16,24,128]{2,1,0:T(8,128)(2,1)}), bf16[16,24,128]{2,1,0:T(8,128)(2,1)S(1)}, u32[]{:S(2)}, u32[]{:S(2)}) async-start(bf16[16,24,128]{2,1,0:T(8,128)(2,1)} %get-tuple-element.30), calls=%async_computation.9 | async-start | bytes 196608 | tf_op jit(solution)/shard_map/all_to_all | solution.py:233

commit v4 on v3

--- a/solution.py
+++ b/solution.py
@@ -114,18 +114,23 @@
     soft_ref[...] = lines_to_pair(lines)
 
 
-def row_body(modes, mass_ref, kernel_ref, row_ref, inverse_ref):
+def row_body(modes, mass_ref, kernel_ref, *refs):
     samples = kernel_ref.shape[0] // modes
     tiles = kernel_ref.shape[1] // LANES
     inverse = 1.0 / mass_ref[...]
-    inverse_ref[...] = inverse
     lines = []
     for m in range(modes):
         terms = two_terms(tiles_to_line(inverse, m * tiles, tiles))
         kernel = kernel_ref[m * samples : (m + 1) * samples, :]
         line = lax.dot_general(terms, kernel, NT, preferred_element_type=F32)
         lines.append(line[0:1] + line[1:2])
-    row_ref[...] = lines_to_pair(lines)
+    pair = lines_to_pair(lines)
+    if len(refs) == 1:
+        refs[0][...] = pair
+    else:
+        soft_ref, row_ref, inverse_ref = refs
+        row_ref[...] = jnp.concatenate([pair, soft_ref[...]], axis=0)
+        inverse_ref[...] = inverse
 
 
 def column_body(modes, row_ref, kernel_ref, mass_ref):
@@ -216,7 +221,8 @@
         ).astype(BF16)
 
 
-def last_body(parts_ref, raw_ref, grad_ref):
+def last_body(parts_ref, raw_ref, protos_ref, grad_ref, proto_grad_ref):
+    proto_grad_ref[...] = protos_ref[...].astype(F32)
     total = jnp.sum(parts_ref[...].astype(F32), axis=0)
     raw = raw_ref[...].astype(F32)
     count = raw.shape[0]
@@ -265,7 +271,10 @@
     dp_place = lax.axis_index(dp).reshape(1)
     x_place = lax.axis_index("x").reshape(1)
 
-    row_call = call(functools.partial(row_body, modes), "row_sum", [row_shape, mass_shape], [WHOLE] * 2)
+    row_call = call(functools.partial(row_body, modes), "row_sum", row_shape, [WHOLE] * 2)
+    last_row_call = call(
+        functools.partial(row_body, modes), "row_sum", [shape((4, lines // 2), F32), mass_shape], [WHOLE] * 3
+    )
     column_call = call(functools.partial(column_body, modes), "column_sum", mass_shape, [WHOLE] * 2)
 
     raw_rows = embeddings.transpose(1, 0, 2).reshape(owned, width)
@@ -280,10 +289,10 @@
     )(gathered, prototypes)
 
     for _ in range(2):
-        row, _ = row_call(sum_over(mass, dp, groups), kernel)
+        row = row_call(sum_over(mass, dp, groups), kernel)
         mass = column_call(sum_over(row, ("x", "z"), nx * nz), kernel)
-    row, inverse = row_call(sum_over(mass, dp, groups), kernel)
-    totals = sum_over(jnp.concatenate([row, soft], axis=0), ("x", "z"), nx * nz)
+    row, inverse = last_row_call(sum_over(mass, dp, groups), kernel, soft)
+    totals = sum_over(row, ("x", "z"), nx * nz)
 
     proto_part = call(
         functools.partial(proto_body, modes), "proto_part", shape((local_protos, width), BF16), [WHOLE] * 4
@@ -305,8 +314,13 @@
         [pltpu.VMEM((width // LANES, x_lines, LANES), F32)],
     )(dp_place, proto_part, prototypes, *pieces)
     rows = exchange(rows, "z")
-    proto_grad = lax.all_gather(proto_grad, dp, axis=0, tiled=True).astype(F32)
-    embed_grad = call(last_body, "last", shape((modes, own_samples, width), F32), [WHOLE] * 2)(rows, raw_rows)
+    proto_grad = lax.all_gather(proto_grad, dp, axis=0, tiled=True)
+    embed_grad, proto_grad = call(
+        last_body,
+        "last",
+        [shape((modes, own_samples, width), F32), shape((local_protos, width), F32)],
+        [WHOLE] * 3,
+    )(rows, raw_rows, proto_grad)
     return (embed_grad.transpose(1, 0, 2), proto_grad)
 
 

time: 183 us -> 180 us (0.984)
  blocking collectives: 134 us -> 143 us
  starting transfers between devices: 25.5 us -> 19.5 us
  waiting for transfers between devices: 9.35 us -> 4.52 us
    all_to_all x7 -> x8, blocking collectives: 118 us -> 128 us  [exchange(): return lax.all_to_all(x, axes, 0, 0, tiled=True)]
    all_to_all x3 -> x2, starting transfers between devices: 15.9 us -> 9.9 us  [exchange(): return lax.all_to_all(x, axes, 0, 0, tiled=True)]
    all_to_all x3 -> x2, waiting for transfers between devices: 4.8 us -> 0.01 us  [exchange(): return lax.all_to_all(x, axes, 0, 0, tiled=True)]
  transfers between devices with their start and end apart: 6 -> 5, of which waited for: 3 -> 2; matrix products, arithmetic and copies ran while one was open for 1% -> 0% of each run, Pallas kernels for 1% -> 1%
where the time goes in v4:
time: 180 us; the launch traced here: 179 us
  blocking collectives  143 us (79%)
  starting transfers between devices  19.5 us (11%)
  Pallas kernels  9.47 us (5%)
  waiting for transfers between devices  4.52 us (3%)
    all_to_all x8, blocking collectives, exchange(): return lax.all_to_all(x, axes, 0, 0, tiled=True)  128 us
    all_gather x1, blocking collectives, per_device(): proto_grad = lax.all_gather(proto_grad, dp, axis=0, tiled=True)  15.5 us
    all_to_all x2, starting transfers between devices, exchange(): return lax.all_to_all(x, axes, 0, 0, tiled=True)  9.9 us
    ppermute x3, starting transfers between devices, swap(): lax.ppermute(x, axis, [(i, i ^ step) for i in range(count)])  9.62 us
    ppermute x3, waiting for transfers between devices, swap(): lax.ppermute(x, axis, [(i, i ^ step) for i in range(count)])  4.51 us
  transfers between devices with their start and end apart: 5, of which 2 were waited for; matrix products, arithmetic and copies ran while one was open for 0% of the time, Pallas kernels for 1%

profile of v4, /device:TPU:1, one launch (start us, length us, event | category | flops | bytes accessed | tf_op | source)
XLA Modules:
  0.0 179.0 jit_solution(10117805483832712393)
XLA Ops:
  0.6 0.8 reshape.29.raw_ref
  1.4 27.4 %all_to_all.54 = bf16[16,24,128]{2,1,0:T(8,128)(2,1)S(1)} all-to-all(bf16[16,24,128]{2,1,0:T(8,128)(2,1)S(1)} %broadcast_in_dim.18), channel_id=1, replica_groups=mesh['y'=4,'core'=2,'x'=4,'z'=16] {'z'}, dimensions={0} | all-to-all | bytes 196608 | tf_op jit(solution)/shard_map/all_to_all | solution.py:239
  28.9 10.0 %all_to_all.55 = bf16[4,384,128]{2,1,0:T(8,128)(2,1)S(1)} all-to-all(bf16[4,384,128]{2,1,0:T(8,128)(2,1)S(1)} %broadcast_in_dim.20), channel_id=1, replica_groups=mesh['y'=4,'core'=2,'x'=4,'z'=16] {'x'}, dimensions={0} | all-to-all | bytes 786432 | tf_op jit(solution)/shard_map/all_to_all | solution.py:239
  38.9 1.5 scores.1
  40.5 13.1 %all_to_all.56 = bf16[8,24,128]{2,1,0:T(8,128)(2,1)S(1)} all-to-all(bf16[8,24,128]{2,1,0:T(8,128)(2,1)S(1)} %broadcast_in_dim.21), channel_id=1, replica_groups=mesh['y'=4,'core'=2,'x'=4,'z'=16] {'y','core'}, dimensions={0} | all-to-all | bytes 98304 | tf_op jit(solution)/shard_map/all_to_all | solution.py:239
  53.6 0.5 row_sum.3
  54.2 18.5 %all_to_all.57 = bf16[64,2,384]{2,1,0:T(2,128)(2,1)S(1)} all-to-all(bf16[64,2,384]{2,1,0:T(2,128)(2,1)S(1)} %broadcast_in_dim.22), channel_id=1, replica_groups=mesh['y'=4,'core'=2,'x'=4,'z'=16] {'x','z'}, dimensions={0} | all-to-all | bytes 196608 | tf_op jit(solution)/shard_map/all_to_all | solution.py:239
  73.1 9.9 %all_to_all.58 = bf16[8,24,128]{2,1,0:T(8,128)(2,1)S(1)} all-to-all(bf16[8,24,128]{2,1,0:T(8,128)(2,1)S(1)} %broadcast_in_dim.23), channel_id=1, replica_groups=mesh['y'=4,'core'=2,'x'=4,'z'=16] {'y','core'}, dimensions={0} | all-to-all | bytes 98304 | tf_op jit(solution)/shard_map/all_to_all | solution.py:239
  82.9 0.5 row_sum.4
  83.5 18.3 %all_to_all.59 = bf16[64,2,384]{2,1,0:T(2,128)(2,1)S(1)} all-to-all(bf16[64,2,384]{2,1,0:T(2,128)(2,1)S(1)} %broadcast_in_dim.24), channel_id=1, replica_groups=mesh['y'=4,'core'=2,'x'=4,'z'=16] {'x','z'}, dimensions={0} | all-to-all | bytes 196608 | tf_op jit(solution)/shard_map/all_to_all | solution.py:239
  102.2 9.9 %all_to_all.60 = bf16[8,24,128]{2,1,0:T(8,128)(2,1)S(1)} all-to-all(bf16[8,24,128]{2,1,0:T(8,128)(2,1)S(1)} %broadcast_in_dim.25), channel_id=1, replica_groups=mesh['y'=4,'core'=2,'x'=4,'z'=16] {'y','core'}, dimensions={0} | all-to-all | bytes 98304 | tf_op jit(solution)/shard_map/all_to_all | solution.py:239
  112.7 20.8 %all_to_all.61 = bf16[64,4,384]{2,1,0:T(4,128)(2,1)S(1)} all-to-all(bf16[64,4,384]{2,1,0:T(4,128)(2,1)S(1)} %broadcast_in_dim.26), channel_id=1, replica_groups=mesh['y'=4,'core'=2,'x'=4,'z'=16] {'x','z'}, dimensions={0} | all-to-all | bytes 393216 | tf_op jit(solution)/shard_map/all_to_all | solution.py:239
  133.5 2.3 %proto_part.1.tied_ref = bf16[1024,256]{1,0:T(8,128)(2,1)} custom-call(f32[4,384]{1,0:T(4,128)S(1)} %convert_reduce_fusion.totals_ref, f32[24,128]{1,0:T(8,128)S(1)} %get-tuple-element.21.inverse_ref, bf16[768,256]{1,0:T(8,128)(2,1)S(1)} %get-tuple-element.22.units_ref, bf16[1024,256]{1,0:T(8,128)(2,1)S(1)} %get-tuple-element.23.unit_protos_ref), custom_call_target="tpu_custom_call" | custom-call | tf_op jit(solution)/shard_map/proto_part/pallas_call | solution.py:297
  135.8 6.4 %all-to-all-start.8 = ((bf16[8,128,256]{2,1,0:T(8,128)(2,1)}), bf16[8,128,256]{2,1,0:T(8,128)(2,1)S(1)}, u32[]{:S(2)}, u32[]{:S(2)}) async-start(bf16[8,128,256]{2,1,0:T(8,128)(2,1)} %bitcast.4), calls=%async_computation.8 | async-start | bytes 1048576 | tf_op jit(solution)/shard_map/all_to_all | solution.py:239
  142.2 1.6 unit_grad.1
  143.9 3.1 %collective-permute-start = (bf16[192,256]{1,0:T(8,128)(2,1)S(1)}, bf16[192,256]{1,0:T(8,128)(2,1)S(1)}, u32[]{:S(2)}, u32[]{:S(2)}) collective-permute-start(bf16[192,256]{1,0:T(8,128)(2,1)S(1)} %get-tuple-element.25), channel_id=1, source_target_pairs={{0,16},{16,0},{32,48},{48,32},{1,17},{17,1},{33,49},{49,33},{2,18}... | collective-permute-start | bytes 294920 | tf_op jit(solution)/shard_map/ppermute | solution.py:255
  147.0 4.5 %collective-permute-start.1 = (bf16[192,256]{1,0:T(8,128)(2,1)S(1)}, bf16[192,256]{1,0:T(8,128)(2,1)S(1)}, u32[]{:S(2)}, u32[]{:S(2)}) collective-permute-start(bf16[192,256]{1,0:T(8,128)(2,1)S(1)} %get-tuple-element.26), channel_id=1, source_target_pairs={{0,32},{16,48},{32,0},{48,16},{1,33},{17,49},{33,1},{49,17},{2,34}... | collective-permute-start | bytes 294920 | tf_op jit(solution)/shard_map/ppermute | solution.py:255
  151.5 2.0 %collective-permute-start.2 = (bf16[192,256]{1,0:T(8,128)(2,1)S(1)}, bf16[192,256]{1,0:T(8,128)(2,1)S(1)}, u32[]{:S(2)}, u32[]{:S(2)}) collective-permute-start(bf16[192,256]{1,0:T(8,128)(2,1)S(1)} %get-tuple-element.27), channel_id=1, source_target_pairs={{0,48},{16,32},{32,16},{48,0},{1,49},{17,33},{33,17},{49,1},{2,50}... | collective-permute-start | bytes 294920 | tf_op jit(solution)/shard_map/ppermute | solution.py:255
  153.5 0.9 collective-permute-done.1.refs_2_
  154.4 3.6 %collective-permute-done.2.refs_3_ = bf16[192,256]{1,0:T(8,128)(2,1)S(1)} collective-permute-done((bf16[192,256]{1,0:T(8,128)(2,1)S(1)}, bf16[192,256]{1,0:T(8,128)(2,1)S(1)}, u32[]{:S(2)}, u32[]{:S(2)}) %collective-permute-start.2) | collective-permute-done | bytes 98336 | tf_op jit(solution)/shard_map/ppermute | solution.py:255
  158.0 0.9 middle.1
  158.9 3.5 %all-to-all-start.9 = ((bf16[16,24,128]{2,1,0:T(8,128)(2,1)}), bf16[16,24,128]{2,1,0:T(8,128)(2,1)S(1)}, u32[]{:S(2)}, u32[]{:S(2)}) async-start(bf16[16,24,128]{2,1,0:T(8,128)(2,1)} %get-tuple-element.28), calls=%async_computation.9 | async-start | bytes 196608 | tf_op jit(solution)/shard_map/all_to_all | solution.py:239
  162.4 15.5 %all_gather.3.protos_ref = bf16[1024,256]{1,0:T(8,128)(2,1)S(1)} all-gather(bf16[128,256]{1,0:T(8,128)(2,1)S(1)} %get-tuple-element.29), channel_id=1, replica_groups=mesh['y'=4,'core'=2,'x'=4,'z'=16] {'y','core'}, dimensions={0}, use_global_device_ids=true | all-gather | bytes 589824 | tf_op jit(solution)/shard_map/all_gather | solution.py:317
  178.0 1.1 last.1
  (30 shorter events, 1.7 us)
Async XLA Ops:
  0.6 38.3 %copy-start = (bf16[1024,256]{1,0:T(8,128)(2,1)S(1)}, bf16[1024,256]{1,0:T(8,128)(2,1)}, u32[]{:S(2)}) copy-start(bf16[1024,256]{1,0:T(8,128)(2,1)} %protos_ref.3) | copy-start | bytes 1572868
  135.8 22.2 %all-to-all-start.8 = ((bf16[8,128,256]{2,1,0:T(8,128)(2,1)}), bf16[8,128,256]{2,1,0:T(8,128)(2,1)S(1)}, u32[]{:S(2)}, u32[]{:S(2)}) async-start(bf16[8,128,256]{2,1,0:T(8,128)(2,1)} %bitcast.4), calls=%async_computation.8 | async-start | bytes 1048576 | tf_op jit(solution)/shard_map/all_to_all | solution.py:239
  143.9 9.6 %collective-permute-start = (bf16[192,256]{1,0:T(8,128)(2,1)S(1)}, bf16[192,256]{1,0:T(8,128)(2,1)S(1)}, u32[]{:S(2)}, u32[]{:S(2)}) collective-permute-start(bf16[192,256]{1,0:T(8,128)(2,1)S(1)} %get-tuple-element.25), channel_id=1, source_target_pairs={{0,16},{16,0},{32,48},{48,32},{1,17},{17,1},{33,49},{49,33},{2,18}... | collective-permute-start | bytes 294920 | tf_op jit(solution)/shard_map/ppermute | solution.py:255
  147.0 7.4 %collective-permute-start.1 = (bf16[192,256]{1,0:T(8,128)(2,1)S(1)}, bf16[192,256]{1,0:T(8,128)(2,1)S(1)}, u32[]{:S(2)}, u32[]{:S(2)}) collective-permute-start(bf16[192,256]{1,0:T(8,128)(2,1)S(1)} %get-tuple-element.26), channel_id=1, source_target_pairs={{0,32},{16,48},{32,0},{48,16},{1,33},{17,49},{33,1},{49,17},{2,34}... | collective-permute-start | bytes 294920 | tf_op jit(solution)/shard_map/ppermute | solution.py:255
  151.5 6.6 %collective-permute-start.2 = (bf16[192,256]{1,0:T(8,128)(2,1)S(1)}, bf16[192,256]{1,0:T(8,128)(2,1)S(1)}, u32[]{:S(2)}, u32[]{:S(2)}) collective-permute-start(bf16[192,256]{1,0:T(8,128)(2,1)S(1)} %get-tuple-element.27), channel_id=1, source_target_pairs={{0,48},{16,32},{32,16},{48,0},{1,49},{17,33},{33,17},{49,1},{2,50}... | collective-permute-start | bytes 294920 | tf_op jit(solution)/shard_map/ppermute | solution.py:255
  158.9 19.1 %all-to-all-start.9 = ((bf16[16,24,128]{2,1,0:T(8,128)(2,1)}), bf16[16,24,128]{2,1,0:T(8,128)(2,1)S(1)}, u32[]{:S(2)}, u32[]{:S(2)}) async-start(bf16[16,24,128]{2,1,0:T(8,128)(2,1)} %get-tuple-element.28), calls=%async_computation.9 | async-start | bytes 196608 | tf_op jit(solution)/shard_map/all_to_all | solution.py:239

commit v5 on v4

--- a/solution.py
+++ b/solution.py
@@ -83,7 +83,7 @@
     return jnp.concatenate(parts, axis=0)
 
 
-def score_body(modes, owned, rows_ref, protos_ref, kernel_ref, units_ref, unit_protos_ref, soft_ref, mass_ref, rows32):
+def score_body(modes, owned, rows_ref, protos_ref, kernel_ref, soft_kernel_ref, units_ref, unit_protos_ref, soft_ref, mass_ref, rows32):
     samples = units_ref.shape[0] // modes
     width = protos_ref.shape[0]
     halves = protos_ref.shape[1] // LANES
@@ -101,6 +101,7 @@
         soft = jnp.exp(scores * 10.0)
         kernel = soft * soft
         kernel_ref[rows, :] = kernel.astype(BF16)
+        soft_kernel_ref[rows, :] = soft.astype(BF16)
         line_to_tiles(mass_ref, m * (width // LANES), jnp.sum(kernel, axis=0, keepdims=True))
         folded = soft[:, :LANES]
         for j in range(1, width // LANES):
@@ -144,30 +145,32 @@
         line_to_tiles(mass_ref, m * (width // LANES), line[0:1] + line[1:2])
 
 
-def unit_body(modes, owned, place_ref, totals_ref, inverse_ref, units_ref, unit_protos_ref, tied_ref, *refs):
-    pieces, (weights, sums) = refs[:-2], refs[-2:]
-    samples = units_ref.shape[0] // modes
-    width = unit_protos_ref.shape[0]
-    tiles = width // LANES
+def upright_factors(totals_ref, width):
+    return [
+        jnp.concatenate([upright(factor)] * (width // LANES), axis=1)
+        for factor in (COEFFICIENT / totals_ref[0:2], 2.0 * COEFFICIENT / totals_ref[2:4])
+    ]
+
+
+def all_but(values, m):
+    return functools.reduce(jnp.add, [values[n] for n in range(len(values)) if n != m])
+
+
+def unit_body(modes, owned, place_ref, totals_ref, inverse_ref, soft_ref, kernel_ref, unit_protos_ref, tied_ref, *refs):
+    pieces, sums = refs[:-1], refs[-1]
+    samples = kernel_ref.shape[0] // modes
+    tiles = kernel_ref.shape[1] // LANES
     chunk = samples // owned // len(pieces)
-    weights[0] = upright(COEFFICIENT / totals_ref[0:2])
-    weights[1] = upright(2.0 * COEFFICIENT / totals_ref[2:4])
-    step = 512
-    for k in range(0, width, step):
-        protos = unit_protos_ref[k : k + step, :]
-        scores = lax.dot_general(units_ref[...], protos, NT, preferred_element_type=F32)
-        codes, predicted = [], []
-        for m in range(modes):
-            rows = slice(m * samples, (m + 1) * samples)
-            soft = jnp.exp(10.0 * scores[rows])
-            inverse = tiles_to_line(inverse_ref[...], m * tiles + k // LANES, step // LANES)
-            codes.append(soft * soft * inverse * jnp.concatenate([weights[0, rows, :]] * (step // LANES), axis=1))
-            predicted.append(soft * jnp.concatenate([weights[1, rows, :]] * (step // LANES), axis=1))
-        for m in range(modes):
-            rows = slice(m * samples, (m + 1) * samples)
-            logit = predicted[m] - functools.reduce(jnp.add, [codes[n] for n in range(modes) if n != m])
-            part = jnp.dot(logit.astype(BF16), protos, preferred_element_type=F32)
-            sums[rows, :] = part if k == 0 else sums[rows, :] + part
+    weight, spread = upright_factors(totals_ref, unit_protos_ref.shape[1])
+    codes, predicted = [], []
+    for m in range(modes):
+        rows = slice(m * samples, (m + 1) * samples)
+        inverse = tiles_to_line(inverse_ref[...], m * tiles, tiles)
+        assigned = (kernel_ref[rows, :].astype(F32) * inverse).astype(BF16)
+        codes.append(weight[rows] * jnp.dot(assigned, unit_protos_ref[...], preferred_element_type=F32))
+        predicted.append(spread[rows] * jnp.dot(soft_ref[rows, :], unit_protos_ref[...], preferred_element_type=F32))
+    for m in range(modes):
+        sums[m * samples : (m + 1) * samples, :] = predicted[m] - all_but(codes, m)
     for step, piece in enumerate(pieces):
         place = lax.bitwise_xor(place_ref[0], jnp.int32(step)) * chunk
         for j in range(modes * owned):
@@ -175,32 +178,23 @@
             piece[j * chunk : (j + 1) * chunk, :] = sums[pl.ds(first, chunk), :].astype(BF16)
 
 
-def proto_body(modes, totals_ref, inverse_ref, units_ref, unit_protos_ref, proto_ref):
+def proto_body(modes, totals_ref, inverse_ref, units_ref, soft_ref, kernel_ref, proto_ref):
     samples = units_ref.shape[0] // modes
-    width = unit_protos_ref.shape[0]
+    width = kernel_ref.shape[1]
     tiles = width // LANES
-    inverse = inverse_ref[...].T
-    weight = COEFFICIENT / totals_ref[0:2]
-    spread = 2.0 * COEFFICIENT / totals_ref[2:4]
-    weight = [mode_of(weight, m, samples // LANES) for m in range(modes)]
-    spread = [mode_of(spread, m, samples // LANES) for m in range(modes)]
+    weight, spread = upright_factors(totals_ref, units_ref.shape[1])
+    units = [units_ref[m * samples : (m + 1) * samples, :].astype(F32) for m in range(modes)]
+    rows = [slice(m * samples, (m + 1) * samples) for m in range(modes)]
+    for_codes = [(weight[rows[m]] * all_but(units, m)).T.astype(BF16) for m in range(modes)]
+    for_predicted = [(spread[rows[m]] * units[m]).T.astype(BF16) for m in range(modes)]
     step = 256
     for k in range(0, width, step):
-        scores = lax.dot_general(unit_protos_ref[k : k + step, :], units_ref[...], NT, preferred_element_type=F32)
-        codes, predicted = [], []
+        total = jnp.zeros((units_ref.shape[1], step), F32)
         for m in range(modes):
-            first = m * tiles + k // LANES
-            upright_inverse = jnp.concatenate([inverse[:, first + j : first + j + 1] for j in range(step // LANES)], axis=0)
-            soft = jnp.exp(10.0 * scores[:, m * samples : (m + 1) * samples])
-            codes.append(soft * soft * upright_inverse * weight[m])
-            predicted.append(soft * spread[m])
-        logit = [
-            (predicted[m] - functools.reduce(jnp.add, [codes[n] for n in range(modes) if n != m])).astype(BF16)
-            for m in range(modes)
-        ]
-        proto_ref[k : k + step, :] = jnp.dot(
-            jnp.concatenate(logit, axis=1), units_ref[...], preferred_element_type=F32
-        ).astype(BF16)
+            inverse = tiles_to_line(inverse_ref[...], m * tiles + k // LANES, step // LANES)
+            total = total + jnp.dot(for_predicted[m], soft_ref[rows[m], k : k + step], preferred_element_type=F32)
+            total = total - inverse * jnp.dot(for_codes[m], kernel_ref[rows[m], k : k + step], preferred_element_type=F32)
+        proto_ref[k : k + step, :] = total.T.astype(BF16)
 
 
 def middle_body(place_ref, parts_ref, protos_ref, *refs):
@@ -280,10 +274,10 @@
     raw_rows = embeddings.transpose(1, 0, 2).reshape(owned, width)
     raw_tiles = jnp.concatenate([raw_rows[:, h : h + LANES] for h in range(0, width, LANES)], axis=0)
     gathered = gather(gather(raw_tiles, "z", nz), "x", nx)
-    kernel, units, unit_protos, soft, mass = call(
+    kernel, soft_kernel, units, unit_protos, soft, mass = call(
         functools.partial(score_body, modes, own_samples),
         "scores",
-        [shape((lines, local_protos), BF16), units_shape, shape((local_protos, width), BF16), row_shape, mass_shape],
+        [shape((lines, local_protos), BF16)] * 2 + [units_shape, shape((local_protos, width), BF16), row_shape, mass_shape],
         [WHOLE] * 2,
         [pltpu.VMEM(gathered.shape, F32)],
     )(gathered, prototypes)
@@ -295,17 +289,17 @@
     totals = sum_over(row, ("x", "z"), nx * nz)
 
     proto_part = call(
-        functools.partial(proto_body, modes), "proto_part", shape((local_protos, width), BF16), [WHOLE] * 4
-    )(totals, inverse, units, unit_protos)
+        functools.partial(proto_body, modes), "proto_part", shape((local_protos, width), BF16), [WHOLE] * 5
+    )(totals, inverse, units, soft_kernel, kernel)
     pieces = call(
         functools.partial(unit_body, modes, own_samples),
         "unit_grad",
         [shape((x_lines, width), BF16)] * nx,
-        [SCALARS] + [WHOLE] * 4 + [ANYWHERE],
-        [pltpu.VMEM((2, lines, LANES), F32), pltpu.VMEM((lines, width), F32)],
-    )(x_place, totals, inverse, units, unit_protos, proto_part)
+        [SCALARS] + [WHOLE] * 5 + [ANYWHERE],
+        [pltpu.VMEM((lines, width), F32)],
+    )(x_place, totals, inverse, soft_kernel, kernel, unit_protos, proto_part)
     proto_part = exchange(proto_part, dp).reshape(groups, local_protos // groups, width)
-    pieces = [swap(piece, "x", nx, step) for step, piece in enumerate(pieces)]
+    pieces = [pieces[0]] + [swap(pieces[step], "x", nx, step) for step in (2, 1, 3)]
     proto_grad, rows = call(
         middle_body,
         "middle",

time: 180 us -> 184 us (1.022)
  local copies, waits for them, and re-layouts: 1.07 us -> 4.93 us
    unnamed x2 -> x12, local copies, waits for them, and re-layouts: 0.01 us -> 3.95 us
where the time goes in v5:
time: 184 us
  blocking collectives  144 us (78%)
  starting transfers between devices  19.8 us (11%)
  Pallas kernels  9.91 us (5%)
  local copies, waits for them, and re-layouts  4.93 us (3%)
  waiting for transfers between devices  4.23 us (2%)
    all_to_all x8, blocking collectives, exchange(): return lax.all_to_all(x, axes, 0, 0, tiled=True)  128 us
    all_gather x1, blocking collectives, per_device(): proto_grad = lax.all_gather(proto_grad, dp, axis=0, tiled=True)  15.5 us
    all_to_all x2, starting transfers between devices, exchange(): return lax.all_to_all(x, axes, 0, 0, tiled=True)  10.5 us
    ppermute x3, starting transfers between devices, swap(): lax.ppermute(x, axis, [(i, i ^ step) for i in range(count)])  9.29 us
    ppermute x3, waiting for transfers between devices, swap(): lax.ppermute(x, axis, [(i, i ^ step) for i in range(count)])  4.22 us
    unnamed x12, local copies, waits for them, and re-layouts  3.95 us
  transfers between devices with their start and end apart: 5, of which 2 were waited for; matrix products, arithmetic and copies ran while one was open for 0% of the time, Pallas kernels for 1%

profile of v5, /device:TPU:1, one launch (start us, length us, event | category | flops | bytes accessed | tf_op | source)
XLA Modules:
  0.0 183.5 jit_solution(17183036668003978002)
XLA Ops:
  1.4 27.5 %all_to_all.54 = bf16[16,24,128]{2,1,0:T(8,128)(2,1)S(1)} all-to-all(bf16[16,24,128]{2,1,0:T(8,128)(2,1)S(1)} %broadcast_in_dim.18), channel_id=1, replica_groups=mesh['y'=4,'core'=2,'x'=4,'z'=16] {'z'}, dimensions={0} | all-to-all | bytes 196608 | tf_op jit(solution)/shard_map/all_to_all | solution.py:233
  29.0 10.0 %all_to_all.55 = bf16[4,384,128]{2,1,0:T(8,128)(2,1)S(1)} all-to-all(bf16[4,384,128]{2,1,0:T(8,128)(2,1)S(1)} %broadcast_in_dim.20), channel_id=1, replica_groups=mesh['y'=4,'core'=2,'x'=4,'z'=16] {'x'}, dimensions={0} | all-to-all | bytes 786432 | tf_op jit(solution)/shard_map/all_to_all | solution.py:233
  39.0 1.5 scores.1
  40.6 13.1 %all_to_all.56 = bf16[8,24,128]{2,1,0:T(8,128)(2,1)S(1)} all-to-all(bf16[8,24,128]{2,1,0:T(8,128)(2,1)S(1)} %broadcast_in_dim.21), channel_id=1, replica_groups=mesh['y'=4,'core'=2,'x'=4,'z'=16] {'y','core'}, dimensions={0} | all-to-all | bytes 98304 | tf_op jit(solution)/shard_map/all_to_all | solution.py:233
  54.4 18.5 %all_to_all.57 = bf16[64,2,384]{2,1,0:T(2,128)(2,1)S(1)} all-to-all(bf16[64,2,384]{2,1,0:T(2,128)(2,1)S(1)} %broadcast_in_dim.22), channel_id=1, replica_groups=mesh['y'=4,'core'=2,'x'=4,'z'=16] {'x','z'}, dimensions={0} | all-to-all | bytes 196608 | tf_op jit(solution)/shard_map/all_to_all | solution.py:233
  73.2 9.9 %all_to_all.58 = bf16[8,24,128]{2,1,0:T(8,128)(2,1)S(1)} all-to-all(bf16[8,24,128]{2,1,0:T(8,128)(2,1)S(1)} %broadcast_in_dim.23), channel_id=1, replica_groups=mesh['y'=4,'core'=2,'x'=4,'z'=16] {'y','core'}, dimensions={0} | all-to-all | bytes 98304 | tf_op jit(solution)/shard_map/all_to_all | solution.py:233
  83.7 18.3 %all_to_all.59 = bf16[64,2,384]{2,1,0:T(2,128)(2,1)S(1)} all-to-all(bf16[64,2,384]{2,1,0:T(2,128)(2,1)S(1)} %broadcast_in_dim.24), channel_id=1, replica_groups=mesh['y'=4,'core'=2,'x'=4,'z'=16] {'x','z'}, dimensions={0} | all-to-all | bytes 196608 | tf_op jit(solution)/shard_map/all_to_all | solution.py:233
  102.4 9.9 %all_to_all.60 = bf16[8,24,128]{2,1,0:T(8,128)(2,1)S(1)} all-to-all(bf16[8,24,128]{2,1,0:T(8,128)(2,1)S(1)} %broadcast_in_dim.25), channel_id=1, replica_groups=mesh['y'=4,'core'=2,'x'=4,'z'=16] {'y','core'}, dimensions={0} | all-to-all | bytes 98304 | tf_op jit(solution)/shard_map/all_to_all | solution.py:233
  112.9 20.8 %all_to_all.61 = bf16[64,4,384]{2,1,0:T(4,128)(2,1)S(1)} all-to-all(bf16[64,4,384]{2,1,0:T(4,128)(2,1)S(1)} %broadcast_in_dim.26), channel_id=1, replica_groups=mesh['y'=4,'core'=2,'x'=4,'z'=16] {'x','z'}, dimensions={0} | all-to-all | bytes 393216 | tf_op jit(solution)/shard_map/all_to_all | solution.py:233
  133.7 1.6 proto_part.1.tied_ref
  136.0 7.0 %all-to-all-start.8 = ((bf16[8,128,256]{2,1,0:T(8,128)(2,1)}), bf16[8,128,256]{2,1,0:T(8,128)(2,1)}, u32[]{:S(2)}, u32[]{:S(2)}) async-start(bf16[8,128,256]{2,1,0:T(8,128)(2,1)} %bitcast.7), calls=%async_computation.8 | async-start | bytes 1048576 | tf_op jit(solution)/shard_map/all_to_all | solution.py:233
  143.0 1.1 copy-done.1
  144.1 1.0 copy-done.5
  145.2 1.7 unit_grad.1
  146.9 4.7 %collective-permute-start = (bf16[192,256]{1,0:T(8,128)(2,1)}, bf16[192,256]{1,0:T(8,128)(2,1)S(1)}, u32[]{:S(2)}, u32[]{:S(2)}) collective-permute-start(bf16[192,256]{1,0:T(8,128)(2,1)} %get-tuple-element.27), channel_id=1, source_target_pairs={{0,32},{16,48},{32,0},{48,16},{1,33},{17,49},{33,1},{49,17},{2,34}... | collective-permute-start | bytes 294920 | tf_op jit(solution)/shard_map/ppermute | solution.py:249
  151.5 2.3 %collective-permute-start.1 = (bf16[192,256]{1,0:T(8,128)(2,1)S(1)}, bf16[192,256]{1,0:T(8,128)(2,1)S(1)}, u32[]{:S(2)}, u32[]{:S(2)}) collective-permute-start(bf16[192,256]{1,0:T(8,128)(2,1)S(1)} %get-tuple-element.28), channel_id=1, source_target_pairs={{0,16},{16,0},{32,48},{48,32},{1,17},{17,1},{33,49},{49,33},{2,18}... | collective-permute-start | bytes 294920 | tf_op jit(solution)/shard_map/ppermute | solution.py:249
  153.8 2.3 %collective-permute-start.2 = (bf16[192,256]{1,0:T(8,128)(2,1)S(1)}, bf16[192,256]{1,0:T(8,128)(2,1)S(1)}, u32[]{:S(2)}, u32[]{:S(2)}) collective-permute-start(bf16[192,256]{1,0:T(8,128)(2,1)S(1)} %get-tuple-element.29), channel_id=1, source_target_pairs={{0,48},{16,32},{32,16},{48,0},{1,49},{17,33},{33,17},{49,1},{2,50}... | collective-permute-start | bytes 294920 | tf_op jit(solution)/shard_map/ppermute | solution.py:249
  156.2 1.2 collective-permute-done.1.refs_2_
  157.4 3.1 %collective-permute-done.2.refs_3_ = bf16[192,256]{1,0:T(8,128)(2,1)S(1)} collective-permute-done((bf16[192,256]{1,0:T(8,128)(2,1)S(1)}, bf16[192,256]{1,0:T(8,128)(2,1)S(1)}, u32[]{:S(2)}, u32[]{:S(2)}) %collective-permute-start.2) | collective-permute-done | bytes 98336 | tf_op jit(solution)/shard_map/ppermute | solution.py:249
  160.4 1.0 copy-done.3
  161.5 1.9 %middle.1 = (bf16[128,256]{1,0:T(8,128)(2,1)S(1)}, bf16[16,24,128]{2,1,0:T(8,128)(2,1)}) custom-call(s32[1]{0:T(128)} %bitcast.place_ref, bf16[8,128,256]{2,1,0:T(8,128)(2,1)} %all-to-all-done.8.parts_ref, bf16[1024,256]{1,0:T(8,128)(2,1)S(1)} %copy-done.3, bf16[192,256]{1,0:T(8,128)(2,1)S(1)} %get-tuple-element.26.refs_0_, ...), custom_call_target="tpu_custom_call" | custom-call | tf_op jit(solution)/shard_map/middle/pallas_call | solution.py:303
  163.4 3.5 %all-to-all-start.9 = ((bf16[16,24,128]{2,1,0:T(8,128)(2,1)}), bf16[16,24,128]{2,1,0:T(8,128)(2,1)S(1)}, u32[]{:S(2)}, u32[]{:S(2)}) async-start(bf16[16,24,128]{2,1,0:T(8,128)(2,1)} %get-tuple-element.30), calls=%async_computation.9 | async-start | bytes 196608 | tf_op jit(solution)/shard_map/all_to_all | solution.py:233
  166.9 15.5 %all_gather.3.protos_ref = bf16[1024,256]{1,0:T(8,128)(2,1)S(1)} all-gather(bf16[128,256]{1,0:T(8,128)(2,1)S(1)} %get-tuple-element.31), channel_id=1, replica_groups=mesh['y'=4,'core'=2,'x'=4,'z'=16] {'y','core'}, dimensions={0}, use_global_device_ids=true | all-gather | bytes 589824 | tf_op jit(solution)/shard_map/all_gather | solution.py:311
  182.4 1.1 last.1
  (40 shorter events, 4.1 us)
Async XLA Ops:
  1.3 37.7 %copy-start.2 = (bf16[1024,256]{1,0:T(8,128)(2,1)S(1)}, bf16[1024,256]{1,0:T(8,128)(2,1)}, u32[]{:S(2)}) copy-start(bf16[1024,256]{1,0:T(8,128)(2,1)} %protos_ref.3) | copy-start | bytes 1572868
  40.5 32.6 %copy-start.4 = (bf16[1024,256]{1,0:T(8,128)(2,1)}, bf16[1024,256]{1,0:T(8,128)(2,1)S(1)}, u32[]{:S(2)}) copy-start(bf16[1024,256]{1,0:T(8,128)(2,1)S(1)} %get-tuple-element.25.unit_protos_ref) | copy-start | bytes 1572868
  135.2 0.8 copy-start
  136.0 24.4 %all-to-all-start.8 = ((bf16[8,128,256]{2,1,0:T(8,128)(2,1)}), bf16[8,128,256]{2,1,0:T(8,128)(2,1)}, u32[]{:S(2)}, u32[]{:S(2)}) async-start(bf16[8,128,256]{2,1,0:T(8,128)(2,1)} %bitcast.7), calls=%async_computation.8 | async-start | bytes 1048576 | tf_op jit(solution)/shard_map/all_to_all | solution.py:233
  143.0 1.1 copy-start.1
  144.1 1.0 copy-start.5
  146.9 9.3 %collective-permute-start = (bf16[192,256]{1,0:T(8,128)(2,1)}, bf16[192,256]{1,0:T(8,128)(2,1)S(1)}, u32[]{:S(2)}, u32[]{:S(2)}) collective-permute-start(bf16[192,256]{1,0:T(8,128)(2,1)} %get-tuple-element.27), channel_id=1, source_target_pairs={{0,32},{16,48},{32,0},{48,16},{1,33},{17,49},{33,1},{49,17},{2,34}... | collective-permute-start | bytes 294920 | tf_op jit(solution)/shard_map/ppermute | solution.py:249
  151.5 5.8 %collective-permute-start.1 = (bf16[192,256]{1,0:T(8,128)(2,1)S(1)}, bf16[192,256]{1,0:T(8,128)(2,1)S(1)}, u32[]{:S(2)}, u32[]{:S(2)}) collective-permute-start(bf16[192,256]{1,0:T(8,128)(2,1)S(1)} %get-tuple-element.28), channel_id=1, source_target_pairs={{0,16},{16,0},{32,48},{48,32},{1,17},{17,1},{33,49},{49,33},{2,18}... | collective-permute-start | bytes 294920 | tf_op jit(solution)/shard_map/ppermute | solution.py:249
  153.8 6.6 %collective-permute-start.2 = (bf16[192,256]{1,0:T(8,128)(2,1)S(1)}, bf16[192,256]{1,0:T(8,128)(2,1)S(1)}, u32[]{:S(2)}, u32[]{:S(2)}) collective-permute-start(bf16[192,256]{1,0:T(8,128)(2,1)S(1)} %get-tuple-element.29), channel_id=1, source_target_pairs={{0,48},{16,32},{32,16},{48,0},{1,49},{17,33},{33,17},{49,1},{2,50}... | collective-permute-start | bytes 294920 | tf_op jit(solution)/shard_map/ppermute | solution.py:249
  160.4 1.0 copy-start.3
  163.4 19.1 %all-to-all-start.9 = ((bf16[16,24,128]{2,1,0:T(8,128)(2,1)}), bf16[16,24,128]{2,1,0:T(8,128)(2,1)S(1)}, u32[]{:S(2)}, u32[]{:S(2)}) async-start(bf16[16,24,128]{2,1,0:T(8,128)(2,1)} %get-tuple-element.30), calls=%async_computation.9 | async-start | bytes 196608 | tf_op jit(solution)/shard_map/all_to_all | solution.py:233

commit v6 on v5

--- a/solution.py
+++ b/solution.py
@@ -83,10 +83,15 @@
     return jnp.concatenate(parts, axis=0)
 
 
-def score_body(modes, owned, rows_ref, protos_ref, kernel_ref, soft_kernel_ref, units_ref, unit_protos_ref, soft_ref, mass_ref, rows32):
+def score_body(
+    modes, owned, place_ref, rows_ref, protos_ref,
+    kernel_ref, soft_kernel_ref, units_ref, unit_protos_ref, soft_ref, mass_ref, share_ref, rows32,
+):
     samples = units_ref.shape[0] // modes
     width = protos_ref.shape[0]
     halves = protos_ref.shape[1] // LANES
+    share = share_ref.shape[0]
+    share_ref[...] = protos_ref[pl.ds(pl.multiple_of(place_ref[0] * share, share), share), :]
     raw = protos_ref[...].astype(F32)
     scale = lax.rsqrt(jnp.sum(raw * raw, axis=-1, keepdims=True) + 1e-6)
     unit_protos_ref[...] = (raw * scale).astype(BF16)
@@ -178,7 +183,8 @@
             piece[j * chunk : (j + 1) * chunk, :] = sums[pl.ds(first, chunk), :].astype(BF16)
 
 
-def proto_body(modes, totals_ref, inverse_ref, units_ref, soft_ref, kernel_ref, proto_ref):
+def proto_body(modes, totals_ref, inverse_ref, units_ref, soft_ref, kernel_ref, unit_protos_ref, proto_ref, mark_ref):
+    mark_ref[...] = jnp.zeros_like(mark_ref)
     samples = units_ref.shape[0] // modes
     width = kernel_ref.shape[1]
     tiles = width // LANES
@@ -197,11 +203,10 @@
         proto_ref[k : k + step, :] = total.T.astype(BF16)
 
 
-def middle_body(place_ref, parts_ref, protos_ref, *refs):
+def middle_body(parts_ref, share_ref, *refs):
     pieces, (grad_ref, rows_ref, unit) = refs[:-3], refs[-3:]
     total = jnp.sum(parts_ref[...].astype(F32), axis=0)
-    share = total.shape[0]
-    raw = protos_ref[pl.ds(pl.multiple_of(place_ref[0] * share, share), share), :].astype(F32)
+    raw = share_ref[...].astype(F32)
     scale = lax.rsqrt(jnp.sum(raw * raw, axis=-1, keepdims=True) + 1e-6)
     inner = jnp.sum(total * raw, axis=-1, keepdims=True)
     grad_ref[...] = (scale * total - scale * scale * scale * inner * raw).astype(BF16)
@@ -274,13 +279,14 @@
     raw_rows = embeddings.transpose(1, 0, 2).reshape(owned, width)
     raw_tiles = jnp.concatenate([raw_rows[:, h : h + LANES] for h in range(0, width, LANES)], axis=0)
     gathered = gather(gather(raw_tiles, "z", nz), "x", nx)
-    kernel, soft_kernel, units, unit_protos, soft, mass = call(
+    kernel, soft_kernel, units, unit_protos, soft, mass, own_share = call(
         functools.partial(score_body, modes, own_samples),
         "scores",
-        [shape((lines, local_protos), BF16)] * 2 + [units_shape, shape((local_protos, width), BF16), row_shape, mass_shape],
-        [WHOLE] * 2,
+        [shape((lines, local_protos), BF16)] * 2
+        + [units_shape, shape((local_protos, width), BF16), row_shape, mass_shape, shape((local_protos // groups, width), BF16)],
+        [SCALARS] + [WHOLE] * 2,
         [pltpu.VMEM(gathered.shape, F32)],
-    )(gathered, prototypes)
+    )(dp_place, gathered, prototypes)
 
     for _ in range(2):
         row = row_call(sum_over(mass, dp, groups), kernel)
@@ -288,25 +294,28 @@
     row, inverse = last_row_call(sum_over(mass, dp, groups), kernel, soft)
     totals = sum_over(row, ("x", "z"), nx * nz)
 
-    proto_part = call(
-        functools.partial(proto_body, modes), "proto_part", shape((local_protos, width), BF16), [WHOLE] * 5
-    )(totals, inverse, units, soft_kernel, kernel)
+    proto_part, mark = call(
+        functools.partial(proto_body, modes),
+        "proto_part",
+        [shape((local_protos, width), BF16), shape((8, LANES), F32)],
+        [WHOLE] * 6,
+    )(totals, inverse, units, soft_kernel, kernel, unit_protos)
     pieces = call(
         functools.partial(unit_body, modes, own_samples),
         "unit_grad",
         [shape((x_lines, width), BF16)] * nx,
-        [SCALARS] + [WHOLE] * 5 + [ANYWHERE],
+        [SCALARS] + [WHOLE] * 6,
         [pltpu.VMEM((lines, width), F32)],
-    )(x_place, totals, inverse, soft_kernel, kernel, unit_protos, proto_part)
+    )(x_place, totals, inverse, soft_kernel, kernel, unit_protos, mark)
     proto_part = exchange(proto_part, dp).reshape(groups, local_protos // groups, width)
     pieces = [pieces[0]] + [swap(pieces[step], "x", nx, step) for step in (2, 1, 3)]
     proto_grad, rows = call(
         middle_body,
         "middle",
         [shape((local_protos // groups, width), BF16), shape((nz, owned * width // LANES, LANES), BF16)],
-        [SCALARS] + [WHOLE] * (2 + nx),
+        [WHOLE] * (2 + nx),
         [pltpu.VMEM((width // LANES, x_lines, LANES), F32)],
-    )(dp_place, proto_part, prototypes, *pieces)
+    )(proto_part, own_share, *pieces)
     rows = exchange(rows, "z")
     proto_grad = lax.all_gather(proto_grad, dp, axis=0, tiled=True)
     embed_grad, proto_grad = call(

time: 184 us -> 184 us (level)
  blocking collectives: 144 us -> 133 us
  waiting for transfers between devices: 4.23 us -> 10.5 us
  starting transfers between devices: 19.8 us -> 23.8 us
    all_to_all x8 -> x7, blocking collectives: 128 us -> 118 us  [exchange(): return lax.all_to_all(x, axes, 0, 0, tiled=True)]
    all_to_all x2 -> x3, waiting for transfers between devices: 0.01 us -> 6.24 us  [exchange(): return lax.all_to_all(x, axes, 0, 0, tiled=True)]
    all_to_all x2 -> x3, starting transfers between devices: 10.5 us -> 14.5 us  [exchange(): return lax.all_to_all(x, axes, 0, 0, tiled=True)]
  transfers between devices with their start and end apart: 5 -> 6, of which waited for: 2 -> 3; matrix products, arithmetic and copies ran while one was open for 0% -> 0% of each run, Pallas kernels for 1% -> 1%
where the time goes in v6:
time: 184 us; the launch traced here: 183 us
  blocking collectives  133 us (72%)
  starting transfers between devices  23.8 us (13%)
  waiting for transfers between devices  10.5 us (6%)
  Pallas kernels  9.31 us (5%)
  local copies, waits for them, and re-layouts  4.6 us (2%)
    all_to_all x7, blocking collectives, exchange(): return lax.all_to_all(x, axes, 0, 0, tiled=True)  118 us
    all_gather x1, blocking collectives, per_device(): proto_grad = lax.all_gather(proto_grad, dp, axis=0, tiled=True)  15.5 us
    all_to_all x3, starting transfers between devices, exchange(): return lax.all_to_all(x, axes, 0, 0, tiled=True)  14.5 us
    ppermute x3, starting transfers between devices, swap(): lax.ppermute(x, axis, [(i, i ^ step) for i in range(count)])  9.31 us
    all_to_all x3, waiting for transfers between devices, exchange(): return lax.all_to_all(x, axes, 0, 0, tiled=True)  6.24 us
    ppermute x3, waiting for transfers between devices, swap(): lax.ppermute(x, axis, [(i, i ^ step) for i in range(count)])  4.24 us
  transfers between devices with their start and end apart: 6, of which 3 were waited for; matrix products, arithmetic and copies ran while one was open for 0% of the time, Pallas kernels for 1%

profile of v6, /device:TPU:1, one launch (start us, length us, event | category | flops | bytes accessed | tf_op | source)
XLA Modules:
  0.0 182.7 jit_solution(8382475069078982871)
XLA Ops:
  1.4 27.4 %all_to_all.54 = bf16[16,24,128]{2,1,0:T(8,128)(2,1)S(1)} all-to-all(bf16[16,24,128]{2,1,0:T(8,128)(2,1)S(1)} %broadcast_in_dim.18), channel_id=1, replica_groups=mesh['y'=4,'core'=2,'x'=4,'z'=16] {'z'}, dimensions={0} | all-to-all | bytes 196608 | tf_op jit(solution)/shard_map/all_to_all | solution.py:238
  29.6 4.0 %all-to-all-start.1 = ((bf16[4,384,128]{2,1,0:T(8,128)(2,1)}), bf16[4,384,128]{2,1,0:T(8,128)(2,1)S(1)}, u32[]{:S(2)}, u32[]{:S(2)}) async-start(bf16[4,384,128]{2,1,0:T(8,128)(2,1)} %broadcast_in_dim.20), calls=%async_computation.1 | async-start | bytes 786432 | tf_op jit(solution)/shard_map/all_to_all | solution.py:238
  33.6 6.2 %all-to-all-done.1 = bf16[4,384,128]{2,1,0:T(8,128)(2,1)S(1)} async-done(((bf16[4,384,128]{2,1,0:T(8,128)(2,1)}), bf16[4,384,128]{2,1,0:T(8,128)(2,1)S(1)}, u32[]{:S(2)}, u32[]{:S(2)}) %all-to-all-start.1) | async-done | bytes 393248 | tf_op jit(solution)/shard_map/all_to_all | solution.py:238
  39.8 1.0 copy-done.2
  40.9 1.5 scores.1
  42.5 13.1 %all_to_all.55 = bf16[8,24,128]{2,1,0:T(8,128)(2,1)S(1)} all-to-all(bf16[8,24,128]{2,1,0:T(8,128)(2,1)S(1)} %broadcast_in_dim.21), channel_id=1, replica_groups=mesh['y'=4,'core'=2,'x'=4,'z'=16] {'y','core'}, dimensions={0} | all-to-all | bytes 98304 | tf_op jit(solution)/shard_map/all_to_all | solution.py:238
  56.2 18.5 %all_to_all.56 = bf16[64,2,384]{2,1,0:T(2,128)(2,1)S(1)} all-to-all(bf16[64,2,384]{2,1,0:T(2,128)(2,1)S(1)} %broadcast_in_dim.22), channel_id=1, replica_groups=mesh['y'=4,'core'=2,'x'=4,'z'=16] {'x','z'}, dimensions={0} | all-to-all | bytes 196608 | tf_op jit(solution)/shard_map/all_to_all | solution.py:238
  75.1 9.9 %all_to_all.57 = bf16[8,24,128]{2,1,0:T(8,128)(2,1)S(1)} all-to-all(bf16[8,24,128]{2,1,0:T(8,128)(2,1)S(1)} %broadcast_in_dim.23), channel_id=1, replica_groups=mesh['y'=4,'core'=2,'x'=4,'z'=16] {'y','core'}, dimensions={0} | all-to-all | bytes 98304 | tf_op jit(solution)/shard_map/all_to_all | solution.py:238
  85.6 18.3 %all_to_all.58 = bf16[64,2,384]{2,1,0:T(2,128)(2,1)S(1)} all-to-all(bf16[64,2,384]{2,1,0:T(2,128)(2,1)S(1)} %broadcast_in_dim.24), channel_id=1, replica_groups=mesh['y'=4,'core'=2,'x'=4,'z'=16] {'x','z'}, dimensions={0} | all-to-all | bytes 196608 | tf_op jit(solution)/shard_map/all_to_all | solution.py:238
  104.3 9.9 %all_to_all.59 = bf16[8,24,128]{2,1,0:T(8,128)(2,1)S(1)} all-to-all(bf16[8,24,128]{2,1,0:T(8,128)(2,1)S(1)} %broadcast_in_dim.25), channel_id=1, replica_groups=mesh['y'=4,'core'=2,'x'=4,'z'=16] {'y','core'}, dimensions={0} | all-to-all | bytes 98304 | tf_op jit(solution)/shard_map/all_to_all | solution.py:238
  114.8 20.8 %all_to_all.60 = bf16[64,4,384]{2,1,0:T(4,128)(2,1)S(1)} all-to-all(bf16[64,4,384]{2,1,0:T(4,128)(2,1)S(1)} %broadcast_in_dim.26), channel_id=1, replica_groups=mesh['y'=4,'core'=2,'x'=4,'z'=16] {'x','z'}, dimensions={0} | all-to-all | bytes 393216 | tf_op jit(solution)/shard_map/all_to_all | solution.py:238
  135.6 1.6 proto_part.1
  137.9 7.0 %all-to-all-start.8 = ((bf16[8,128,256]{2,1,0:T(8,128)(2,1)}), bf16[8,128,256]{2,1,0:T(8,128)(2,1)}, u32[]{:S(2)}, u32[]{:S(2)}) async-start(bf16[8,128,256]{2,1,0:T(8,128)(2,1)} %bitcast.8), calls=%async_computation.8 | async-start | bytes 1048576 | tf_op jit(solution)/shard_map/all_to_all | solution.py:238
  145.0 1.0 copy-done.1
  146.0 1.1 unit_grad.1
  147.1 4.7 %collective-permute-start = (bf16[192,256]{1,0:T(8,128)(2,1)S(1)}, bf16[192,256]{1,0:T(8,128)(2,1)S(1)}, u32[]{:S(2)}, u32[]{:S(2)}) collective-permute-start(bf16[192,256]{1,0:T(8,128)(2,1)S(1)} %get-tuple-element.33), channel_id=1, source_target_pairs={{0,32},{16,48},{32,0},{48,16},{1,33},{17,49},{33,1},{49,17},{2,34}... | collective-permute-start | bytes 294920 | tf_op jit(solution)/shard_map/ppermute | solution.py:254
  151.8 2.3 %collective-permute-start.1 = (bf16[192,256]{1,0:T(8,128)(2,1)S(1)}, bf16[192,256]{1,0:T(8,128)(2,1)S(1)}, u32[]{:S(2)}, u32[]{:S(2)}) collective-permute-start(bf16[192,256]{1,0:T(8,128)(2,1)S(1)} %get-tuple-element.34), channel_id=1, source_target_pairs={{0,16},{16,0},{32,48},{48,32},{1,17},{17,1},{33,49},{49,33},{2,18}... | collective-permute-start | bytes 294920 | tf_op jit(solution)/shard_map/ppermute | solution.py:254
  154.1 2.3 %collective-permute-start.2 = (bf16[192,256]{1,0:T(8,128)(2,1)S(1)}, bf16[192,256]{1,0:T(8,128)(2,1)S(1)}, u32[]{:S(2)}, u32[]{:S(2)}) collective-permute-start(bf16[192,256]{1,0:T(8,128)(2,1)S(1)} %get-tuple-element.35), channel_id=1, source_target_pairs={{0,48},{16,32},{32,16},{48,0},{1,49},{17,33},{33,17},{49,1},{2,50}... | collective-permute-start | bytes 294920 | tf_op jit(solution)/shard_map/ppermute | solution.py:254
  156.4 1.2 collective-permute-done.1.refs_2_
  157.6 3.0 %collective-permute-done.2.refs_3_ = bf16[192,256]{1,0:T(8,128)(2,1)S(1)} collective-permute-done((bf16[192,256]{1,0:T(8,128)(2,1)S(1)}, bf16[192,256]{1,0:T(8,128)(2,1)S(1)}, u32[]{:S(2)}, u32[]{:S(2)}) %collective-permute-start.2) | collective-permute-done | bytes 98336 | tf_op jit(solution)/shard_map/ppermute | solution.py:254
  160.7 1.9 %middle.1 = (bf16[128,256]{1,0:T(8,128)(2,1)S(1)}, bf16[16,24,128]{2,1,0:T(8,128)(2,1)}) custom-call(bf16[8,128,256]{2,1,0:T(8,128)(2,1)} %all-to-all-done.8.parts_ref, bf16[128,256]{1,0:T(8,128)(2,1)S(1)} %copy-done.5, bf16[192,256]{1,0:T(8,128)(2,1)S(1)} %get-tuple-element.32.refs_0_, bf16[192,256]{1,0:T(8,128)(2,1)S(1)} %collective-permute-done.refs_1_, ...), custom_call_target="tpu_custom_call" | custom-call | tf_op jit(solution)/shard_map/middle/pallas_call | solution.py:312
  162.6 3.5 %all-to-all-start.9 = ((bf16[16,24,128]{2,1,0:T(8,128)(2,1)}), bf16[16,24,128]{2,1,0:T(8,128)(2,1)S(1)}, u32[]{:S(2)}, u32[]{:S(2)}) async-start(bf16[16,24,128]{2,1,0:T(8,128)(2,1)} %get-tuple-element.36), calls=%async_computation.9 | async-start | bytes 196608 | tf_op jit(solution)/shard_map/all_to_all | solution.py:238
  166.1 15.5 %all_gather.3.protos_ref = bf16[1024,256]{1,0:T(8,128)(2,1)S(1)} all-gather(bf16[128,256]{1,0:T(8,128)(2,1)S(1)} %get-tuple-element.37), channel_id=1, replica_groups=mesh['y'=4,'core'=2,'x'=4,'z'=16] {'y','core'}, dimensions={0}, use_global_device_ids=true | all-gather | bytes 589824 | tf_op jit(solution)/shard_map/all_gather | solution.py:320
  181.7 1.1 last.1
  (41 shorter events, 4.9 us)
Async XLA Ops:
  29.6 10.2 %all-to-all-start.1 = ((bf16[4,384,128]{2,1,0:T(8,128)(2,1)}), bf16[4,384,128]{2,1,0:T(8,128)(2,1)S(1)}, u32[]{:S(2)}, u32[]{:S(2)}) async-start(bf16[4,384,128]{2,1,0:T(8,128)(2,1)} %broadcast_in_dim.20), calls=%async_computation.1 | async-start | bytes 786432 | tf_op jit(solution)/shard_map/all_to_all | solution.py:238
  39.8 1.0 copy-start.2
  42.4 32.7 %copy-start.4 = (bf16[128,256]{1,0:T(8,128)(2,1)}, bf16[128,256]{1,0:T(8,128)(2,1)S(1)}, u32[]{:S(2)}) copy-start(bf16[128,256]{1,0:T(8,128)(2,1)S(1)} %get-tuple-element.30.share_ref) | copy-start | bytes 196612
  42.4 93.2 %copy-start = (bf16[1024,256]{1,0:T(8,128)(2,1)}, bf16[1024,256]{1,0:T(8,128)(2,1)S(1)}, u32[]{:S(2)}) copy-start(bf16[1024,256]{1,0:T(8,128)(2,1)S(1)} %get-tuple-element.28.unit_protos_ref) | copy-start | bytes 1572868
  137.1 0.8 copy-start.3
  137.9 22.7 %all-to-all-start.8 = ((bf16[8,128,256]{2,1,0:T(8,128)(2,1)}), bf16[8,128,256]{2,1,0:T(8,128)(2,1)}, u32[]{:S(2)}, u32[]{:S(2)}) async-start(bf16[8,128,256]{2,1,0:T(8,128)(2,1)} %bitcast.8), calls=%async_computation.8 | async-start | bytes 1048576 | tf_op jit(solution)/shard_map/all_to_all | solution.py:238
  145.0 1.0 copy-start.1
  146.0 14.7 %copy-start.5 = (bf16[128,256]{1,0:T(8,128)(2,1)S(1)}, bf16[128,256]{1,0:T(8,128)(2,1)}, u32[]{:S(2)}) copy-start(bf16[128,256]{1,0:T(8,128)(2,1)} %copy-done.4) | copy-start | bytes 196612
  147.1 9.3 %collective-permute-start = (bf16[192,256]{1,0:T(8,128)(2,1)S(1)}, bf16[192,256]{1,0:T(8,128)(2,1)S(1)}, u32[]{:S(2)}, u32[]{:S(2)}) collective-permute-start(bf16[192,256]{1,0:T(8,128)(2,1)S(1)} %get-tuple-element.33), channel_id=1, source_target_pairs={{0,32},{16,48},{32,0},{48,16},{1,33},{17,49},{33,1},{49,17},{2,34}... | collective-permute-start | bytes 294920 | tf_op jit(solution)/shard_map/ppermute | solution.py:254
  151.8 5.8 %collective-permute-start.1 = (bf16[192,256]{1,0:T(8,128)(2,1)S(1)}, bf16[192,256]{1,0:T(8,128)(2,1)S(1)}, u32[]{:S(2)}, u32[]{:S(2)}) collective-permute-start(bf16[192,256]{1,0:T(8,128)(2,1)S(1)} %get-tuple-element.34), channel_id=1, source_target_pairs={{0,16},{16,0},{32,48},{48,32},{1,17},{17,1},{33,49},{49,33},{2,18}... | collective-permute-start | bytes 294920 | tf_op jit(solution)/shard_map/ppermute | solution.py:254
  154.1 6.6 %collective-permute-start.2 = (bf16[192,256]{1,0:T(8,128)(2,1)S(1)}, bf16[192,256]{1,0:T(8,128)(2,1)S(1)}, u32[]{:S(2)}, u32[]{:S(2)}) collective-permute-start(bf16[192,256]{1,0:T(8,128)(2,1)S(1)} %get-tuple-element.35), channel_id=1, source_target_pairs={{0,48},{16,32},{32,16},{48,0},{1,49},{17,33},{33,17},{49,1},{2,50}... | collective-permute-start | bytes 294920 | tf_op jit(solution)/shard_map/ppermute | solution.py:254
  162.6 19.0 %all-to-all-start.9 = ((bf16[16,24,128]{2,1,0:T(8,128)(2,1)}), bf16[16,24,128]{2,1,0:T(8,128)(2,1)S(1)}, u32[]{:S(2)}, u32[]{:S(2)}) async-start(bf16[16,24,128]{2,1,0:T(8,128)(2,1)} %get-tuple-element.36), calls=%async_computation.9 | async-start | bytes 196608 | tf_op jit(solution)/shard_map/all_to_all | solution.py:238

commit v7 on v4

--- a/solution.py
+++ b/solution.py
@@ -11,6 +11,7 @@
 BF16 = jnp.bfloat16
 LANES = 128
 COEFFICIENT = 64.0 * 10.0 / 6.0
+LOG2_E = 1.4426950408889634
 NT = (((1,), (1,)), ((), ()))
 SCALARS = pl.BlockSpec(memory_space=pltpu.SMEM)
 WHOLE = pl.BlockSpec(memory_space=pltpu.VMEM)
@@ -98,7 +99,7 @@
         units = (raw * lax.rsqrt(jnp.sum(raw * raw, axis=-1, keepdims=True) + 1e-6)).astype(BF16)
         units_ref[rows, :] = units
         scores = lax.dot_general(units, unit_protos_ref[...], NT, preferred_element_type=F32)
-        soft = jnp.exp(scores * 10.0)
+        soft = jnp.exp2(scores * (10.0 * LOG2_E))
         kernel = soft * soft
         kernel_ref[rows, :] = kernel.astype(BF16)
         line_to_tiles(mass_ref, m * (width // LANES), jnp.sum(kernel, axis=0, keepdims=True))
@@ -159,7 +160,7 @@
         codes, predicted = [], []
         for m in range(modes):
             rows = slice(m * samples, (m + 1) * samples)
-            soft = jnp.exp(10.0 * scores[rows])
+            soft = jnp.exp2((10.0 * LOG2_E) * scores[rows])
             inverse = tiles_to_line(inverse_ref[...], m * tiles + k // LANES, step // LANES)
             codes.append(soft * soft * inverse * jnp.concatenate([weights[0, rows, :]] * (step // LANES), axis=1))
             predicted.append(soft * jnp.concatenate([weights[1, rows, :]] * (step // LANES), axis=1))
@@ -191,7 +192,7 @@
         for m in range(modes):
             first = m * tiles + k // LANES
             upright_inverse = jnp.concatenate([inverse[:, first + j : first + j + 1] for j in range(step // LANES)], axis=0)
-            soft = jnp.exp(10.0 * scores[:, m * samples : (m + 1) * samples])
+            soft = jnp.exp2((10.0 * LOG2_E) * scores[:, m * samples : (m + 1) * samples])
             codes.append(soft * soft * upright_inverse * weight[m])
             predicted.append(soft * spread[m])
         logit = [
@@ -305,7 +306,7 @@
         [pltpu.VMEM((2, lines, LANES), F32), pltpu.VMEM((lines, width), F32)],
     )(x_place, totals, inverse, units, unit_protos, proto_part)
     proto_part = exchange(proto_part, dp).reshape(groups, local_protos // groups, width)
-    pieces = [swap(piece, "x", nx, step) for step, piece in enumerate(pieces)]
+    pieces = [pieces[0]] + [swap(pieces[step], "x", nx, step) for step in (2, 1, 3)]
     proto_grad, rows = call(
         middle_body,
         "middle",

time: 180 us -> 179 us (level)
  no operation moved by 1% of the time
where the time goes in v7:
time: 179 us; the launch traced here: 178 us
  blocking collectives  143 us (80%)
  starting transfers between devices  19.2 us (11%)
  Pallas kernels  9.31 us (5%)
  waiting for transfers between devices  4.26 us (2%)
    all_to_all x8, blocking collectives, exchange(): return lax.all_to_all(x, axes, 0, 0, tiled=True)  128 us
    all_gather x1, blocking collectives, per_device(): proto_grad = lax.all_gather(proto_grad, dp, axis=0, tiled=True)  15.5 us
    all_to_all x2, starting transfers between devices, exchange(): return lax.all_to_all(x, axes, 0, 0, tiled=True)  9.9 us
    ppermute x3, starting transfers between devices, swap(): lax.ppermute(x, axis, [(i, i ^ step) for i in range(count)])  9.3 us
    ppermute x3, waiting for transfers between devices, swap(): lax.ppermute(x, axis, [(i, i ^ step) for i in range(count)])  4.26 us
  transfers between devices with their start and end apart: 5, of which 2 were waited for; matrix products, arithmetic and copies ran while one was open for 0% of the time, Pallas kernels for 1%

profile of v7, /device:TPU:1, one launch (start us, length us, event | category | flops | bytes accessed | tf_op | source)
XLA Modules:
  0.0 178.2 jit_solution(17334033085708640784)
XLA Ops:
  0.6 0.8 reshape.29.raw_ref
  1.4 27.4 %all_to_all.54 = bf16[16,24,128]{2,1,0:T(8,128)(2,1)S(1)} all-to-all(bf16[16,24,128]{2,1,0:T(8,128)(2,1)S(1)} %broadcast_in_dim.18), channel_id=1, replica_groups=mesh['y'=4,'core'=2,'x'=4,'z'=16] {'z'}, dimensions={0} | all-to-all | bytes 196608 | tf_op jit(solution)/shard_map/all_to_all | solution.py:240
  28.9 10.0 %all_to_all.55 = bf16[4,384,128]{2,1,0:T(8,128)(2,1)S(1)} all-to-all(bf16[4,384,128]{2,1,0:T(8,128)(2,1)S(1)} %broadcast_in_dim.20), channel_id=1, replica_groups=mesh['y'=4,'core'=2,'x'=4,'z'=16] {'x'}, dimensions={0} | all-to-all | bytes 786432 | tf_op jit(solution)/shard_map/all_to_all | solution.py:240
  38.9 1.4 scores.1
  40.4 13.1 %all_to_all.56 = bf16[8,24,128]{2,1,0:T(8,128)(2,1)S(1)} all-to-all(bf16[8,24,128]{2,1,0:T(8,128)(2,1)S(1)} %broadcast_in_dim.21), channel_id=1, replica_groups=mesh['y'=4,'core'=2,'x'=4,'z'=16] {'y','core'}, dimensions={0} | all-to-all | bytes 98304 | tf_op jit(solution)/shard_map/all_to_all | solution.py:240
  53.6 0.5 row_sum.3
  54.2 18.5 %all_to_all.57 = bf16[64,2,384]{2,1,0:T(2,128)(2,1)S(1)} all-to-all(bf16[64,2,384]{2,1,0:T(2,128)(2,1)S(1)} %broadcast_in_dim.22), channel_id=1, replica_groups=mesh['y'=4,'core'=2,'x'=4,'z'=16] {'x','z'}, dimensions={0} | all-to-all | bytes 196608 | tf_op jit(solution)/shard_map/all_to_all | solution.py:240
  73.0 9.9 %all_to_all.58 = bf16[8,24,128]{2,1,0:T(8,128)(2,1)S(1)} all-to-all(bf16[8,24,128]{2,1,0:T(8,128)(2,1)S(1)} %broadcast_in_dim.23), channel_id=1, replica_groups=mesh['y'=4,'core'=2,'x'=4,'z'=16] {'y','core'}, dimensions={0} | all-to-all | bytes 98304 | tf_op jit(solution)/shard_map/all_to_all | solution.py:240
  82.9 0.5 row_sum.4
  83.5 18.3 %all_to_all.59 = bf16[64,2,384]{2,1,0:T(2,128)(2,1)S(1)} all-to-all(bf16[64,2,384]{2,1,0:T(2,128)(2,1)S(1)} %broadcast_in_dim.24), channel_id=1, replica_groups=mesh['y'=4,'core'=2,'x'=4,'z'=16] {'x','z'}, dimensions={0} | all-to-all | bytes 196608 | tf_op jit(solution)/shard_map/all_to_all | solution.py:240
  102.2 9.9 %all_to_all.60 = bf16[8,24,128]{2,1,0:T(8,128)(2,1)S(1)} all-to-all(bf16[8,24,128]{2,1,0:T(8,128)(2,1)S(1)} %broadcast_in_dim.25), channel_id=1, replica_groups=mesh['y'=4,'core'=2,'x'=4,'z'=16] {'y','core'}, dimensions={0} | all-to-all | bytes 98304 | tf_op jit(solution)/shard_map/all_to_all | solution.py:240
  112.7 20.8 %all_to_all.61 = bf16[64,4,384]{2,1,0:T(4,128)(2,1)S(1)} all-to-all(bf16[64,4,384]{2,1,0:T(4,128)(2,1)S(1)} %broadcast_in_dim.26), channel_id=1, replica_groups=mesh['y'=4,'core'=2,'x'=4,'z'=16] {'x','z'}, dimensions={0} | all-to-all | bytes 393216 | tf_op jit(solution)/shard_map/all_to_all | solution.py:240
  133.5 2.2 %proto_part.1.tied_ref = bf16[1024,256]{1,0:T(8,128)(2,1)} custom-call(f32[4,384]{1,0:T(4,128)S(1)} %convert_reduce_fusion.totals_ref, f32[24,128]{1,0:T(8,128)S(1)} %get-tuple-element.21.inverse_ref, bf16[768,256]{1,0:T(8,128)(2,1)S(1)} %get-tuple-element.22.units_ref, bf16[1024,256]{1,0:T(8,128)(2,1)S(1)} %get-tuple-element.23.unit_protos_ref), custom_call_target="tpu_custom_call" | custom-call | tf_op jit(solution)/shard_map/proto_part/pallas_call | solution.py:298
  135.7 6.4 %all-to-all-start.8 = ((bf16[8,128,256]{2,1,0:T(8,128)(2,1)}), bf16[8,128,256]{2,1,0:T(8,128)(2,1)S(1)}, u32[]{:S(2)}, u32[]{:S(2)}) async-start(bf16[8,128,256]{2,1,0:T(8,128)(2,1)} %bitcast.4), calls=%async_computation.8 | async-start | bytes 1048576 | tf_op jit(solution)/shard_map/all_to_all | solution.py:240
  142.1 1.6 unit_grad.1
  143.7 4.7 %collective-permute-start = (bf16[192,256]{1,0:T(8,128)(2,1)S(1)}, bf16[192,256]{1,0:T(8,128)(2,1)S(1)}, u32[]{:S(2)}, u32[]{:S(2)}) collective-permute-start(bf16[192,256]{1,0:T(8,128)(2,1)S(1)} %get-tuple-element.25), channel_id=1, source_target_pairs={{0,32},{16,48},{32,0},{48,16},{1,33},{17,49},{33,1},{49,17},{2,34}... | collective-permute-start | bytes 294920 | tf_op jit(solution)/shard_map/ppermute | solution.py:256
  148.4 2.3 %collective-permute-start.1 = (bf16[192,256]{1,0:T(8,128)(2,1)S(1)}, bf16[192,256]{1,0:T(8,128)(2,1)S(1)}, u32[]{:S(2)}, u32[]{:S(2)}) collective-permute-start(bf16[192,256]{1,0:T(8,128)(2,1)S(1)} %get-tuple-element.26), channel_id=1, source_target_pairs={{0,16},{16,0},{32,48},{48,32},{1,17},{17,1},{33,49},{49,33},{2,18}... | collective-permute-start | bytes 294920 | tf_op jit(solution)/shard_map/ppermute | solution.py:256
  150.7 2.3 %collective-permute-start.2 = (bf16[192,256]{1,0:T(8,128)(2,1)S(1)}, bf16[192,256]{1,0:T(8,128)(2,1)S(1)}, u32[]{:S(2)}, u32[]{:S(2)}) collective-permute-start(bf16[192,256]{1,0:T(8,128)(2,1)S(1)} %get-tuple-element.27), channel_id=1, source_target_pairs={{0,48},{16,32},{32,16},{48,0},{1,49},{17,33},{33,17},{49,1},{2,50}... | collective-permute-start | bytes 294920 | tf_op jit(solution)/shard_map/ppermute | solution.py:256
  153.0 1.3 collective-permute-done.1.refs_2_
  154.3 3.0 %collective-permute-done.2.refs_3_ = bf16[192,256]{1,0:T(8,128)(2,1)S(1)} collective-permute-done((bf16[192,256]{1,0:T(8,128)(2,1)S(1)}, bf16[192,256]{1,0:T(8,128)(2,1)S(1)}, u32[]{:S(2)}, u32[]{:S(2)}) %collective-permute-start.2) | collective-permute-done | bytes 98336 | tf_op jit(solution)/shard_map/ppermute | solution.py:256
  157.3 0.9 middle.1
  158.2 3.5 %all-to-all-start.9 = ((bf16[16,24,128]{2,1,0:T(8,128)(2,1)}), bf16[16,24,128]{2,1,0:T(8,128)(2,1)S(1)}, u32[]{:S(2)}, u32[]{:S(2)}) async-start(bf16[16,24,128]{2,1,0:T(8,128)(2,1)} %get-tuple-element.28), calls=%async_computation.9 | async-start | bytes 196608 | tf_op jit(solution)/shard_map/all_to_all | solution.py:240
  161.7 15.5 %all_gather.3.protos_ref = bf16[1024,256]{1,0:T(8,128)(2,1)S(1)} all-gather(bf16[128,256]{1,0:T(8,128)(2,1)S(1)} %get-tuple-element.29), channel_id=1, replica_groups=mesh['y'=4,'core'=2,'x'=4,'z'=16] {'y','core'}, dimensions={0}, use_global_device_ids=true | all-gather | bytes 589824 | tf_op jit(solution)/shard_map/all_gather | solution.py:318
  177.2 1.1 last.1
  (30 shorter events, 1.7 us)
Async XLA Ops:
  0.6 38.3 %copy-start = (bf16[1024,256]{1,0:T(8,128)(2,1)S(1)}, bf16[1024,256]{1,0:T(8,128)(2,1)}, u32[]{:S(2)}) copy-start(bf16[1024,256]{1,0:T(8,128)(2,1)} %protos_ref.3) | copy-start | bytes 1572868
  135.7 21.5 %all-to-all-start.8 = ((bf16[8,128,256]{2,1,0:T(8,128)(2,1)}), bf16[8,128,256]{2,1,0:T(8,128)(2,1)S(1)}, u32[]{:S(2)}, u32[]{:S(2)}) async-start(bf16[8,128,256]{2,1,0:T(8,128)(2,1)} %bitcast.4), calls=%async_computation.8 | async-start | bytes 1048576 | tf_op jit(solution)/shard_map/all_to_all | solution.py:240
  143.7 9.3 %collective-permute-start = (bf16[192,256]{1,0:T(8,128)(2,1)S(1)}, bf16[192,256]{1,0:T(8,128)(2,1)S(1)}, u32[]{:S(2)}, u32[]{:S(2)}) collective-permute-start(bf16[192,256]{1,0:T(8,128)(2,1)S(1)} %get-tuple-element.25), channel_id=1, source_target_pairs={{0,32},{16,48},{32,0},{48,16},{1,33},{17,49},{33,1},{49,17},{2,34}... | collective-permute-start | bytes 294920 | tf_op jit(solution)/shard_map/ppermute | solution.py:256
  148.4 5.9 %collective-permute-start.1 = (bf16[192,256]{1,0:T(8,128)(2,1)S(1)}, bf16[192,256]{1,0:T(8,128)(2,1)S(1)}, u32[]{:S(2)}, u32[]{:S(2)}) collective-permute-start(bf16[192,256]{1,0:T(8,128)(2,1)S(1)} %get-tuple-element.26), channel_id=1, source_target_pairs={{0,16},{16,0},{32,48},{48,32},{1,17},{17,1},{33,49},{49,33},{2,18}... | collective-permute-start | bytes 294920 | tf_op jit(solution)/shard_map/ppermute | solution.py:256
  150.7 6.6 %collective-permute-start.2 = (bf16[192,256]{1,0:T(8,128)(2,1)S(1)}, bf16[192,256]{1,0:T(8,128)(2,1)S(1)}, u32[]{:S(2)}, u32[]{:S(2)}) collective-permute-start(bf16[192,256]{1,0:T(8,128)(2,1)S(1)} %get-tuple-element.27), channel_id=1, source_target_pairs={{0,48},{16,32},{32,16},{48,0},{1,49},{17,33},{33,17},{49,1},{2,50}... | collective-permute-start | bytes 294920 | tf_op jit(solution)/shard_map/ppermute | solution.py:256
  158.2 19.0 %all-to-all-start.9 = ((bf16[16,24,128]{2,1,0:T(8,128)(2,1)}), bf16[16,24,128]{2,1,0:T(8,128)(2,1)S(1)}, u32[]{:S(2)}, u32[]{:S(2)}) async-start(bf16[16,24,128]{2,1,0:T(8,128)(2,1)} %get-tuple-element.28), calls=%async_computation.9 | async-start | bytes 196608 | tf_op jit(solution)/shard_map/all_to_all | solution.py:240

commit v8 on v7

--- a/solution.py
+++ b/solution.py
@@ -290,10 +290,10 @@
     )(gathered, prototypes)
 
     for _ in range(2):
-        row = row_call(sum_over(mass, dp, groups), kernel)
-        mass = column_call(sum_over(row, ("x", "z"), nx * nz), kernel)
-    row, inverse = last_row_call(sum_over(mass, dp, groups), kernel, soft)
-    totals = sum_over(row, ("x", "z"), nx * nz)
+        row = row_call(sum_over(mass, ("core", "y"), groups), kernel)
+        mass = column_call(sum_over(row, ("z", "x"), nx * nz), kernel)
+    row, inverse = last_row_call(sum_over(mass, ("core", "y"), groups), kernel, soft)
+    totals = sum_over(row, ("z", "x"), nx * nz)
 
     proto_part = call(
         functools.partial(proto_body, modes), "proto_part", shape((local_protos, width), BF16), [WHOLE] * 4

time: 179 us -> 180 us (level)
  blocking collectives: 143 us -> 147 us
    all_to_all x8, blocking collectives: 128 us -> 131 us  [exchange(): return lax.all_to_all(x, axes, 0, 0, tiled=True)]
  transfers between devices with their start and end apart: 5 -> 5, of which waited for: 2 -> 1; matrix products, arithmetic and copies ran while one was open for 0% -> 0% of each run, Pallas kernels for 1% -> 1%
where the time goes in v8:
time: 180 us; the launch traced here: 179 us
  blocking collectives  147 us (82%)
  starting transfers between devices  18.4 us (10%)
  Pallas kernels  9.31 us (5%)
  waiting for transfers between devices  2.79 us (2%)
    all_to_all x8, blocking collectives, exchange(): return lax.all_to_all(x, axes, 0, 0, tiled=True)  131 us
    all_gather x1, blocking collectives, per_device(): proto_grad = lax.all_gather(proto_grad, dp, axis=0, tiled=True)  15.5 us
    all_to_all x2, starting transfers between devices, exchange(): return lax.all_to_all(x, axes, 0, 0, tiled=True)  9.34 us
    ppermute x3, starting transfers between devices, swap(): lax.ppermute(x, axis, [(i, i ^ step) for i in range(count)])  9.01 us
  transfers between devices with their start and end apart: 5, of which 1 were waited for; matrix products, arithmetic and copies ran while one was open for 0% of the time, Pallas kernels for 1%

profile of v8, /device:TPU:1, one launch (start us, length us, event | category | flops | bytes accessed | tf_op | source)
XLA Modules:
  0.0 179.1 jit_solution(11584831355492482785)
XLA Ops:
  0.6 0.8 reshape.29.raw_ref
  1.4 27.4 %all_to_all.54 = bf16[16,24,128]{2,1,0:T(8,128)(2,1)S(1)} all-to-all(bf16[16,24,128]{2,1,0:T(8,128)(2,1)S(1)} %broadcast_in_dim.18), channel_id=1, replica_groups=mesh['y'=4,'core'=2,'x'=4,'z'=16] {'z'}, dimensions={0} | all-to-all | bytes 196608 | tf_op jit(solution)/shard_map/all_to_all | solution.py:240
  28.9 10.0 %all_to_all.55 = bf16[4,384,128]{2,1,0:T(8,128)(2,1)S(1)} all-to-all(bf16[4,384,128]{2,1,0:T(8,128)(2,1)S(1)} %broadcast_in_dim.20), channel_id=1, replica_groups=mesh['y'=4,'core'=2,'x'=4,'z'=16] {'x'}, dimensions={0} | all-to-all | bytes 786432 | tf_op jit(solution)/shard_map/all_to_all | solution.py:240
  38.9 1.4 scores.1
  40.4 13.3 %all_to_all.56 = bf16[8,24,128]{2,1,0:T(8,128)(2,1)S(1)} all-to-all(bf16[8,24,128]{2,1,0:T(8,128)(2,1)S(1)} %broadcast_in_dim.21), channel_id=1, replica_groups=mesh['y'=4,'core'=2,'x'=4,'z'=16] {'core','y'}, dimensions={0} | all-to-all | bytes 98304 | tf_op jit(solution)/shard_map/all_to_all | solution.py:240
  53.7 0.5 row_sum.3
  54.3 19.3 %all_to_all.57 = bf16[64,2,384]{2,1,0:T(2,128)(2,1)S(1)} all-to-all(bf16[64,2,384]{2,1,0:T(2,128)(2,1)S(1)} %broadcast_in_dim.22), channel_id=1, replica_groups=mesh['y'=4,'core'=2,'x'=4,'z'=16] {'z','x'}, dimensions={0} | all-to-all | bytes 196608 | tf_op jit(solution)/shard_map/all_to_all | solution.py:240
  74.0 9.9 %all_to_all.58 = bf16[8,24,128]{2,1,0:T(8,128)(2,1)S(1)} all-to-all(bf16[8,24,128]{2,1,0:T(8,128)(2,1)S(1)} %broadcast_in_dim.23), channel_id=1, replica_groups=mesh['y'=4,'core'=2,'x'=4,'z'=16] {'core','y'}, dimensions={0} | all-to-all | bytes 98304 | tf_op jit(solution)/shard_map/all_to_all | solution.py:240
  83.9 0.5 row_sum.4
  84.5 18.5 %all_to_all.59 = bf16[64,2,384]{2,1,0:T(2,128)(2,1)S(1)} all-to-all(bf16[64,2,384]{2,1,0:T(2,128)(2,1)S(1)} %broadcast_in_dim.24), channel_id=1, replica_groups=mesh['y'=4,'core'=2,'x'=4,'z'=16] {'z','x'}, dimensions={0} | all-to-all | bytes 196608 | tf_op jit(solution)/shard_map/all_to_all | solution.py:240
  103.5 9.9 %all_to_all.60 = bf16[8,24,128]{2,1,0:T(8,128)(2,1)S(1)} all-to-all(bf16[8,24,128]{2,1,0:T(8,128)(2,1)S(1)} %broadcast_in_dim.25), channel_id=1, replica_groups=mesh['y'=4,'core'=2,'x'=4,'z'=16] {'core','y'}, dimensions={0} | all-to-all | bytes 98304 | tf_op jit(solution)/shard_map/all_to_all | solution.py:240
  113.4 0.5 row_sum.5
  114.0 22.7 %all_to_all.61 = bf16[64,4,384]{2,1,0:T(4,128)(2,1)S(1)} all-to-all(bf16[64,4,384]{2,1,0:T(4,128)(2,1)S(1)} %broadcast_in_dim.26), channel_id=1, replica_groups=mesh['y'=4,'core'=2,'x'=4,'z'=16] {'z','x'}, dimensions={0} | all-to-all | bytes 393216 | tf_op jit(solution)/shard_map/all_to_all | solution.py:240
  136.7 2.2 %proto_part.1.tied_ref = bf16[1024,256]{1,0:T(8,128)(2,1)} custom-call(f32[4,384]{1,0:T(4,128)S(1)} %convert_reduce_fusion.totals_ref, f32[24,128]{1,0:T(8,128)S(1)} %get-tuple-element.21.inverse_ref, bf16[768,256]{1,0:T(8,128)(2,1)S(1)} %get-tuple-element.22.units_ref, bf16[1024,256]{1,0:T(8,128)(2,1)S(1)} %get-tuple-element.23.unit_protos_ref), custom_call_target="tpu_custom_call" | custom-call | tf_op jit(solution)/shard_map/proto_part/pallas_call | solution.py:298
  138.9 5.8 %all-to-all-start.8 = ((bf16[8,128,256]{2,1,0:T(8,128)(2,1)}), bf16[8,128,256]{2,1,0:T(8,128)(2,1)S(1)}, u32[]{:S(2)}, u32[]{:S(2)}) async-start(bf16[8,128,256]{2,1,0:T(8,128)(2,1)} %bitcast.4), calls=%async_computation.8 | async-start | bytes 1048576 | tf_op jit(solution)/shard_map/all_to_all | solution.py:240
  144.8 1.6 unit_grad.1
  146.3 3.1 %collective-permute-start = (bf16[192,256]{1,0:T(8,128)(2,1)S(1)}, bf16[192,256]{1,0:T(8,128)(2,1)S(1)}, u32[]{:S(2)}, u32[]{:S(2)}) collective-permute-start(bf16[192,256]{1,0:T(8,128)(2,1)S(1)} %get-tuple-element.25), channel_id=1, source_target_pairs={{0,32},{16,48},{32,0},{48,16},{1,33},{17,49},{33,1},{49,17},{2,34}... | collective-permute-start | bytes 294920 | tf_op jit(solution)/shard_map/ppermute | solution.py:256
  149.4 2.2 %collective-permute-start.1 = (bf16[192,256]{1,0:T(8,128)(2,1)S(1)}, bf16[192,256]{1,0:T(8,128)(2,1)S(1)}, u32[]{:S(2)}, u32[]{:S(2)}) collective-permute-start(bf16[192,256]{1,0:T(8,128)(2,1)S(1)} %get-tuple-element.26), channel_id=1, source_target_pairs={{0,16},{16,0},{32,48},{48,32},{1,17},{17,1},{33,49},{49,33},{2,18}... | collective-permute-start | bytes 294920 | tf_op jit(solution)/shard_map/ppermute | solution.py:256
  151.6 3.8 %collective-permute-start.2 = (bf16[192,256]{1,0:T(8,128)(2,1)S(1)}, bf16[192,256]{1,0:T(8,128)(2,1)S(1)}, u32[]{:S(2)}, u32[]{:S(2)}) collective-permute-start(bf16[192,256]{1,0:T(8,128)(2,1)S(1)} %get-tuple-element.27), channel_id=1, source_target_pairs={{0,48},{16,32},{32,16},{48,0},{1,49},{17,33},{33,17},{49,1},{2,50}... | collective-permute-start | bytes 294920 | tf_op jit(solution)/shard_map/ppermute | solution.py:256
  155.4 2.8 %collective-permute-done.2.refs_3_ = bf16[192,256]{1,0:T(8,128)(2,1)S(1)} collective-permute-done((bf16[192,256]{1,0:T(8,128)(2,1)S(1)}, bf16[192,256]{1,0:T(8,128)(2,1)S(1)}, u32[]{:S(2)}, u32[]{:S(2)}) %collective-permute-start.2) | collective-permute-done | bytes 98336 | tf_op jit(solution)/shard_map/ppermute | solution.py:256
  158.2 0.9 middle.1
  159.1 3.5 %all-to-all-start.9 = ((bf16[16,24,128]{2,1,0:T(8,128)(2,1)}), bf16[16,24,128]{2,1,0:T(8,128)(2,1)S(1)}, u32[]{:S(2)}, u32[]{:S(2)}) async-start(bf16[16,24,128]{2,1,0:T(8,128)(2,1)} %get-tuple-element.28), calls=%async_computation.9 | async-start | bytes 196608 | tf_op jit(solution)/shard_map/all_to_all | solution.py:240
  162.6 15.5 %all_gather.3.protos_ref = bf16[1024,256]{1,0:T(8,128)(2,1)S(1)} all-gather(bf16[128,256]{1,0:T(8,128)(2,1)S(1)} %get-tuple-element.29), channel_id=1, replica_groups=mesh['y'=4,'core'=2,'x'=4,'z'=16] {'y','core'}, dimensions={0}, use_global_device_ids=true | all-gather | bytes 589824 | tf_op jit(solution)/shard_map/all_gather | solution.py:318
  178.1 1.1 last.1
  (30 shorter events, 1.2 us)
Async XLA Ops:
  0.6 38.3 %copy-start = (bf16[1024,256]{1,0:T(8,128)(2,1)S(1)}, bf16[1024,256]{1,0:T(8,128)(2,1)}, u32[]{:S(2)}) copy-start(bf16[1024,256]{1,0:T(8,128)(2,1)} %protos_ref.3) | copy-start | bytes 1572868
  138.9 19.2 %all-to-all-start.8 = ((bf16[8,128,256]{2,1,0:T(8,128)(2,1)}), bf16[8,128,256]{2,1,0:T(8,128)(2,1)S(1)}, u32[]{:S(2)}, u32[]{:S(2)}) async-start(bf16[8,128,256]{2,1,0:T(8,128)(2,1)} %bitcast.4), calls=%async_computation.8 | async-start | bytes 1048576 | tf_op jit(solution)/shard_map/all_to_all | solution.py:240
  146.3 9.0 %collective-permute-start = (bf16[192,256]{1,0:T(8,128)(2,1)S(1)}, bf16[192,256]{1,0:T(8,128)(2,1)S(1)}, u32[]{:S(2)}, u32[]{:S(2)}) collective-permute-start(bf16[192,256]{1,0:T(8,128)(2,1)S(1)} %get-tuple-element.25), channel_id=1, source_target_pairs={{0,32},{16,48},{32,0},{48,16},{1,33},{17,49},{33,1},{49,17},{2,34}... | collective-permute-start | bytes 294920 | tf_op jit(solution)/shard_map/ppermute | solution.py:256
  149.4 6.0 %collective-permute-start.1 = (bf16[192,256]{1,0:T(8,128)(2,1)S(1)}, bf16[192,256]{1,0:T(8,128)(2,1)S(1)}, u32[]{:S(2)}, u32[]{:S(2)}) collective-permute-start(bf16[192,256]{1,0:T(8,128)(2,1)S(1)} %get-tuple-element.26), channel_id=1, source_target_pairs={{0,16},{16,0},{32,48},{48,32},{1,17},{17,1},{33,49},{49,33},{2,18}... | collective-permute-start | bytes 294920 | tf_op jit(solution)/shard_map/ppermute | solution.py:256
  151.6 6.6 %collective-permute-start.2 = (bf16[192,256]{1,0:T(8,128)(2,1)S(1)}, bf16[192,256]{1,0:T(8,128)(2,1)S(1)}, u32[]{:S(2)}, u32[]{:S(2)}) collective-permute-start(bf16[192,256]{1,0:T(8,128)(2,1)S(1)} %get-tuple-element.27), channel_id=1, source_target_pairs={{0,48},{16,32},{32,16},{48,0},{1,49},{17,33},{33,17},{49,1},{2,50}... | collective-permute-start | bytes 294920 | tf_op jit(solution)/shard_map/ppermute | solution.py:256
  159.1 19.0 %all-to-all-start.9 = ((bf16[16,24,128]{2,1,0:T(8,128)(2,1)}), bf16[16,24,128]{2,1,0:T(8,128)(2,1)S(1)}, u32[]{:S(2)}, u32[]{:S(2)}) async-start(bf16[16,24,128]{2,1,0:T(8,128)(2,1)} %get-tuple-element.28), calls=%async_computation.9 | async-start | bytes 196608 | tf_op jit(solution)/shard_map/all_to_all | solution.py:240

commit v9 on v8

--- a/solution.py
+++ b/solution.py
@@ -236,20 +236,20 @@
         grad_ref[m] = grad[m * owned : (m + 1) * owned]
 
 
-def exchange(x, axes):
-    return lax.all_to_all(x, axes, 0, 0, tiled=True)
-
-
-def copies(x, axes, count):
-    return exchange(jnp.broadcast_to(x[None], (count,) + x.shape), axes)
-
-
-def gather(x, axes, count):
-    return copies(x, axes, count).reshape((count * x.shape[0],) + x.shape[1:])
-
-
-def sum_over(x, axes, count):
-    return jnp.sum(copies(x.astype(BF16), axes, count).astype(F32), axis=0)
+def exchange(x, axes, order=None):
+    return lax.all_to_all(x, axes, 0, 0, axis_index_groups=None if order is None else [order], tiled=True)
+
+
+def copies(x, axes, count, order=None):
+    return exchange(jnp.broadcast_to(x[None], (count,) + x.shape), axes, order)
+
+
+def gather(x, axes, count, order=None):
+    return copies(x, axes, count, order).reshape((count * x.shape[0],) + x.shape[1:])
+
+
+def sum_over(x, axes, count, order=None):
+    return jnp.sum(copies(x.astype(BF16), axes, count, order).astype(F32), axis=0)
 
 
 def swap(x, axis, count, step):
@@ -278,9 +278,10 @@
     )
     column_call = call(functools.partial(column_body, modes), "column_sum", mass_shape, [WHOLE] * 2)
 
+    folded = list(range(0, nz, 2)) + list(range(1, nz, 2))[::-1]
     raw_rows = embeddings.transpose(1, 0, 2).reshape(owned, width)
     raw_tiles = jnp.concatenate([raw_rows[:, h : h + LANES] for h in range(0, width, LANES)], axis=0)
-    gathered = gather(gather(raw_tiles, "z", nz), "x", nx)
+    gathered = gather(gather(raw_tiles, "z", nz, folded), "x", nx)
     kernel, units, unit_protos, soft, mass = call(
         functools.partial(score_body, modes, own_samples),
         "scores",
@@ -291,9 +292,9 @@
 
     for _ in range(2):
         row = row_call(sum_over(mass, ("core", "y"), groups), kernel)
-        mass = column_call(sum_over(row, ("z", "x"), nx * nz), kernel)
+        mass = column_call(sum_over(row, ("x", "z"), nx * nz, [x * nz + z for x in range(nx) for z in folded]), kernel)
     row, inverse = last_row_call(sum_over(mass, ("core", "y"), groups), kernel, soft)
-    totals = sum_over(row, ("z", "x"), nx * nz)
+    totals = sum_over(row, ("x", "z"), nx * nz, [x * nz + z for x in range(nx) for z in folded])
 
     proto_part = call(
         functools.partial(proto_body, modes), "proto_part", shape((local_protos, width), BF16), [WHOLE] * 4
@@ -314,7 +315,7 @@
         [SCALARS] + [WHOLE] * (2 + nx),
         [pltpu.VMEM((width // LANES, x_lines, LANES), F32)],
     )(dp_place, proto_part, prototypes, *pieces)
-    rows = exchange(rows, "z")
+    rows = exchange(rows, "z", folded)
     proto_grad = lax.all_gather(proto_grad, dp, axis=0, tiled=True)
     embed_grad, proto_grad = call(
         last_body,

time: 180 us -> 179 us (level)
  blocking collectives: 147 us -> 145 us
  transfers between devices with their start and end apart: 5 -> 5, of which waited for: 1 -> 2; matrix products, arithmetic and copies ran while one was open for 0% -> 0% of each run, Pallas kernels for 1% -> 1%
where the time goes in v9:
time: 179 us
  blocking collectives  145 us (81%)
  starting transfers between devices  18.2 us (10%)
  Pallas kernels  9.31 us (5%)
  waiting for transfers between devices  4.13 us (2%)
    all_to_all x8, blocking collectives, exchange(): lax.all_to_all(x, axes, 0, 0, axis_index_groups=None if order is None els...  130 us
    all_gather x1, blocking collectives, per_device(): proto_grad = lax.all_gather(proto_grad, dp, axis=0, tiled=True)  14.7 us
    all_to_all x2, starting transfers between devices, exchange(): lax.all_to_all(x, axes, 0, 0, axis_index_groups=None if order is None els...  9.18 us
    ppermute x3, starting transfers between devices, swap(): lax.ppermute(x, axis, [(i, i ^ step) for i in range(count)])  9.07 us
    ppermute x3, waiting for transfers between devices, swap(): lax.ppermute(x, axis, [(i, i ^ step) for i in range(count)])  4.12 us
  transfers between devices with their start and end apart: 5, of which 2 were waited for; matrix products, arithmetic and copies ran while one was open for 0% of the time, Pallas kernels for 1%

profile of v9, /device:TPU:1, one launch (start us, length us, event | category | flops | bytes accessed | tf_op | source)
XLA Modules:
  0.0 178.8 jit_solution(6648891459280864206)
XLA Ops:
  0.6 0.8 reshape.29.raw_ref
  1.4 27.6 %all_to_all.54 = bf16[16,24,128]{2,1,0:T(8,128)(2,1)S(1)} all-to-all(bf16[16,24,128]{2,1,0:T(8,128)(2,1)S(1)} %broadcast_in_dim.18), channel_id=1, replica_groups={{0,2,4,6,8,10,12,14,15,13,11,9,7,5,3,1},{16,18,20,22,24,26,28,30,31,29,..., dimensions={0} | all-to-all | bytes 196608 | tf_op jit(solution)/shard_map/all_to_all | solution.py:240
  29.1 10.0 %all_to_all.55 = bf16[4,384,128]{2,1,0:T(8,128)(2,1)S(1)} all-to-all(bf16[4,384,128]{2,1,0:T(8,128)(2,1)S(1)} %broadcast_in_dim.20), channel_id=1, replica_groups=mesh['y'=4,'core'=2,'x'=4,'z'=16] {'x'}, dimensions={0} | all-to-all | bytes 786432 | tf_op jit(solution)/shard_map/all_to_all | solution.py:240
  39.2 1.4 scores.1
  40.7 13.2 %all_to_all.56 = bf16[8,24,128]{2,1,0:T(8,128)(2,1)S(1)} all-to-all(bf16[8,24,128]{2,1,0:T(8,128)(2,1)S(1)} %broadcast_in_dim.21), channel_id=1, replica_groups=mesh['y'=4,'core'=2,'x'=4,'z'=16] {'core','y'}, dimensions={0} | all-to-all | bytes 98304 | tf_op jit(solution)/shard_map/all_to_all | solution.py:240
  53.9 0.5 row_sum.3
  54.5 19.1 %all_to_all.57 = bf16[64,2,384]{2,1,0:T(2,128)(2,1)S(1)} all-to-all(bf16[64,2,384]{2,1,0:T(2,128)(2,1)S(1)} %broadcast_in_dim.22), channel_id=1, replica_groups={{0,2,4,6,8,10,12,14,15,13,11,9,7,5,3,1,16,18,20,22,24,26,28,30,31,29,27..., dimensions={0} | all-to-all | bytes 196608 | tf_op jit(solution)/shard_map/all_to_all | solution.py:240
  74.0 9.9 %all_to_all.58 = bf16[8,24,128]{2,1,0:T(8,128)(2,1)S(1)} all-to-all(bf16[8,24,128]{2,1,0:T(8,128)(2,1)S(1)} %broadcast_in_dim.23), channel_id=1, replica_groups=mesh['y'=4,'core'=2,'x'=4,'z'=16] {'core','y'}, dimensions={0} | all-to-all | bytes 98304 | tf_op jit(solution)/shard_map/all_to_all | solution.py:240
  83.9 0.5 row_sum.4
  84.5 18.4 %all_to_all.59 = bf16[64,2,384]{2,1,0:T(2,128)(2,1)S(1)} all-to-all(bf16[64,2,384]{2,1,0:T(2,128)(2,1)S(1)} %broadcast_in_dim.24), channel_id=1, replica_groups={{0,2,4,6,8,10,12,14,15,13,11,9,7,5,3,1,16,18,20,22,24,26,28,30,31,29,27..., dimensions={0} | all-to-all | bytes 196608 | tf_op jit(solution)/shard_map/all_to_all | solution.py:240
  103.2 9.9 %all_to_all.60 = bf16[8,24,128]{2,1,0:T(8,128)(2,1)S(1)} all-to-all(bf16[8,24,128]{2,1,0:T(8,128)(2,1)S(1)} %broadcast_in_dim.25), channel_id=1, replica_groups=mesh['y'=4,'core'=2,'x'=4,'z'=16] {'core','y'}, dimensions={0} | all-to-all | bytes 98304 | tf_op jit(solution)/shard_map/all_to_all | solution.py:240
  113.8 22.2 %all_to_all.61 = bf16[64,4,384]{2,1,0:T(4,128)(2,1)S(1)} all-to-all(bf16[64,4,384]{2,1,0:T(4,128)(2,1)S(1)} %broadcast_in_dim.26), channel_id=1, replica_groups={{0,2,4,6,8,10,12,14,15,13,11,9,7,5,3,1,16,18,20,22,24,26,28,30,31,29,27..., dimensions={0} | all-to-all | bytes 393216 | tf_op jit(solution)/shard_map/all_to_all | solution.py:240
  136.0 2.2 %proto_part.1.tied_ref = bf16[1024,256]{1,0:T(8,128)(2,1)} custom-call(f32[4,384]{1,0:T(4,128)S(1)} %convert_reduce_fusion.totals_ref, f32[24,128]{1,0:T(8,128)S(1)} %get-tuple-element.21.inverse_ref, bf16[768,256]{1,0:T(8,128)(2,1)S(1)} %get-tuple-element.22.units_ref, bf16[1024,256]{1,0:T(8,128)(2,1)S(1)} %get-tuple-element.23.unit_protos_ref), custom_call_target="tpu_custom_call" | custom-call | tf_op jit(solution)/shard_map/proto_part/pallas_call | solution.py:299
  138.3 5.7 %all-to-all-start.8 = ((bf16[8,128,256]{2,1,0:T(8,128)(2,1)}), bf16[8,128,256]{2,1,0:T(8,128)(2,1)S(1)}, u32[]{:S(2)}, u32[]{:S(2)}) async-start(bf16[8,128,256]{2,1,0:T(8,128)(2,1)} %bitcast.4), calls=%async_computation.8 | async-start | bytes 1048576 | tf_op jit(solution)/shard_map/all_to_all | solution.py:240
  143.9 1.6 unit_grad.1
  145.5 4.2 %collective-permute-start = (bf16[192,256]{1,0:T(8,128)(2,1)S(1)}, bf16[192,256]{1,0:T(8,128)(2,1)S(1)}, u32[]{:S(2)}, u32[]{:S(2)}) collective-permute-start(bf16[192,256]{1,0:T(8,128)(2,1)S(1)} %get-tuple-element.25), channel_id=1, source_target_pairs={{0,32},{16,48},{32,0},{48,16},{1,33},{17,49},{33,1},{49,17},{2,34}... | collective-permute-start | bytes 294920 | tf_op jit(solution)/shard_map/ppermute | solution.py:256
  149.7 1.9 %collective-permute-start.1 = (bf16[192,256]{1,0:T(8,128)(2,1)S(1)}, bf16[192,256]{1,0:T(8,128)(2,1)S(1)}, u32[]{:S(2)}, u32[]{:S(2)}) collective-permute-start(bf16[192,256]{1,0:T(8,128)(2,1)S(1)} %get-tuple-element.26), channel_id=1, source_target_pairs={{0,16},{16,0},{32,48},{48,32},{1,17},{17,1},{33,49},{49,33},{2,18}... | collective-permute-start | bytes 294920 | tf_op jit(solution)/shard_map/ppermute | solution.py:256
  151.6 3.0 %collective-permute-start.2 = (bf16[192,256]{1,0:T(8,128)(2,1)S(1)}, bf16[192,256]{1,0:T(8,128)(2,1)S(1)}, u32[]{:S(2)}, u32[]{:S(2)}) collective-permute-start(bf16[192,256]{1,0:T(8,128)(2,1)S(1)} %get-tuple-element.27), channel_id=1, source_target_pairs={{0,48},{16,32},{32,16},{48,0},{1,49},{17,33},{33,17},{49,1},{2,50}... | collective-permute-start | bytes 294920 | tf_op jit(solution)/shard_map/ppermute | solution.py:256
  154.6 1.0 collective-permute-done.1.refs_2_
  155.6 3.1 %collective-permute-done.2.refs_3_ = bf16[192,256]{1,0:T(8,128)(2,1)S(1)} collective-permute-done((bf16[192,256]{1,0:T(8,128)(2,1)S(1)}, bf16[192,256]{1,0:T(8,128)(2,1)S(1)}, u32[]{:S(2)}, u32[]{:S(2)}) %collective-permute-start.2) | collective-permute-done | bytes 98336 | tf_op jit(solution)/shard_map/ppermute | solution.py:256
  158.7 0.9 middle.1
  159.6 3.5 %all-to-all-start.9 = ((bf16[16,24,128]{2,1,0:T(8,128)(2,1)}), bf16[16,24,128]{2,1,0:T(8,128)(2,1)S(1)}, u32[]{:S(2)}, u32[]{:S(2)}) async-start(bf16[16,24,128]{2,1,0:T(8,128)(2,1)} %get-tuple-element.28), calls=%async_computation.9 | async-start | bytes 196608 | tf_op jit(solution)/shard_map/all_to_all | solution.py:240
  163.1 14.7 %all_gather.3.protos_ref = bf16[1024,256]{1,0:T(8,128)(2,1)S(1)} all-gather(bf16[128,256]{1,0:T(8,128)(2,1)S(1)} %get-tuple-element.29), channel_id=1, replica_groups=mesh['y'=4,'core'=2,'x'=4,'z'=16] {'y','core'}, dimensions={0}, use_global_device_ids=true | all-gather | bytes 589824 | tf_op jit(solution)/shard_map/all_gather | solution.py:319
  177.8 1.1 last.1
  (30 shorter events, 1.7 us)
Async XLA Ops:
  0.6 38.5 %copy-start = (bf16[1024,256]{1,0:T(8,128)(2,1)S(1)}, bf16[1024,256]{1,0:T(8,128)(2,1)}, u32[]{:S(2)}) copy-start(bf16[1024,256]{1,0:T(8,128)(2,1)} %protos_ref.3) | copy-start | bytes 1572868
  138.3 20.5 %all-to-all-start.8 = ((bf16[8,128,256]{2,1,0:T(8,128)(2,1)}), bf16[8,128,256]{2,1,0:T(8,128)(2,1)S(1)}, u32[]{:S(2)}, u32[]{:S(2)}) async-start(bf16[8,128,256]{2,1,0:T(8,128)(2,1)} %bitcast.4), calls=%async_computation.8 | async-start | bytes 1048576 | tf_op jit(solution)/shard_map/all_to_all | solution.py:240
  145.5 9.1 %collective-permute-start = (bf16[192,256]{1,0:T(8,128)(2,1)S(1)}, bf16[192,256]{1,0:T(8,128)(2,1)S(1)}, u32[]{:S(2)}, u32[]{:S(2)}) collective-permute-start(bf16[192,256]{1,0:T(8,128)(2,1)S(1)} %get-tuple-element.25), channel_id=1, source_target_pairs={{0,32},{16,48},{32,0},{48,16},{1,33},{17,49},{33,1},{49,17},{2,34}... | collective-permute-start | bytes 294920 | tf_op jit(solution)/shard_map/ppermute | solution.py:256
  149.7 5.9 %collective-permute-start.1 = (bf16[192,256]{1,0:T(8,128)(2,1)S(1)}, bf16[192,256]{1,0:T(8,128)(2,1)S(1)}, u32[]{:S(2)}, u32[]{:S(2)}) collective-permute-start(bf16[192,256]{1,0:T(8,128)(2,1)S(1)} %get-tuple-element.26), channel_id=1, source_target_pairs={{0,16},{16,0},{32,48},{48,32},{1,17},{17,1},{33,49},{49,33},{2,18}... | collective-permute-start | bytes 294920 | tf_op jit(solution)/shard_map/ppermute | solution.py:256
  151.6 7.1 %collective-permute-start.2 = (bf16[192,256]{1,0:T(8,128)(2,1)S(1)}, bf16[192,256]{1,0:T(8,128)(2,1)S(1)}, u32[]{:S(2)}, u32[]{:S(2)}) collective-permute-start(bf16[192,256]{1,0:T(8,128)(2,1)S(1)} %get-tuple-element.27), channel_id=1, source_target_pairs={{0,48},{16,32},{32,16},{48,0},{1,49},{17,33},{33,17},{49,1},{2,50}... | collective-permute-start | bytes 294920 | tf_op jit(solution)/shard_map/ppermute | solution.py:256
  159.6 18.2 %all-to-all-start.9 = ((bf16[16,24,128]{2,1,0:T(8,128)(2,1)}), bf16[16,24,128]{2,1,0:T(8,128)(2,1)S(1)}, u32[]{:S(2)}, u32[]{:S(2)}) async-start(bf16[16,24,128]{2,1,0:T(8,128)(2,1)} %get-tuple-element.28), calls=%async_computation.9 | async-start | bytes 196608 | tf_op jit(solution)/shard_map/all_to_all | solution.py:240

commit v10 on v8

--- a/solution.py
+++ b/solution.py
@@ -176,32 +176,30 @@
             piece[j * chunk : (j + 1) * chunk, :] = sums[pl.ds(first, chunk), :].astype(BF16)
 
 
-def proto_body(modes, totals_ref, inverse_ref, units_ref, unit_protos_ref, proto_ref):
+def proto_body(modes, totals_ref, inverse_ref, units_ref, unit_protos_ref, kernel_ref, proto_ref):
     samples = units_ref.shape[0] // modes
     width = unit_protos_ref.shape[0]
     tiles = width // LANES
-    inverse = inverse_ref[...].T
-    weight = COEFFICIENT / totals_ref[0:2]
-    spread = 2.0 * COEFFICIENT / totals_ref[2:4]
-    weight = [mode_of(weight, m, samples // LANES) for m in range(modes)]
-    spread = [mode_of(spread, m, samples // LANES) for m in range(modes)]
+    copies_across = units_ref.shape[1] // LANES
+    rows = [slice(m * samples, (m + 1) * samples) for m in range(modes)]
+    weight = jnp.concatenate([upright(COEFFICIENT / totals_ref[0:2])] * copies_across, axis=1)
+    spread = jnp.concatenate([upright(2.0 * COEFFICIENT / totals_ref[2:4])] * copies_across, axis=1)
+    units = [units_ref[rows[m], :].astype(F32) for m in range(modes)]
+    for_predicted = jnp.concatenate([(spread[rows[m]] * units[m]).astype(BF16) for m in range(modes)], axis=0)
+    for_codes = [
+        (weight[rows[m]] * functools.reduce(jnp.add, [units[n] for n in range(modes) if n != m])).T.astype(BF16)
+        for m in range(modes)
+    ]
     step = 256
     for k in range(0, width, step):
         scores = lax.dot_general(unit_protos_ref[k : k + step, :], units_ref[...], NT, preferred_element_type=F32)
-        codes, predicted = [], []
+        soft = jnp.exp2((10.0 * LOG2_E) * scores).astype(BF16)
+        total = jnp.dot(soft, for_predicted, preferred_element_type=F32)
+        codes = jnp.zeros((units_ref.shape[1], step), F32)
         for m in range(modes):
-            first = m * tiles + k // LANES
-            upright_inverse = jnp.concatenate([inverse[:, first + j : first + j + 1] for j in range(step // LANES)], axis=0)
-            soft = jnp.exp2((10.0 * LOG2_E) * scores[:, m * samples : (m + 1) * samples])
-            codes.append(soft * soft * upright_inverse * weight[m])
-            predicted.append(soft * spread[m])
-        logit = [
-            (predicted[m] - functools.reduce(jnp.add, [codes[n] for n in range(modes) if n != m])).astype(BF16)
-            for m in range(modes)
-        ]
-        proto_ref[k : k + step, :] = jnp.dot(
-            jnp.concatenate(logit, axis=1), units_ref[...], preferred_element_type=F32
-        ).astype(BF16)
+            inverse = tiles_to_line(inverse_ref[...], m * tiles + k // LANES, step // LANES)
+            codes = codes + inverse * jnp.dot(for_codes[m], kernel_ref[rows[m], k : k + step], preferred_element_type=F32)
+        proto_ref[k : k + step, :] = (total - codes.T).astype(BF16)
 
 
 def middle_body(place_ref, parts_ref, protos_ref, *refs):
@@ -291,13 +289,13 @@
 
     for _ in range(2):
         row = row_call(sum_over(mass, ("core", "y"), groups), kernel)
-        mass = column_call(sum_over(row, ("z", "x"), nx * nz), kernel)
+        mass = column_call(sum_over(row, ("x", "z"), nx * nz), kernel)
     row, inverse = last_row_call(sum_over(mass, ("core", "y"), groups), kernel, soft)
-    totals = sum_over(row, ("z", "x"), nx * nz)
+    totals = sum_over(row, ("x", "z"), nx * nz)
 
     proto_part = call(
-        functools.partial(proto_body, modes), "proto_part", shape((local_protos, width), BF16), [WHOLE] * 4
-    )(totals, inverse, units, unit_protos)
+        functools.partial(proto_body, modes), "proto_part", shape((local_protos, width), BF16), [WHOLE] * 5
+    )(totals, inverse, units, unit_protos, kernel)
     pieces = call(
         functools.partial(unit_body, modes, own_samples),
         "unit_grad",

time: 180 us -> 180 us (level)
  blocking collectives: 147 us -> 144 us
    all_to_all x8, blocking collectives: 131 us -> 129 us  [exchange(): return lax.all_to_all(x, axes, 0, 0, tiled=True)]
  transfers between devices with their start and end apart: 5 -> 5, of which waited for: 1 -> 2; matrix products, arithmetic and copies ran while one was open for 0% -> 0% of each run, Pallas kernels for 1% -> 1%
where the time goes in v10:
time: 180 us; the launch traced here: 179 us
  blocking collectives  144 us (80%)
  starting transfers between devices  18.6 us (10%)
  Pallas kernels  9.76 us (5%)
  waiting for transfers between devices  4.21 us (2%)
    all_to_all x8, blocking collectives, exchange(): return lax.all_to_all(x, axes, 0, 0, tiled=True)  129 us
    all_gather x1, blocking collectives, per_device(): proto_grad = lax.all_gather(proto_grad, dp, axis=0, tiled=True)  15.5 us
    all_to_all x2, starting transfers between devices, exchange(): return lax.all_to_all(x, axes, 0, 0, tiled=True)  9.34 us
    ppermute x3, starting transfers between devices, swap(): lax.ppermute(x, axis, [(i, i ^ step) for i in range(count)])  9.29 us
    ppermute x3, waiting for transfers between devices, swap(): lax.ppermute(x, axis, [(i, i ^ step) for i in range(count)])  4.2 us
  transfers between devices with their start and end apart: 5, of which 2 were waited for; matrix products, arithmetic and copies ran while one was open for 0% of the time, Pallas kernels for 1%

profile of v10, /device:TPU:1, one launch (start us, length us, event | category | flops | bytes accessed | tf_op | source)
XLA Modules:
  0.0 179.2 jit_solution(14984345686367344866)
XLA Ops:
  0.6 0.8 reshape.29.raw_ref
  1.4 27.4 %all_to_all.54 = bf16[16,24,128]{2,1,0:T(8,128)(2,1)S(1)} all-to-all(bf16[16,24,128]{2,1,0:T(8,128)(2,1)S(1)} %broadcast_in_dim.18), channel_id=1, replica_groups=mesh['y'=4,'core'=2,'x'=4,'z'=16] {'z'}, dimensions={0} | all-to-all | bytes 196608 | tf_op jit(solution)/shard_map/all_to_all | solution.py:238
  28.9 10.0 %all_to_all.55 = bf16[4,384,128]{2,1,0:T(8,128)(2,1)S(1)} all-to-all(bf16[4,384,128]{2,1,0:T(8,128)(2,1)S(1)} %broadcast_in_dim.20), channel_id=1, replica_groups=mesh['y'=4,'core'=2,'x'=4,'z'=16] {'x'}, dimensions={0} | all-to-all | bytes 786432 | tf_op jit(solution)/shard_map/all_to_all | solution.py:238
  38.9 1.4 scores.1
  40.4 13.3 %all_to_all.56 = bf16[8,24,128]{2,1,0:T(8,128)(2,1)S(1)} all-to-all(bf16[8,24,128]{2,1,0:T(8,128)(2,1)S(1)} %broadcast_in_dim.21), channel_id=1, replica_groups=mesh['y'=4,'core'=2,'x'=4,'z'=16] {'core','y'}, dimensions={0} | all-to-all | bytes 98304 | tf_op jit(solution)/shard_map/all_to_all | solution.py:238
  53.7 0.5 row_sum.3
  54.3 18.5 %all_to_all.57 = bf16[64,2,384]{2,1,0:T(2,128)(2,1)S(1)} all-to-all(bf16[64,2,384]{2,1,0:T(2,128)(2,1)S(1)} %broadcast_in_dim.22), channel_id=1, replica_groups=mesh['y'=4,'core'=2,'x'=4,'z'=16] {'x','z'}, dimensions={0} | all-to-all | bytes 196608 | tf_op jit(solution)/shard_map/all_to_all | solution.py:238
  73.2 10.0 %all_to_all.58 = bf16[8,24,128]{2,1,0:T(8,128)(2,1)S(1)} all-to-all(bf16[8,24,128]{2,1,0:T(8,128)(2,1)S(1)} %broadcast_in_dim.23), channel_id=1, replica_groups=mesh['y'=4,'core'=2,'x'=4,'z'=16] {'core','y'}, dimensions={0} | all-to-all | bytes 98304 | tf_op jit(solution)/shard_map/all_to_all | solution.py:238
  83.3 0.5 row_sum.4
  83.9 18.3 %all_to_all.59 = bf16[64,2,384]{2,1,0:T(2,128)(2,1)S(1)} all-to-all(bf16[64,2,384]{2,1,0:T(2,128)(2,1)S(1)} %broadcast_in_dim.24), channel_id=1, replica_groups=mesh['y'=4,'core'=2,'x'=4,'z'=16] {'x','z'}, dimensions={0} | all-to-all | bytes 196608 | tf_op jit(solution)/shard_map/all_to_all | solution.py:238
  102.6 10.0 %all_to_all.60 = bf16[8,24,128]{2,1,0:T(8,128)(2,1)S(1)} all-to-all(bf16[8,24,128]{2,1,0:T(8,128)(2,1)S(1)} %broadcast_in_dim.25), channel_id=1, replica_groups=mesh['y'=4,'core'=2,'x'=4,'z'=16] {'core','y'}, dimensions={0} | all-to-all | bytes 98304 | tf_op jit(solution)/shard_map/all_to_all | solution.py:238
  113.2 21.4 %all_to_all.61 = bf16[64,4,384]{2,1,0:T(4,128)(2,1)S(1)} all-to-all(bf16[64,4,384]{2,1,0:T(4,128)(2,1)S(1)} %broadcast_in_dim.26), channel_id=1, replica_groups=mesh['y'=4,'core'=2,'x'=4,'z'=16] {'x','z'}, dimensions={0} | all-to-all | bytes 393216 | tf_op jit(solution)/shard_map/all_to_all | solution.py:238
  134.6 2.7 %proto_part.1.tied_ref = bf16[1024,256]{1,0:T(8,128)(2,1)} custom-call(f32[4,384]{1,0:T(4,128)S(1)} %convert_reduce_fusion.totals_ref, f32[24,128]{1,0:T(8,128)S(1)} %get-tuple-element.21.inverse_ref, bf16[768,256]{1,0:T(8,128)(2,1)S(1)} %get-tuple-element.22.units_ref, bf16[1024,256]{1,0:T(8,128)(2,1)S(1)} %get-tuple-element.23.unit_protos_ref, ...), custom_call_target="tpu_custom_call" | custom-call | tf_op jit(solution)/shard_map/proto_part/pallas_call | solution.py:296
  137.3 5.8 %all-to-all-start.8 = ((bf16[8,128,256]{2,1,0:T(8,128)(2,1)}), bf16[8,128,256]{2,1,0:T(8,128)(2,1)S(1)}, u32[]{:S(2)}, u32[]{:S(2)}) async-start(bf16[8,128,256]{2,1,0:T(8,128)(2,1)} %bitcast.4), calls=%async_computation.8 | async-start | bytes 1048576 | tf_op jit(solution)/shard_map/all_to_all | solution.py:238
  143.1 1.6 unit_grad.1
  144.7 4.6 %collective-permute-start = (bf16[192,256]{1,0:T(8,128)(2,1)S(1)}, bf16[192,256]{1,0:T(8,128)(2,1)S(1)}, u32[]{:S(2)}, u32[]{:S(2)}) collective-permute-start(bf16[192,256]{1,0:T(8,128)(2,1)S(1)} %get-tuple-element.25), channel_id=1, source_target_pairs={{0,32},{16,48},{32,0},{48,16},{1,33},{17,49},{33,1},{49,17},{2,34}... | collective-permute-start | bytes 294920 | tf_op jit(solution)/shard_map/ppermute | solution.py:254
  149.3 2.3 %collective-permute-start.1 = (bf16[192,256]{1,0:T(8,128)(2,1)S(1)}, bf16[192,256]{1,0:T(8,128)(2,1)S(1)}, u32[]{:S(2)}, u32[]{:S(2)}) collective-permute-start(bf16[192,256]{1,0:T(8,128)(2,1)S(1)} %get-tuple-element.26), channel_id=1, source_target_pairs={{0,16},{16,0},{32,48},{48,32},{1,17},{17,1},{33,49},{49,33},{2,18}... | collective-permute-start | bytes 294920 | tf_op jit(solution)/shard_map/ppermute | solution.py:254
  151.6 2.3 %collective-permute-start.2 = (bf16[192,256]{1,0:T(8,128)(2,1)S(1)}, bf16[192,256]{1,0:T(8,128)(2,1)S(1)}, u32[]{:S(2)}, u32[]{:S(2)}) collective-permute-start(bf16[192,256]{1,0:T(8,128)(2,1)S(1)} %get-tuple-element.27), channel_id=1, source_target_pairs={{0,48},{16,32},{32,16},{48,0},{1,49},{17,33},{33,17},{49,1},{2,50}... | collective-permute-start | bytes 294920 | tf_op jit(solution)/shard_map/ppermute | solution.py:254
  154.0 1.2 collective-permute-done.1.refs_2_
  155.2 3.0 %collective-permute-done.2.refs_3_ = bf16[192,256]{1,0:T(8,128)(2,1)S(1)} collective-permute-done((bf16[192,256]{1,0:T(8,128)(2,1)S(1)}, bf16[192,256]{1,0:T(8,128)(2,1)S(1)}, u32[]{:S(2)}, u32[]{:S(2)}) %collective-permute-start.2) | collective-permute-done | bytes 98336 | tf_op jit(solution)/shard_map/ppermute | solution.py:254
  158.2 0.9 middle.1
  159.1 3.5 %all-to-all-start.9 = ((bf16[16,24,128]{2,1,0:T(8,128)(2,1)}), bf16[16,24,128]{2,1,0:T(8,128)(2,1)S(1)}, u32[]{:S(2)}, u32[]{:S(2)}) async-start(bf16[16,24,128]{2,1,0:T(8,128)(2,1)} %get-tuple-element.28), calls=%async_computation.9 | async-start | bytes 196608 | tf_op jit(solution)/shard_map/all_to_all | solution.py:238
  162.6 15.5 %all_gather.3.protos_ref = bf16[1024,256]{1,0:T(8,128)(2,1)S(1)} all-gather(bf16[128,256]{1,0:T(8,128)(2,1)S(1)} %get-tuple-element.29), channel_id=1, replica_groups=mesh['y'=4,'core'=2,'x'=4,'z'=16] {'y','core'}, dimensions={0}, use_global_device_ids=true | all-gather | bytes 589824 | tf_op jit(solution)/shard_map/all_gather | solution.py:316
  178.1 1.1 last.1
  (30 shorter events, 1.7 us)
Async XLA Ops:
  0.6 38.3 %copy-start = (bf16[1024,256]{1,0:T(8,128)(2,1)S(1)}, bf16[1024,256]{1,0:T(8,128)(2,1)}, u32[]{:S(2)}) copy-start(bf16[1024,256]{1,0:T(8,128)(2,1)} %protos_ref.3) | copy-start | bytes 1572868
  137.3 20.9 %all-to-all-start.8 = ((bf16[8,128,256]{2,1,0:T(8,128)(2,1)}), bf16[8,128,256]{2,1,0:T(8,128)(2,1)S(1)}, u32[]{:S(2)}, u32[]{:S(2)}) async-start(bf16[8,128,256]{2,1,0:T(8,128)(2,1)} %bitcast.4), calls=%async_computation.8 | async-start | bytes 1048576 | tf_op jit(solution)/shard_map/all_to_all | solution.py:238
  144.7 9.3 %collective-permute-start = (bf16[192,256]{1,0:T(8,128)(2,1)S(1)}, bf16[192,256]{1,0:T(8,128)(2,1)S(1)}, u32[]{:S(2)}, u32[]{:S(2)}) collective-permute-start(bf16[192,256]{1,0:T(8,128)(2,1)S(1)} %get-tuple-element.25), channel_id=1, source_target_pairs={{0,32},{16,48},{32,0},{48,16},{1,33},{17,49},{33,1},{49,17},{2,34}... | collective-permute-start | bytes 294920 | tf_op jit(solution)/shard_map/ppermute | solution.py:254
  149.3 5.9 %collective-permute-start.1 = (bf16[192,256]{1,0:T(8,128)(2,1)S(1)}, bf16[192,256]{1,0:T(8,128)(2,1)S(1)}, u32[]{:S(2)}, u32[]{:S(2)}) collective-permute-start(bf16[192,256]{1,0:T(8,128)(2,1)S(1)} %get-tuple-element.26), channel_id=1, source_target_pairs={{0,16},{16,0},{32,48},{48,32},{1,17},{17,1},{33,49},{49,33},{2,18}... | collective-permute-start | bytes 294920 | tf_op jit(solution)/shard_map/ppermute | solution.py:254
  151.6 6.6 %collective-permute-start.2 = (bf16[192,256]{1,0:T(8,128)(2,1)S(1)}, bf16[192,256]{1,0:T(8,128)(2,1)S(1)}, u32[]{:S(2)}, u32[]{:S(2)}) collective-permute-start(bf16[192,256]{1,0:T(8,128)(2,1)S(1)} %get-tuple-element.27), channel_id=1, source_target_pairs={{0,48},{16,32},{32,16},{48,0},{1,49},{17,33},{33,17},{49,1},{2,50}... | collective-permute-start | bytes 294920 | tf_op jit(solution)/shard_map/ppermute | solution.py:254
  159.1 19.0 %all-to-all-start.9 = ((bf16[16,24,128]{2,1,0:T(8,128)(2,1)}), bf16[16,24,128]{2,1,0:T(8,128)(2,1)S(1)}, u32[]{:S(2)}, u32[]{:S(2)}) async-start(bf16[16,24,128]{2,1,0:T(8,128)(2,1)} %get-tuple-element.28), calls=%async_computation.9 | async-start | bytes 196608 | tf_op jit(solution)/shard_map/all_to_all | solution.py:238
